TPU v7x, 32 devices: a whole 2x2x4 slice. The times are simulated.
32 devices in a mesh: dp: 4 (over z), ctx: 2 (over y), tensor: 4 (over x, core).
Axes of the slice: x: 2, y: 2, z: 4, core: 2. Of those that a mesh axis runs over, the one named last changes fastest.
Arguments:
- tokens: bfloat16 [16384, 2048], P(('dp', 'ctx')), may hold values from -6 to 6
- cotangent: bfloat16 [16384, 2048], P(('dp', 'ctx')), may hold values from -6 to 6
- lengths: int32 [4, 6], P('dp'), may hold values from 1 to 2048, as said below
- offsets: int32 [4, 32], P('dp'), may hold values from 0 to 3968, as said below
- ln1_gain: bfloat16 [2048], replicated, may hold values from 0.5 to 1.5
- ln1_bias: bfloat16 [2048], replicated, may hold values from -1 to 1
- w_qkv: bfloat16 [2048, 3, 2048], P(('dp', 'ctx'), None, 'tensor'), may hold values from -0.125 to 0.125
- b_qkv: bfloat16 [3, 2048], P(None, 'tensor'), may hold values from -2.5 to 2.5
- w_out: bfloat16 [2048, 2048], P('tensor', ('dp', 'ctx')), may hold values from -2 to 2
- ln2_gain: bfloat16 [2048], replicated, may hold values from 0.5 to 1.5
- ln2_bias: bfloat16 [2048], replicated, may hold values from -1 to 1
- w_gate_up: bfloat16 [2048, 2, 5632], P(('dp', 'ctx'), None, 'tensor'), may hold values from -0.125 to 0.125
- w_down: bfloat16 [5632, 2048], P('tensor', ('dp', 'ctx')), may hold values from -0.4375 to 0.4375
Outputs:
- output: bfloat16 [16384, 2048], P(('dp', 'ctx'))
- grad_tokens: bfloat16 [16384, 2048], P(('dp', 'ctx'))
- grad_ln1_gain: float32 [2048], replicated
- grad_ln1_bias: float32 [2048], replicated
- grad_w_qkv: float32 [2048, 3, 2048], P(('dp', 'ctx'), None, 'tensor')
- grad_b_qkv: float32 [3, 2048], P(None, 'tensor')
- grad_w_out: float32 [2048, 2048], P('tensor', ('dp', 'ctx'))
- grad_ln2_gain: float32 [2048], replicated
- grad_ln2_bias: float32 [2048], replicated
- grad_w_gate_up: float32 [2048, 2, 5632], P(('dp', 'ctx'), None, 'tensor')
- grad_w_down: float32 [5632, 2048], P('tensor', ('dp', 'ctx'))
Inputs may be any that keep to these rules, and one draw needn't show every extreme that they name: Each row lists one group's sequence lengths in stream order; they sum to 4096, and the first is 2048, the longest of the row. `offsets`: each row is 128 times a permutation of 0 to 31.
All inputs are finite; a program needn't handle non-finite values.
Results may differ from a plain program's by a relative error of at most 0.025.
Values may be sent and summed in bfloat16 or wider, within the bound.
A program may use at most 768 MiB of HBM per device.

v0:
```python
import math

import jax
import jax.numpy as jnp
from jax import lax
from jax.sharding import PartitionSpec as P

HD = 64
ROT = 16
TILE = 128


def layer_norm(values, norm_gain, norm_shift):
    row_mean = jnp.mean(values, axis=-1, keepdims=True)
    centred = values - row_mean
    spread = jnp.mean(centred * centred, axis=-1, keepdims=True)
    return centred * lax.rsqrt(spread + 1e-05) * norm_gain + norm_shift


def rotate(values, cosine, sine_table):
    half_rot = ROT // 2
    first_half = values[..., :half_rot]
    second_half = values[..., half_rot:ROT]
    return jnp.concatenate(
        [
            first_half * cosine - second_half * sine_table,
            second_half * cosine + first_half * sine_table,
            values[..., ROT:],
        ],
        axis=-1,
    )


def rotary_tables(relative):
    half_rot = ROT // 2
    frequency = jnp.exp(jnp.arange(half_rot, dtype=jnp.float32) * (-2.0 * math.log(10000.0) / ROT))
    angles = relative.astype(jnp.float32)[..., None] * frequency
    return (jnp.cos(angles), jnp.sin(angles))


def tile_places(offsets_row, first_row, row_count):
    row_index = first_row + jnp.arange(row_count, dtype=jnp.int32)
    tile_index = row_index // TILE
    tile_match = tile_index[:, None] == jnp.arange(offsets_row.shape[0], dtype=jnp.int32)[None, :]
    return jnp.sum(jnp.where(tile_match, offsets_row[None, :], 0), axis=1) + row_index % TILE


def contract_rows(left, right):
    return lax.dot_general(
        left, right, (((0,), (0,)), ((), ())), preferred_element_type=jnp.float32
    )


def contract_cols(left, right):
    return lax.dot_general(
        left, right, (((1,), (1,)), ((), ())), preferred_element_type=jnp.float32
    )


def body(
    tokens,
    cotangent,
    lengths,
    offsets,
    ln1_gain,
    ln1_bias,
    w_qkv,
    b_qkv,
    w_out,
    ln2_gain,
    ln2_bias,
    w_gate_up,
    w_down,
):
    row_count = tokens.shape[0]
    head_width = w_qkv.shape[2]
    head_count = head_width // HD
    score_scale = HD ** (-0.5)
    offsets_row = offsets[0]
    lengths_row = lengths[0]
    sequence_end = jnp.cumsum(lengths_row)
    own_place = tile_places(offsets_row, lax.axis_index("ctx") * row_count, row_count)
    own_begin = jnp.sum(
        jnp.where(own_place[:, None] >= sequence_end[None, :], lengths_row[None, :], 0), axis=1
    )
    cosine, sine_table = rotary_tables(own_place - own_begin)
    cosine = cosine[:, None, :]
    sine_table = sine_table[:, None, :]
    qkv_full, out_full = (
        lax.all_gather(w_qkv, ("dp", "ctx"), axis=0, tiled=True),
        lax.all_gather(w_out, ("dp", "ctx"), axis=1, tiled=True),
    )
    inputs = tokens.astype(jnp.float32)
    gain_one = ln1_gain.astype(jnp.float32)
    shift_one = ln1_bias.astype(jnp.float32)
    normed1_low = layer_norm(inputs, gain_one, shift_one).astype(jnp.bfloat16)
    projected = (
        jnp.einsum("td,dkf->tkf", normed1_low, qkv_full, preferred_element_type=jnp.float32)
        + b_qkv.astype(jnp.float32)[None]
    )
    query_raw = projected[:, 0].reshape(row_count, head_count, HD)
    key_raw = projected[:, 1].reshape(row_count, head_count, HD)
    query = rotate(query_raw, cosine, sine_table).astype(jnp.bfloat16)
    key_flat = (
        rotate(key_raw, cosine, sine_table).astype(jnp.bfloat16).reshape(row_count, head_width)
    )
    value_flat = projected[:, 2].astype(jnp.bfloat16)

    def visibility(first_row, piece_rows):
        key_place = tile_places(offsets_row, first_row, piece_rows)
        return (key_place[None, :] <= own_place[:, None]) & (
            key_place[None, :] >= own_begin[:, None]
        )

    shard_piece = (
        lax.all_gather(key_flat, "ctx", axis=0, tiled=True),
        lax.all_gather(value_flat, "ctx", axis=0, tiled=True),
    )
    running_top = jnp.full((head_count, row_count), -1e30, jnp.float32)
    piece_rows = shard_piece[0].shape[0]
    key_block = shard_piece[0].reshape(piece_rows, head_count, HD)
    value_block = shard_piece[1].reshape(piece_rows, head_count, HD)
    visible = visibility(jnp.int32(0), piece_rows)
    scores = (
        jnp.einsum("qhd,khd->hqk", query, key_block, preferred_element_type=jnp.float32)
        * score_scale
    )
    masked = jnp.where(visible[None], scores, -1e30)
    new_top = jnp.maximum(running_top, jnp.max(masked, axis=-1))
    expw = jnp.where(visible[None], jnp.exp(masked - new_top[..., None]), 0.0)
    row_total = jnp.sum(expw, axis=-1)
    weighted = jnp.einsum(
        "hqk,khd->hqd", expw.astype(jnp.bfloat16), value_block, preferred_element_type=jnp.float32
    )
    running_top, row_total, weighted = (new_top, row_total, weighted)
    attended = jnp.transpose(weighted / row_total[..., None], (1, 0, 2))
    attended_low = attended.reshape(row_count, head_width).astype(jnp.bfloat16)
    log_total = running_top + jnp.log(row_total)
    branch = lax.psum(
        jnp.dot(attended_low, out_full, preferred_element_type=jnp.float32).astype(jnp.bfloat16),
        "tensor",
    ).astype(jnp.float32)
    middle = inputs + branch
    gate_up_full, down_full = (
        lax.all_gather(w_gate_up, ("dp", "ctx"), axis=0, tiled=True),
        lax.all_gather(w_down, ("dp", "ctx"), axis=1, tiled=True),
    )
    gain_two = ln2_gain.astype(jnp.float32)
    shift_two = ln2_bias.astype(jnp.float32)
    normed2_low = layer_norm(middle, gain_two, shift_two).astype(jnp.bfloat16)
    gate_up = jnp.einsum(
        "td,dkf->tkf", normed2_low, gate_up_full, preferred_element_type=jnp.float32
    )

    def swiglu(gate_pair):
        return jax.nn.silu(gate_pair[:, 0]) * gate_pair[:, 1]

    hidden_full, swiglu_back = jax.vjp(swiglu, gate_up)
    hidden = hidden_full.astype(jnp.bfloat16)
    feed = lax.psum(
        jnp.dot(hidden, down_full, preferred_element_type=jnp.float32).astype(jnp.bfloat16),
        "tensor",
    ).astype(jnp.float32)
    output = (middle + feed).astype(jnp.bfloat16)
    gate_up_back, down_back = (
        lax.all_gather(w_gate_up, ("dp", "ctx"), axis=0, tiled=True),
        lax.all_gather(w_down, ("dp", "ctx"), axis=1, tiled=True),
    )
    upstream = cotangent.astype(jnp.float32)
    grad_down = contract_rows(hidden, cotangent)
    d_hidden = contract_cols(cotangent, down_back)
    d_gate_up = swiglu_back(d_hidden)[0].astype(jnp.bfloat16)
    grad_gate_up = jnp.einsum(
        "td,tkf->dkf", normed2_low, d_gate_up, preferred_element_type=jnp.float32
    )
    ffn_parts = (
        lax.psum_scatter(
            grad_gate_up.astype(jnp.bfloat16), ("dp", "ctx"), scatter_dimension=0, tiled=True
        ).astype(jnp.float32),
        lax.psum_scatter(
            grad_down.astype(jnp.bfloat16), ("dp", "ctx"), scatter_dimension=1, tiled=True
        ).astype(jnp.float32),
    )
    d_normed2 = lax.psum(
        jnp.einsum(
            "tkf,dkf->td", d_gate_up, gate_up_back, preferred_element_type=jnp.float32
        ).astype(jnp.bfloat16),
        "tensor",
    ).astype(jnp.float32)
    norm_two_back = jax.vjp(layer_norm, middle, gain_two, shift_two)[1]
    d_middle_norm, d_gain_two, d_shift_two = norm_two_back(d_normed2)
    d_middle = upstream + d_middle_norm
    d_middle_low = d_middle.astype(jnp.bfloat16)
    qkv_back, out_back = (
        lax.all_gather(w_qkv, ("dp", "ctx"), axis=0, tiled=True),
        lax.all_gather(w_out, ("dp", "ctx"), axis=1, tiled=True),
    )
    grad_out = contract_rows(attended_low, d_middle_low)
    d_attended = (
        contract_cols(d_middle_low, out_back)
        .astype(jnp.bfloat16)
        .reshape(row_count, head_count, HD)
    )
    row_delta = jnp.transpose(jnp.sum(d_attended.astype(jnp.float32) * attended, axis=-1))
    shard_piece = (
        lax.all_gather(key_flat, "ctx", axis=0, tiled=True),
        lax.all_gather(value_flat, "ctx", axis=0, tiled=True),
    )
    piece_rows = shard_piece[0].shape[0]
    key_block = shard_piece[0].reshape(piece_rows, head_count, HD)
    value_block = shard_piece[1].reshape(piece_rows, head_count, HD)
    visible = visibility(jnp.int32(0), piece_rows)
    scores = (
        jnp.einsum("qhd,khd->hqk", query, key_block, preferred_element_type=jnp.float32)
        * score_scale
    )
    masked = jnp.where(visible[None], scores, -1e30)
    chances = jnp.where(visible[None], jnp.exp(masked - log_total[..., None]), 0.0)
    d_chances = jnp.einsum(
        "qhd,khd->hqk", d_attended, value_block, preferred_element_type=jnp.float32
    )
    d_raw = (chances * (d_chances - row_delta[..., None]) * score_scale).astype(jnp.bfloat16)
    piece_rows, key_block, chances, d_raw = (piece_rows, key_block, chances, d_raw)
    d_values = jnp.einsum(
        "hqk,qhd->khd", chances.astype(jnp.bfloat16), d_attended, preferred_element_type=jnp.float32
    )
    d_query = jnp.einsum("hqk,khd->qhd", d_raw, key_block, preferred_element_type=jnp.float32)
    d_keys = jnp.einsum("hqk,qhd->khd", d_raw, query, preferred_element_type=jnp.float32)
    d_keys_all = d_keys.reshape(piece_rows, head_width)
    d_values_all = d_values.reshape(piece_rows, head_width)
    d_query, d_keys_all, d_values_all = (d_query, d_keys_all, d_values_all)
    d_keys, d_values = (
        lax.psum_scatter(
            d_keys_all.astype(jnp.bfloat16), "ctx", scatter_dimension=0, tiled=True
        ).astype(jnp.float32),
        lax.psum_scatter(
            d_values_all.astype(jnp.bfloat16), "ctx", scatter_dimension=0, tiled=True
        ).astype(jnp.float32),
    )

    def turn(values):
        return rotate(values, cosine, sine_table)

    turn_back = jax.vjp(turn, query_raw)[1]
    d_query_pre = turn_back(d_query)[0].reshape(row_count, head_width)
    d_key_pre = turn_back(d_keys.reshape(row_count, head_count, HD))[0].reshape(
        row_count, head_width
    )
    d_projected = jnp.stack([d_query_pre, d_key_pre, d_values], axis=1).astype(jnp.bfloat16)
    grad_bias = jnp.sum(d_projected.astype(jnp.float32), axis=0)
    grad_qkv = jnp.einsum(
        "td,tkf->dkf", normed1_low, d_projected, preferred_element_type=jnp.float32
    )
    attn_parts = (
        lax.psum_scatter(
            grad_qkv.astype(jnp.bfloat16), ("dp", "ctx"), scatter_dimension=0, tiled=True
        ).astype(jnp.float32),
        lax.psum_scatter(
            grad_out.astype(jnp.bfloat16), ("dp", "ctx"), scatter_dimension=1, tiled=True
        ).astype(jnp.float32),
    )
    d_normed1 = lax.psum(
        jnp.einsum("tkf,dkf->td", d_projected, qkv_back, preferred_element_type=jnp.float32).astype(
            jnp.bfloat16
        ),
        "tensor",
    ).astype(jnp.float32)
    norm_one_back = jax.vjp(layer_norm, inputs, gain_one, shift_one)[1]
    d_input, d_gain_one, d_shift_one = norm_one_back(d_normed1)
    grad_tokens = (d_middle + d_input).astype(jnp.bfloat16)
    small_parts = (
        lax.psum(d_gain_one.astype(jnp.bfloat16), ("dp", "ctx")).astype(jnp.float32),
        lax.psum(d_shift_one.astype(jnp.bfloat16), ("dp", "ctx")).astype(jnp.float32),
        lax.psum(grad_bias.astype(jnp.bfloat16), ("dp", "ctx")).astype(jnp.float32),
        lax.psum(d_gain_two.astype(jnp.bfloat16), ("dp", "ctx")).astype(jnp.float32),
        lax.psum(d_shift_two.astype(jnp.bfloat16), ("dp", "ctx")).astype(jnp.float32),
    )
    return (
        output,
        grad_tokens,
        small_parts[0],
        small_parts[1],
        attn_parts[0],
        small_parts[2],
        attn_parts[1],
        small_parts[3],
        small_parts[4],
        ffn_parts[0],
        ffn_parts[1],
    )


def solution(mesh):
    placed = (
        P(("dp", "ctx"), None),
        P(("dp", "ctx"), None),
        P("dp", None),
        P("dp", None),
        P(),
        P(),
        P(("dp", "ctx"), None, "tensor"),
        P(None, "tensor"),
        P("tensor", ("dp", "ctx")),
        P(),
        P(),
        P(("dp", "ctx"), None, "tensor"),
        P("tensor", ("dp", "ctx")),
    )
    return jax.shard_map(
        body,
        mesh=mesh,
        in_specs=placed,
        out_specs=(
            P(("dp", "ctx"), None),
            P(("dp", "ctx"), None),
            P(),
            P(),
            P(("dp", "ctx"), None, "tensor"),
            P(None, "tensor"),
            P("tensor", ("dp", "ctx")),
            P(),
            P(),
            P(("dp", "ctx"), None, "tensor"),
            P("tensor", ("dp", "ctx")),
        ),
        check_vma=False,
    )
```

profile of v0, /device:TPU:0, one launch (start us, length us, event | category | flops | bytes accessed | tf_op | source)
XLA Modules:
  0.0 2312.2 jit_solution(4245873596515066318)
XLA Ops:
  14.4 4.8 convert_reduce_fusion
  22.5 90.8 %all-gather.8.cloned.1.call-done = bf16[2048,3,512]{0,2,1:T(8,128)(2,1)} async-done(((bf16[256,3,512]{0,2,1:T(8,128)(2,1)}), bf16[2048,3,512]{0,2,1:T(8,128)(2,1)}) %all-gather.8.cloned.1.call-update) | async-done | bytes 6291472 | tf_op jit(solution)/shard_map/all_gather | solution.py:90
  113.4 19.1 broadcast_add_fusion
  133.6 3.4 copy-done.6
  140.8 3.9 slice.83
  145.7 8.7 compare_and_fusion
  156.5 39.3 %all-gather.10.cloned.1.call-done = bf16[4096,512]{0,1:T(8,128)(2,1)} async-done(((bf16[2048,512]{0,1:T(8,128)(2,1)}), bf16[4096,512]{0,1:T(8,128)(2,1)}) %all-gather.10.cloned.1.call-update) | async-done | bytes 4194320 | tf_op jit(solution)/shard_map/all_gather | solution.py:116
  195.8 92.1 %fusion.3 = (f32[8,2048]{1,0:T(8,128)S(1)}, f32[8,2048,4096]{2,1,0:T(8,128)}) fusion(pred[2048,4096]{1,0:T(8,128)(4,1)} %compare_and_fusion, bf16[4096,8,64]{0,2,1:T(8,128)(2,1)} %bitcast.89, bf16[2048,8,48]{0,2,1:T(8,128)(2,1)S(1)} %slice.85, bf16[2048,8,8]{0,2,1:T(8,128)(2,1)S(1)} %get-tuple-element.58, bf16[2048,8,8]{0,2,1:T(8,128)(2,1)S(1)} %get-tuple-element.57), kind=kOutput, calls=%fused_computation.7 | convolution fusion | flops 8797536256 | bytes 283181056 | tf_op jit(solution)/shard_map/qhd,khd->hqk/dot_general | solution.py:125
  287.9 89.7 %fusion = f32[8,2048]{1,0:T(8,128)S(1)} fusion(f32[8,2048,4096]{2,1,0:T(8,128)} %get-tuple-element.68, f32[8,2048]{1,0:T(8,128)S(1)} %broadcast_maximum_fusion, pred[2048,4096]{1,0:T(8,128)(4,1)} %compare_and_fusion), kind=kLoop, calls=%fused_computation.4 | loop fusion | flops 335527936 | bytes 276955136 | tf_op jit(solution)/shard_map/reduce_sum | solution.py:131
  377.7 90.7 %fusion.75 = (bf16[2048,8,64]{0,2,1:T(8,128)(2,1)S(1)}, f32[2048,8,64]{0,2,1:T(8,128)}) fusion(f32[2048,8]{0,1:T(8,128)S(1)} %bitcast.107, bf16[4096,8,64]{0,2,1:T(8,128)(2,1)} %bitcast.113, f32[8,2048,4096]{2,1,0:T(8,128)} %get-tuple-element.68, f32[8,2048]{1,0:T(8,128)S(1)} %broadcast_maximum_fusion, pred[2048,4096]{1,0:T(8,128)(4,1)} %compare_and_fusion), kind=kOutput, calls=%fused_computation.151 | convolution fusion | flops 8927576064 | bytes 287440896 | tf_op jit(solution)/shard_map/hqk,khd->hqd/dot_general | solution.py:132
  469.8 8.4 convolution_convert_fusion.2
  481.7 150.0 %all-reduce.14.cloned.1.call-done = bf16[2048,2048]{1,0:T(8,128)(2,1)} async-done(((bf16[2048,2048]{1,0:T(8,128)(2,1)}), bf16[2048,2048]{1,0:T(8,128)(2,1)}) %all-reduce.14.cloned.1.call-update) | async-done | bytes 8388624 | tf_op jit(solution)/shard_map/psum | solution.py:139
  631.7 8.0 fusion.26
  639.8 9.2 multiply_reduce_fusion
  649.0 149.2 %all-gather.14.cloned.1.call-done = bf16[2048,2,1408]{2,0,1:T(8,128)(2,1)} async-done(((bf16[256,2,1408]{2,0,1:T(8,128)(2,1)}), bf16[2048,2,1408]{2,0,1:T(8,128)(2,1)}) %all-gather.14.cloned.1.call-update) | async-done | bytes 11534352 | tf_op jit(solution)/shard_map/all_gather | solution.py:145
  798.2 34.8 %fusion.71 = f32[2048,2,1408]{2,0,1:T(8,128)} fusion(bf16[2048,2,1408]{2,0,1:T(8,128)(2,1)} %all-gather.14.cloned.1.call-done, bf16[2048,2048]{1,0:T(8,128)(2,1)} %all-reduce.14.cloned.1.call-done, bf16[2048,2048]{1,0:T(8,128)(2,1)} %param.13, f32[2048]{0:T(1024)S(1)} %convert_element_type.188, f32[2048]{0:T(1024)S(1)} %convert_element_type.187, ...), kind=kOutput, calls=%fused_computation.148 | convolution fusion | flops 23655874560 | bytes 51412992 | tf_op jit(solution)/shard_map/td,dkf->tkf/dot_general | solution.py:151
  833.0 59.1 %all-gather.16.cloned.1.call-done = bf16[1408,2048]{1,0:T(8,128)(2,1)} async-done(((bf16[1408,256]{1,0:T(8,128)(2,1)}), bf16[1408,2048]{1,0:T(8,128)(2,1)}) %all-gather.16.cloned.1.call-update) | async-done | bytes 5767184 | tf_op jit(solution)/shard_map/all_gather | solution.py:146
  892.0 29.9 %multiply_bitcast_fusion = (f32[2048,1,1408]{2,0,1:T(8,128)}, f32[2048,1,1408]{2,0,1:T(8,128)}, bf16[2048,1408]{1,0:T(8,128)(2,1)}) fusion(f32[2048,2,1408]{2,0,1:T(8,128)} %fusion.71, bf16[2048,2048]{1,0:T(8,128)(2,1)} %param.14, bf16[1408,2048]{1,0:T(8,128)(2,1)} %all-gather.16.cloned.1.call-done), kind=kOutput, calls=%fused_computation.53 | convolution fusion | flops 11851530240 | bytes 66060288 | tf_op jit(solution)/shard_map/dot_general | solution.py:55
  921.9 32.1 %bitcast_convert_fusion.1 = bf16[2048,2048]{1,0:T(8,128)(2,1)} fusion(bf16[2048,2,1408]{2,0,1:T(8,128)(2,1)} %all-gather.14.cloned.1.call-done, f32[2048,1,1408]{2,0,1:T(8,128)} %get-tuple-element.47, f32[2048,1,1408]{2,0,1:T(8,128)} %get-tuple-element.46), kind=kOutput, calls=%fused_computation.40 | convolution fusion | flops 23638048768 | bytes 42991616 | tf_op jit(solution)/shard_map/tkf,dkf->td/dot_general | solution.py:185
  955.0 150.3 %all-reduce.16.cloned.1.call-done = bf16[2048,2048]{1,0:T(8,128)(2,1)} async-done(((bf16[2048,2048]{1,0:T(8,128)(2,1)}), bf16[2048,2048]{1,0:T(8,128)(2,1)}) %all-reduce.16.cloned.1.call-update) | async-done | bytes 8388624 | tf_op jit(solution)/shard_map/psum | solution.py:184
  1105.3 14.0 fusion.21
  1119.4 10.2 fusion.73
  1135.3 11.3 multiply_reduce_fusion.1
  1146.7 157.2 %multiply_convert_fusion = bf16[8,2048,4096]{2,1,0:T(8,128)(2,1)} fusion(f32[8,2048,4096]{2,1,0:T(8,128)} %get-tuple-element.68, f32[8,2048]{1,0:T(8,128)S(1)} %bitcast.119, f32[8,2048]{1,0:T(8,128)S(1)} %log_add_fusion, pred[2048,4096]{1,0:T(8,128)(4,1)} %compare_and_fusion, bf16[2048,8,64]{0,2,1:T(8,128)(2,1)} %bitcast.117, bf16[4096,8,64]{0,2,1:T(8,128)(2,1)} %bitcast.114), kind=kOutput, calls=%fused_computation | convolution fusion | flops 9126805504 | bytes 417464320 | tf_op jit(solution)/shard_map/qhd,khd->hqk/dot_general | solution.py:219
  1303.9 46.1 %convolution_convert_fusion.4 = bf16[8,64,4096]{2,1,0:T(8,128)(2,1)} fusion(bf16[8,2048,4096]{2,1,0:T(8,128)(2,1)} %multiply_convert_fusion, bf16[2048,8,48]{0,2,1:T(8,128)(2,1)S(1)} %copy-done.9, bf16[2048,8,8]{0,2,1:T(8,128)(2,1)S(1)} %copy-done.14, bf16[2048,8,8]{0,2,1:T(8,128)(2,1)S(1)} %copy-done.12), kind=kOutput, calls=%fused_computation.67 | convolution fusion | flops 8598323200 | bytes 140509184 | tf_op jit(solution)/shard_map/hqk,qhd->khd/dot_general | solution.py:228
  1350.0 98.1 %fusion.35 = bf16[8,64,4096]{2,1,0:T(8,128)(2,1)} fusion(bf16[2048,8,64]{0,2,1:T(8,128)(2,1)} %bitcast.118, f32[8,2048,4096]{2,1,0:T(8,128)} %get-tuple-element.68, f32[8,2048]{1,0:T(8,128)S(1)} %log_add_fusion, pred[2048,4096]{1,0:T(8,128)(4,1)} %compare_and_fusion), kind=kOutput, calls=%fused_computation.68 | convolution fusion | flops 8927576064 | bytes 283181056 | tf_op jit(solution)/shard_map/hqk,qhd->khd/dot_general | solution.py:224
  1448.1 6.6 copy.35
  1454.7 9.0 convolution_convert_fusion.6
  1463.9 18.1 convolution_convert_fusion.3
  1482.1 18.4 convolution_convert_fusion.1
  1500.5 55.5 %convolution_bitcast_fusion = f32[2048,8,64]{0,2,1:T(8,128)} fusion(bf16[4096,8,64]{0,2,1:T(8,128)(2,1)} %bitcast.90, bf16[8,2048,4096]{2,1,0:T(8,128)(2,1)} %multiply_convert_fusion), kind=kOutput, calls=%fused_computation.75 | convolution fusion | flops 8589934592 | bytes 142606336 | tf_op jit(solution)/shard_map/hqk,khd->qhd/dot_general | solution.py:227
  1557.9 2.9 convert.46
  1566.4 3.9 copy.36
  1570.3 18.4 bitcast_convert_fusion
  1589.5 45.4 %convolution_convert_fusion = bf16[2048,2,1408]{2,0,1:T(8,128)(2,1)} fusion(f32[2048,1,1408]{2,0,1:T(8,128)} %get-tuple-element.47, f32[2048,1,1408]{2,0,1:T(8,128)} %get-tuple-element.46, bf16[2048,2048]{1,0:T(8,128)(2,1)} %all-reduce.14.cloned.1.call-done, bf16[2048,2048]{1,0:T(8,128)(2,1)} %param.13, f32[2048]{0:T(1024)S(1)} %copy-done.43, ...), kind=kOutput, calls=%fused_computation.58 | convolution fusion | flops 23673176064 | bytes 51412992 | tf_op jit(solution)/shard_map/td,tkf->dkf/dot_general | solution.py:173
  1635.7 21.9 convolution_convert_fusion.5
  1657.6 4.9 reduce_sum.203
  1664.2 29.7 %reduce-scatter.17.cloned.1.call-done = bf16[1408,256]{1,0:T(8,128)(2,1)} async-done(((bf16[1408,2048]{1,0:T(8,128)(2,1)}), bf16[1408,256]{1,0:T(8,128)(2,1)}) %reduce-scatter.17.cloned.1.call-update) | async-done | bytes 720912 | tf_op jit(solution)/shard_map/reduce_scatter | solution.py:180
  1696.2 3.3 fusion.69
  1699.5 286.2 %all-reduce.18.cloned.1.call-done = (bf16[2048,2048]{1,0:T(8,128)(2,1)}, bf16[2048,2048]{1,0:T(8,128)(2,1)}) async-done(((bf16[2048,2048]{1,0:T(8,128)(2,1)}, bf16[2048,2048]{1,0:T(8,128)(2,1)}), (bf16[2048,2048]{1,0:T(8,128)(2,1)}, bf16[2048,2048]{1,0:T(8,128)(2,1)})) %all-reduce.18.cloned.1.call-update) | async-done | bytes 16777232 | tf_op jit(solution)/shard_map/psum | solution.py:160
  1985.8 4.7 reduce_sum.197
  1990.5 9.5 fusion.24
  2000.1 10.5 fusion.22
  2010.7 39.7 %all-reduce.8 = (bf16[2048]{0:T(1024)(128)(2,1)S(1)}, bf16[2048]{0:T(1024)(128)(2,1)S(1)}, bf16[3,512]{1,0:T(4,128)(2,1)S(1)}, bf16[2048]{0:T(1024)(128)(2,1)S(1)}, bf16[2048]{0:T(1024)(128)(2,1)S(1)}) all-reduce(bf16[2048]{0:T(1024)(128)(2,1)S(1)} %get-tuple-element.35, ...), channel_id=1, replica_groups=mesh['dp'=4,'ctx'=2,'tensor'=4] {'dp','ctx'}, use_global_device_ids=true, to_apply=%region_22.23 | all-reduce | flops 9728 | bytes 38912 | tf_op jit(solution)/shard_map/psum | solution.py:272
  2053.4 27.2 %add_convert_fusion.1 = (bf16[2048,2048]{1,0:T(8,128)(2,1)}, bf16[2048,2048]{1,0:T(8,128)(2,1)}) fusion(bf16[2048,2048]{1,0:T(8,128)(2,1)} %param.13, bf16[2048,2048]{1,0:T(8,128)(2,1)} %get-tuple-element.43, f32[2048,2048]{1,0:T(8,128)} %copy-done.2, bf16[2048,2048]{1,0:T(8,128)(2,1)} %param.14, f32[2048]{0:T(1024)S(1)} %negate_multiply_fusion, ...), kind=kLoop, calls=%fused_computation.41 | loop fusion | flops 79691776 | bytes 75546624 | tf_op jit(solution)/shard_map/convert_element_type | solution.py:270
  2080.7 101.3 %reduce-scatter.15.cloned.1.call-done = bf16[256,2,1408]{2,0,1:T(8,128)(2,1)} async-done(((bf16[2048,2,1408]{2,0,1:T(8,128)(2,1)}), bf16[256,2,1408]{2,0,1:T(8,128)(2,1)}) %reduce-scatter.15.cloned.1.call-update) | async-done | bytes 1441808 | tf_op jit(solution)/shard_map/reduce_scatter | solution.py:177
  2182.0 4.4 copy.41
  2186.4 116.5 %reduce-scatter.11.cloned.1.call-done = bf16[256,3,512]{2,0,1:T(8,128)(2,1)} async-done(((bf16[2048,3,512]{2,0,1:T(8,128)(2,1)}), bf16[256,3,512]{2,0,1:T(8,128)(2,1)}) %reduce-scatter.11.cloned.1.call-update) | async-done | bytes 786448 | tf_op jit(solution)/shard_map/reduce_scatter | solution.py:255
  (186 shorter events, 48.5 us)
Async XLA Ops:
  7.2 106.2 %all-gather.8.cloned.1.call-start = ((), (), s32[]{:S(2)}) async-start(), calls=%async_computation.6 | async-start | bytes 7077888 | tf_op jit(solution)/shard_map/all_gather | solution.py:90
  9.5 186.3 %all-gather.10.cloned.1.call-start = ((), (), s32[]{:S(2)}) async-start(), calls=%async_computation.7 | async-start | bytes 6291456 | tf_op jit(solution)/shard_map/all_gather | solution.py:116
  10.3 103.1 %copy-start.27 = (f32[2048]{0:T(1024)}, f32[2048]{0:T(1024)S(1)}, u32[]{:S(2)}) copy-start(f32[2048]{0:T(1024)S(1)} %convert_element_type.175) | copy-start | bytes 24580
  11.0 102.4 %copy-start.40 = (f32[2048]{0:T(1024)}, f32[2048]{0:T(1024)S(1)}, u32[]{:S(2)}) copy-start(f32[2048]{0:T(1024)S(1)} %convert_element_type.176) | copy-start | bytes 24580
  12.5 6.8 copy-start
  19.3 113.2 %copy-start.23 = (f32[2048]{0:T(1024)}, f32[2048]{0:T(1024)S(1)}, u32[]{:S(2)}) copy-start(f32[2048]{0:T(1024)S(1)} %broadcast_multiply_fusion.1) | copy-start | bytes 24580
  21.6 110.8 %copy-start.29 = (f32[2048]{0:T(1024)}, f32[2048]{0:T(1024)S(1)}, u32[]{:S(2)}) copy-start(f32[2048]{0:T(1024)S(1)} %fusion.57) | copy-start | bytes 24580
  22.5 114.7 %copy-start.15 = (f32[2048,8]{0,1:T(8,128)}, f32[2048,8]{0,1:T(8,128)S(1)}, u32[]{:S(2)}) copy-start(f32[2048,8]{0,1:T(8,128)S(1)} %get-tuple-element.65) | copy-start | bytes 196612
  22.5 114.7 %copy-start.17 = (f32[2048,8]{0,1:T(8,128)}, f32[2048,8]{0,1:T(8,128)S(1)}, u32[]{:S(2)}) copy-start(f32[2048,8]{0,1:T(8,128)S(1)} %get-tuple-element.66) | copy-start | bytes 196612
  137.2 8.3 copy-start.46
  139.2 56.6 %copy-start.11 = (bf16[2048,8,8]{0,2,1:T(8,128)(2,1)}, bf16[2048,8,8]{0,2,1:T(8,128)(2,1)S(1)}, u32[]{:S(2)}) copy-start(bf16[2048,8,8]{0,2,1:T(8,128)(2,1)S(1)} %get-tuple-element.57) | copy-start | bytes 786436
  139.2 56.6 %copy-start.13 = (bf16[2048,8,8]{0,2,1:T(8,128)(2,1)}, bf16[2048,8,8]{0,2,1:T(8,128)(2,1)S(1)}, u32[]{:S(2)}) copy-start(bf16[2048,8,8]{0,2,1:T(8,128)(2,1)S(1)} %get-tuple-element.58) | copy-start | bytes 786436
  140.8 236.9 %all-gather.18.cloned.1.call-start = ((), (), s32[]{:S(2)}) async-start(), calls=%async_computation.19 | async-start | bytes 6291456 | tf_op jit(solution)/shard_map/all_gather | solution.py:117
  144.7 323.8 %all-gather.12.cloned.1.call-start = ((), (), s32[]{:S(2)}) async-start(), calls=%async_computation.8 | async-start | bytes 2359296 | tf_op jit(solution)/shard_map/all_gather | solution.py:91
  145.3 486.5 %all-reduce.14.cloned.1.call-start = ((), (), s32[]{:S(2)}) async-start(), calls=%async_computation.9 | async-start | bytes 16777216 | tf_op jit(solution)/shard_map/psum | solution.py:139
  156.5 131.4 %copy-start.8 = (bf16[2048,8,48]{0,2,1:T(8,128)(2,1)}, bf16[2048,8,48]{0,2,1:T(8,128)(2,1)S(1)}, u32[]{:S(2)}) copy-start(bf16[2048,8,48]{0,2,1:T(8,128)(2,1)S(1)} %slice.85) | copy-start | bytes 4718596
  287.9 89.7 %copy-start.19 = (f32[8,2048]{1,0:T(8,128)}, f32[8,2048]{1,0:T(8,128)S(1)}, u32[]{:S(2)}) copy-start(f32[8,2048]{1,0:T(8,128)S(1)} %get-tuple-element.67) | copy-start | bytes 196612
  377.6 90.8 %copy-start.21 = (f32[8,2048]{1,0:T(8,128)}, f32[8,2048]{1,0:T(8,128)S(1)}, u32[]{:S(2)}) copy-start(f32[8,2048]{1,0:T(8,128)S(1)} %fusion) | copy-start | bytes 196612
  478.2 320.0 %all-gather.14.cloned.1.call-start = ((), (), s32[]{:S(2)}) async-start(), calls=%async_computation.10 | async-start | bytes 12976128 | tf_op jit(solution)/shard_map/all_gather | solution.py:145
  480.8 411.2 %all-gather.16.cloned.1.call-start = ((), (), s32[]{:S(2)}) async-start(), calls=%async_computation.11 | async-start | bytes 6488064 | tf_op jit(solution)/shard_map/all_gather | solution.py:146
  481.6 623.7 %all-reduce.16.cloned.1.call-start = ((), (), s32[]{:S(2)}) async-start(), calls=%async_computation.12 | async-start | bytes 16777216 | tf_op jit(solution)/shard_map/psum | solution.py:184
  481.7 637.7 %copy-start.33 = (f32[2048]{0:T(1024)}, f32[2048]{0:T(1024)S(1)}, u32[]{:S(2)}) copy-start(f32[2048]{0:T(1024)S(1)} %convert_element_type.187) | copy-start | bytes 24580
  481.7 316.5 %copy-start.42 = (f32[2048]{0:T(1024)}, f32[2048]{0:T(1024)S(1)}, u32[]{:S(2)}) copy-start(f32[2048]{0:T(1024)S(1)} %convert_element_type.188) | copy-start | bytes 24580
  639.8 479.6 %copy-start.25 = (f32[2048]{0:T(1024)}, f32[2048]{0:T(1024)S(1)}, u32[]{:S(2)}) copy-start(f32[2048]{0:T(1024)S(1)} %broadcast_multiply_fusion) | copy-start | bytes 24580
  649.0 470.3 %copy-start.35 = (f32[2048]{0:T(1024)}, f32[2048]{0:T(1024)S(1)}, u32[]{:S(2)}) copy-start(f32[2048]{0:T(1024)S(1)} %fusion.58) | copy-start | bytes 24580
  954.1 601.9 %reduce-scatter.7.cloned.1.call-start = ((), (), s32[]{:S(2)}) async-start(), calls=%async_computation.13 | async-start | bytes 6291456 | tf_op jit(solution)/shard_map/reduce_scatter | solution.py:233
  1105.3 14.1 copy-start.4
  1105.3 24.3 %slice-start.1 = ((s8[8388608]{0:T(1024)(128)(4,1)}), s8[4194304]{0:T(1024)(128)(4,1)S(1)}, s32[]{:S(2)}) async-start(s8[8388608]{0:T(1024)(128)(4,1)} %bitcast.92), calls=%async_computation.22 | async-start | bytes 8388608
  1119.4 10.3 slice-start.2
  1129.6 5.7 copy-start.2
  1129.6 5.7 copy-start.31
  1135.3 11.3 copy-start.7
  1146.6 157.2 %copy-start.9 = (bf16[2048,8,48]{0,2,1:T(8,128)(2,1)S(1)}, bf16[2048,8,48]{0,2,1:T(8,128)(2,1)}, u32[]{:S(2)}) copy-start(bf16[2048,8,48]{0,2,1:T(8,128)(2,1)} %copy-done.8) | copy-start | bytes 4718596
  1146.6 157.2 %copy-start.12 = (bf16[2048,8,8]{0,2,1:T(8,128)(2,1)S(1)}, bf16[2048,8,8]{0,2,1:T(8,128)(2,1)}, u32[]{:S(2)}) copy-start(bf16[2048,8,8]{0,2,1:T(8,128)(2,1)} %copy-done.11) | copy-start | bytes 786436
  1146.6 157.2 %copy-start.14 = (bf16[2048,8,8]{0,2,1:T(8,128)(2,1)S(1)}, bf16[2048,8,8]{0,2,1:T(8,128)(2,1)}, u32[]{:S(2)}) copy-start(bf16[2048,8,8]{0,2,1:T(8,128)(2,1)} %copy-done.13) | copy-start | bytes 786436
  1350.0 220.4 %reduce-scatter.9.cloned.1.call-start = ((), (), s32[]{:S(2)}) async-start(), calls=%async_computation.14 | async-start | bytes 6291456 | tf_op jit(solution)/shard_map/reduce_scatter | solution.py:236
  1448.1 6.7 copy-start.48
  1454.7 207.8 %reduce-scatter.13.cloned.1.call-start = ((), (), s32[]{:S(2)}) async-start(), calls=%async_computation.16 | async-start | bytes 2359296 | tf_op jit(solution)/shard_map/reduce_scatter | solution.py:258
  1463.8 230.1 %reduce-scatter.17.cloned.1.call-start = ((), (), s32[]{:S(2)}) async-start(), calls=%async_computation.18 | async-start | bytes 6488064 | tf_op jit(solution)/shard_map/reduce_scatter | solution.py:180
  1482.0 503.8 %all-reduce.18.cloned.1.call-start = ((), (), s32[]{:S(2)}) async-start(), calls=%async_computation.20 | async-start | bytes 33554432 | tf_op jit(solution)/shard_map/psum | solution.py:160
  1556.0 4.9 copy-start.1
  1556.0 5.2 slice-start
  1588.8 593.2 %reduce-scatter.15.cloned.1.call-start = ((), (), s32[]{:S(2)}) async-start(), calls=%async_computation.17 | async-start | bytes 12976128 | tf_op jit(solution)/shard_map/reduce_scatter | solution.py:177
  1635.0 668.0 %reduce-scatter.11.cloned.1.call-start = ((), (), s32[]{:S(2)}) async-start(), calls=%async_computation.15 | async-start | bytes 7077888 | tf_op jit(solution)/shard_map/reduce_scatter | solution.py:255
  1990.5 9.5 copy-start.38
  1990.5 9.6 copy-start.3
  2000.1 10.5 copy-start.39
  2000.1 53.3 %copy-start.32 = (f32[2048]{0:T(1024)S(1)}, f32[2048]{0:T(1024)}, u32[]{:S(2)}) copy-start(f32[2048]{0:T(1024)} %copy-done.31) | copy-start | bytes 24580
  (19 other events, 34.0 us)
Sparse Core Ops, SparseCore 0:
  10.6 102.6 all-gather.7
  140.9 54.9 all-gather.9
  197.4 56.7 all-gather.17
  256.1 51.0 all-gather.11
  478.3 153.3 all-reduce.13
  634.4 163.7 all-gather.13
  800.2 91.7 all-gather.15
  954.2 151.0 all-reduce.15
  1350.1 54.4 reduce-scatter.6
  1454.8 54.4 reduce-scatter.8
  1512.8 68.1 reduce-scatter.12
  1584.5 109.3 reduce-scatter.16
  1697.1 288.6 all-reduce.17
  1989.2 192.7 reduce-scatter.14
  2185.4 117.4 reduce-scatter.10
where the time goes:
time: 2320 us; the launch traced here: 2310 us
  waiting for transfers between devices  1170 us (50%)
  matrix products  807 us (35%)
  other arithmetic  232 us (10%)
  local copies, waits for them, and re-layouts  44.1 us (2%)
  blocking collectives  39.7 us (2%)
    psum x1, waiting for transfers between devices, body(): lax.psum(jnp.dot(hidden, down_full, preferred_element_type=jnp.float32).a...  286 us
    dot_general x1, matrix products, body(): jnp.einsum('qhd,khd->hqk', d_attended, value_block, preferred_element_typ...  157 us
    psum x1, waiting for transfers between devices, body(): lax.psum(jnp.einsum('tkf,dkf->td', d_gate_up, gate_up_back, preferred_ele...  150 us
    psum x1, waiting for transfers between devices, body(): lax.psum(jnp.dot(attended_low, out_full, preferred_element_type=jnp.float...  150 us
    all_gather x1, waiting for transfers between devices, body(): lax.all_gather(w_gate_up, ('dp', 'ctx'), axis=0, tiled=True)  149 us
    reduce_scatter x1, waiting for transfers between devices, body(): lax.psum_scatter(grad_qkv.astype(jnp.bfloat16), ('dp', 'ctx'), scatter_di...  117 us
    reduce_scatter x1, waiting for transfers between devices, body(): lax.psum_scatter(grad_gate_up.astype(jnp.bfloat16), ('dp', 'ctx'), scatte...  101 us
    dot_general x1, matrix products, body(): jnp.einsum('hqk,qhd->khd', chances.astype(jnp.bfloat16), d_attended, pref...  98.1 us
  transfers between devices with their start and end apart: 15, of which 10 were waited for; matrix products, arithmetic and copies ran while one was open for 32% of the time, Pallas kernels for 0%

commit v1 on v0

v1 whole, which is shorter than its diff:
```python
import functools
import math

import jax
import jax.numpy as jnp
from jax import lax
from jax.experimental import pallas as pl
from jax.experimental.pallas import tpu as pltpu
from jax.sharding import PartitionSpec as P

HD = 64
ROT = 16
TILE = 128
VMEM_LIMIT = 60 * 1024 * 1024
LOW_SCORE = -1e30
START_TOP = -1e20


def layer_norm(values, norm_gain, norm_shift):
    row_mean = jnp.mean(values, axis=-1, keepdims=True)
    centred = values - row_mean
    spread = jnp.mean(centred * centred, axis=-1, keepdims=True)
    return centred * lax.rsqrt(spread + 1e-05) * norm_gain + norm_shift


def dot_f32(left, right, left_dim, right_dim):
    return lax.dot_general(
        left, right, (((left_dim,), (right_dim,)), ((), ())), preferred_element_type=jnp.float32
    )


def spin(values, cosine, sine, lanes):
    if lanes % 128 == 0:
        ahead = pltpu.roll(values, lanes - ROT // 2, 1)
        behind = pltpu.roll(values, ROT // 2, 1)
    else:
        half_rot = ROT // 2
        ahead = jnp.concatenate([values[:, half_rot:], values[:, :half_rot]], axis=1)
        behind = jnp.concatenate([values[:, -half_rot:], values[:, :-half_rot]], axis=1)
    lane = lax.broadcasted_iota(jnp.int32, values.shape, 1) % HD
    return values * cosine + jnp.where(lane < ROT // 2, ahead, behind) * sine


def begin_of(places, len_ref, seqs):
    begin = jnp.zeros_like(places)
    end = jnp.int32(0)
    for index in range(seqs):
        end = end + len_ref[index]
        begin = jnp.where(places >= end, end, begin)
    return begin


def begin_scalar(place, len_ref, seqs):
    begin = jnp.int32(0)
    end = jnp.int32(0)
    for index in range(seqs):
        end = end + len_ref[index]
        begin = jnp.where(place >= end, end, begin)
    return begin


def finish_scalar(place, len_ref, seqs):
    finish = jnp.int32(0)
    end = jnp.int32(0)
    for index in range(seqs):
        finish = jnp.where(place >= end, end + len_ref[index], finish)
        end = end + len_ref[index]
    return finish


def fold_rows(values):
    return jnp.sum(values.reshape(-1, 8, values.shape[1]), axis=0)


def head_masks(rows, lanes, heads):
    lane = lax.broadcasted_iota(jnp.int32, (rows, lanes), 1)
    return [(lane // HD) == index for index in range(heads)]


def attend_kernel(parts, tiles, width, stream, seqs, block, slot_ref, len_ref, *refs):
    qkv_ref, cos_ref, sin_ref = refs[:3]
    out_parts = refs[3 : parts + 3]
    sorted_ref, mixed_ref, lse_ref = refs[parts + 3 : parts + 6]
    loaded, value_aug, load_sem, store_sem = refs[parts + 6 :]
    lanes = min(128, width)
    per_group = lanes // HD
    groups = width // lanes

    @pl.loop(0, parts * tiles)
    def _(tile):
        place = pl.multiple_of(slot_ref[tile] * TILE, TILE)
        row = pl.multiple_of(tile * TILE, TILE)
        pltpu.make_async_copy(
            qkv_ref.at[pl.ds(row, TILE)], loaded.at[pl.ds(place, TILE)], load_sem
        ).start()

    pltpu.make_async_copy(loaded, loaded, load_sem).wait()

    @pl.loop(0, stream // 256)
    def _(step):
        rows = pl.ds(pl.multiple_of(step * 256, 256), 256)
        cosine, sine = cos_ref[rows, :], sin_ref[rows, :]
        masks = head_masks(256, lanes, per_group)
        for group in range(groups):
            cols = slice(group * lanes, (group + 1) * lanes)
            query = spin(loaded[rows, cols].astype(jnp.float32), cosine, sine, lanes)
            query = query.astype(jnp.bfloat16) * jnp.bfloat16(HD**-0.5)
            sorted_ref[rows, cols] = query
            cols = slice(width + group * lanes, width + (group + 1) * lanes)
            key = spin(loaded[rows, cols].astype(jnp.float32), cosine, sine, lanes)
            sorted_ref[rows, cols] = key.astype(jnp.bfloat16)
            cols = slice(2 * width + group * lanes, 2 * width + (group + 1) * lanes)
            value = loaded[rows, cols]
            sorted_ref[rows, cols] = value
            ones = jnp.ones((256, lanes), jnp.bfloat16)
            for index in range(per_group):
                head = group * per_group + index
                if per_group == 2:
                    value_aug[rows, head * 128 : (head + 1) * 128] = jnp.where(
                        masks[index], value, ones
                    )
                else:
                    value_aug[rows, head * 128 : head * 128 + HD] = value
                    value_aug[rows, head * 128 + HD : (head + 1) * 128] = ones

    for group in range(groups):
        cols = slice(group * lanes, (group + 1) * lanes)
        key_cols = slice(width + group * lanes, width + (group + 1) * lanes)

        @pl.loop(0, stream // block)
        def _(index):
            first = index * block
            rows = pl.ds(pl.multiple_of(first, block), block)
            query = sorted_ref[rows, cols]
            masks = head_masks(block, lanes, per_group)
            query_heads = [jnp.where(mask, query, jnp.bfloat16(0)) for mask in masks]
            place = first + lax.broadcasted_iota(jnp.int32, (block, 1), 0)
            begin = begin_of(place, len_ref, seqs)
            begin_low = begin_scalar(first, len_ref, seqs)
            begin_high = begin_scalar(first + block - 1, len_ref, seqs)

            def step(number, carry, masked):
                start = number * block
                key_rows = pl.ds(pl.multiple_of(start, block), block)
                key = sorted_ref[key_rows, key_cols]
                out = []
                for which in range(per_group):
                    top, total = carry[which]
                    head = group * per_group + which
                    scores = dot_f32(query_heads[which], key, 1, 1)
                    if masked:
                        key_place = start + lax.broadcasted_iota(jnp.int32, (1, block), 1)
                        visible = (key_place <= place) & (key_place >= begin)
                        scores = jnp.where(visible, scores, LOW_SCORE)
                    new_top = jnp.maximum(top, jnp.max(scores, axis=1, keepdims=True))
                    expw = jnp.exp(scores - new_top).astype(jnp.bfloat16)
                    shrink = jnp.exp(top - new_top)
                    mixed = dot_f32(
                        expw, value_aug[key_rows, head * 128 : (head + 1) * 128], 1, 0
                    )
                    out.append((new_top, total * shrink + mixed))
                return tuple(out)

            carry = tuple(
                (jnp.full((block, 1), START_TOP, jnp.float32), jnp.zeros((block, 128), jnp.float32))
                for _ in range(per_group)
            )
            first_block = begin_low // block
            inner = jnp.minimum((begin_high + block - 1) // block, index)
            carry = lax.fori_loop(
                first_block, inner, functools.partial(step, masked=True), carry
            )
            carry = lax.fori_loop(inner, index, functools.partial(step, masked=False), carry)
            carry = step(index, carry, True)
            lane = lax.broadcasted_iota(jnp.int32, (block, 128), 1)
            mixed, logs = [], []
            for which in range(per_group):
                top, total = carry[which]
                swapped = pltpu.roll(total, HD, 1)
                own = (lane // HD) == which
                sums = jnp.where(own, swapped, total)
                mixed.append(total / sums)
                logs.append(top + jnp.log(sums))
            if per_group == 2:
                both = jnp.where(lane < HD, mixed[0], mixed[1])
                log_both = jnp.where(lane < HD, logs[0], logs[1])
            else:
                both = mixed[0][:, :HD]
                log_both = logs[0]
            mixed_ref[rows, cols] = both.astype(jnp.bfloat16)
            turned = jnp.transpose(log_both)
            for which in range(per_group):
                head = group * per_group + which
                lse_ref[head : head + 1, rows] = turned[which * HD : which * HD + 1, :]

    for part in range(parts):

        @pl.loop(0, tiles)
        def _(tile, part=part):
            place = pl.multiple_of(slot_ref[part * tiles + tile] * TILE, TILE)
            row = pl.multiple_of(tile * TILE, TILE)
            pltpu.make_async_copy(
                mixed_ref.at[pl.ds(place, TILE)], out_parts[part].at[pl.ds(row, TILE)], store_sem
            ).start()

    pltpu.make_async_copy(mixed_ref, mixed_ref, store_sem).wait()


def attend(slots, lengths, projected, tables, count):
    stream, triple = projected.shape
    rows = stream // count
    width = triple // 3
    heads = width // HD
    block = min(512, stream)
    anywhere = pl.BlockSpec(memory_space=pl.ANY)
    whole = pl.BlockSpec(memory_space=pltpu.VMEM)
    kernel = functools.partial(
        attend_kernel, count, rows // TILE, width, stream, lengths.shape[0], block
    )
    pairs = stream * stream // 3 * heads
    outs = pl.pallas_call(
        kernel,
        name="attention_forward",
        out_shape=[jax.ShapeDtypeStruct((rows, width), jnp.bfloat16)] * count
        + [
            jax.ShapeDtypeStruct((stream, triple), jnp.bfloat16),
            jax.ShapeDtypeStruct((stream, width), jnp.bfloat16),
            jax.ShapeDtypeStruct((max(heads, 8), stream), jnp.float32),
        ],
        in_specs=[pl.BlockSpec(memory_space=pltpu.SMEM)] * 2 + [anywhere, whole, whole],
        out_specs=[anywhere] * count + [whole] * 3,
        scratch_shapes=[
            pltpu.VMEM((stream, triple), jnp.bfloat16),
            pltpu.VMEM((stream, heads * 128), jnp.bfloat16),
            pltpu.SemaphoreType.DMA,
            pltpu.SemaphoreType.DMA,
        ],
        compiler_params=pltpu.CompilerParams(vmem_limit_bytes=VMEM_LIMIT),
        cost_estimate=pl.CostEstimate(
            flops=pairs * 4 * 256, bytes_accessed=stream * width * 20, transcendentals=pairs
        ),
    )(slots, lengths, projected, *tables)
    return outs[:count], outs[count], outs[count + 1], outs[count + 2]


def attend_back_kernel(
    given, column, width, stream, seqs, block, slot_ref, len_ref, *refs
):
    back_parts = refs[:given]
    sorted_ref, mixed_ref, lse_ref, cos_ref, sin_ref, out_ref, sums_ref = refs[given : given + 7]
    back, grads, query_grad, delta, load_sem, store_sem = refs[given + 7 :]
    given_tiles = stream // TILE // given
    lanes = min(128, width)
    per_group = lanes // HD
    groups = width // lanes
    for part in range(given):

        @pl.loop(0, given_tiles)
        def _(tile, part=part):
            place = pl.multiple_of(slot_ref[part * given_tiles + tile] * TILE, TILE)
            row = pl.multiple_of(tile * TILE, TILE)
            pltpu.make_async_copy(
                back_parts[part].at[pl.ds(row, TILE), pl.ds(column, width)],
                back.at[pl.ds(place, TILE)],
                load_sem,
            ).start()

    pltpu.make_async_copy(back, back, load_sem).wait()

    for group in range(groups):
        cols = slice(group * lanes, (group + 1) * lanes)
        key_cols = slice(width + group * lanes, width + (group + 1) * lanes)
        value_cols = slice(2 * width + group * lanes, 2 * width + (group + 1) * lanes)
        query_grad[...] = jnp.zeros_like(query_grad)
        sums_ref[...] = jnp.zeros_like(sums_ref)

        @pl.loop(0, stream // block)
        def _(index):
            rows = pl.ds(pl.multiple_of(index * block, block), block)
            product = back[rows, cols].astype(jnp.float32) * mixed_ref[rows, cols].astype(
                jnp.float32
            )
            pick = (
                lax.broadcasted_iota(jnp.int32, (8, lanes), 1) // HD
                == lax.broadcasted_iota(jnp.int32, (8, lanes), 0)
            ).astype(jnp.float32)
            delta[:, rows] = lax.dot_general(
                pick,
                product,
                (((1,), (1,)), ((), ())),
                precision=lax.Precision.HIGHEST,
                preferred_element_type=jnp.float32,
            )

        @pl.loop(0, stream // block)
        def _(index):
            first = index * block
            key_rows = pl.ds(pl.multiple_of(first, block), block)
            key = sorted_ref[key_rows, key_cols]
            value = sorted_ref[key_rows, value_cols]
            masks = head_masks(block, lanes, per_group)
            key_heads = [jnp.where(mask, key, jnp.bfloat16(0)) for mask in masks]
            key_place = first + lax.broadcasted_iota(jnp.int32, (block, 1), 0)
            finish_low = finish_scalar(first, len_ref, seqs)
            finish_high = finish_scalar(first + block - 1, len_ref, seqs)

            def step(number, carry, masked):
                key_grad, value_grad = carry
                start = number * block
                rows = pl.ds(pl.multiple_of(start, block), block)
                query = sorted_ref[rows, cols]
                upstream = back[rows, cols]
                query_add = None
                if masked:
                    place = start + lax.broadcasted_iota(jnp.int32, (1, block), 1)
                    begin = begin_of(place, len_ref, seqs)
                    visible = (key_place <= place) & (key_place >= begin)
                for which in range(per_group):
                    head = group * per_group + which
                    query_head = jnp.where(masks[which], query, jnp.bfloat16(0))
                    back_head = jnp.where(masks[which], upstream, jnp.bfloat16(0))
                    scores = dot_f32(key, query_head, 1, 1)
                    if masked:
                        scores = jnp.where(visible, scores, LOW_SCORE)
                    chances = jnp.exp(scores - lse_ref[head : head + 1, rows])
                    d_chances = dot_f32(value, back_head, 1, 1)
                    d_raw = (chances * (d_chances - delta[which : which + 1, rows])).astype(
                        jnp.bfloat16
                    )
                    value_grad = value_grad + dot_f32(
                        chances.astype(jnp.bfloat16), back_head, 1, 0
                    )
                    key_grad = key_grad + dot_f32(d_raw, query_head, 1, 0)
                    part_add = dot_f32(d_raw, key_heads[which], 0, 0)
                    query_add = part_add if query_add is None else query_add + part_add
                query_grad[rows, :] += query_add
                return (key_grad, value_grad)

            zeros = jnp.zeros((block, lanes), jnp.float32)
            carry = step(index, (zeros, zeros), True)
            inner = jnp.maximum(finish_low // block, index + 1)
            last = jnp.maximum((finish_high + block - 1) // block, inner)
            carry = lax.fori_loop(
                index + 1, inner, functools.partial(step, masked=False), carry
            )
            carry = lax.fori_loop(inner, last, functools.partial(step, masked=True), carry)
            key_grad = spin(carry[0], cos_ref[key_rows, :], -sin_ref[key_rows, :], lanes)
            grads[key_rows, key_cols] = key_grad.astype(jnp.bfloat16)
            grads[key_rows, value_cols] = carry[1].astype(jnp.bfloat16)
            sums_ref[:, key_cols] += fold_rows(key_grad)
            sums_ref[:, value_cols] += fold_rows(carry[1])

        @pl.loop(0, stream // 256)
        def _(step):
            rows = pl.ds(pl.multiple_of(step * 256, 256), 256)
            turned = spin(query_grad[rows, :], cos_ref[rows, :], -sin_ref[rows, :], lanes)
            turned = turned * (HD**-0.5)
            grads[rows, cols] = turned.astype(jnp.bfloat16)
            sums_ref[:, cols] += fold_rows(turned)

    @pl.loop(0, stream // TILE)
    def _(tile):
        place = pl.multiple_of(slot_ref[tile] * TILE, TILE)
        row = pl.multiple_of(tile * TILE, TILE)
        pltpu.make_async_copy(
            grads.at[pl.ds(place, TILE)], out_ref.at[pl.ds(row, TILE)], store_sem
        ).start()

    pltpu.make_async_copy(grads, grads, store_sem).wait()


def attend_back(slots, lengths, parts, column, kept, mixed, lse, tables):
    stream, width = mixed.shape
    heads = width // HD
    block = min(512, stream)
    lanes = min(128, width)
    anywhere = pl.BlockSpec(memory_space=pl.ANY)
    whole = pl.BlockSpec(memory_space=pltpu.VMEM)
    kernel = functools.partial(
        attend_back_kernel, len(parts), column, width, stream, lengths.shape[0], block
    )
    pairs = stream * stream // 3 * heads
    return pl.pallas_call(
        kernel,
        name="attention_backward",
        out_shape=[
            jax.ShapeDtypeStruct((stream, 3 * width), jnp.bfloat16),
            jax.ShapeDtypeStruct((8, 3 * width), jnp.float32),
        ],
        in_specs=[pl.BlockSpec(memory_space=pltpu.SMEM)] * 2
        + [anywhere] * len(parts)
        + [whole] * 5,
        out_specs=[anywhere, whole],
        scratch_shapes=[
            pltpu.VMEM((stream, width), jnp.bfloat16),
            pltpu.VMEM((stream, 3 * width), jnp.bfloat16),
            pltpu.VMEM((stream, lanes), jnp.float32),
            pltpu.VMEM((8, stream), jnp.float32),
            pltpu.SemaphoreType.DMA,
            pltpu.SemaphoreType.DMA,
        ],
        compiler_params=pltpu.CompilerParams(vmem_limit_bytes=VMEM_LIMIT),
        cost_estimate=pl.CostEstimate(
            flops=pairs * 10 * 256, bytes_accessed=stream * width * 20, transcendentals=pairs
        ),
    )(slots, lengths, *parts, kept, mixed, lse, *tables)


def rotary_kernel(lanes, table_ref, cos_ref, sin_ref):
    half_rot = ROT // 2
    lane = lax.broadcasted_iota(jnp.int32, (half_rot, lanes), 1) % HD
    entry = lax.broadcasted_iota(jnp.int32, (half_rot, lanes), 0)
    first, second = lane == entry, lane == entry + half_rot
    pick_cos = (first | second).astype(jnp.float32)
    pick_sin = second.astype(jnp.float32) - first.astype(jnp.float32)

    def spread(values, pick):
        return lax.dot_general(
            values,
            pick,
            (((0,), (0,)), ((), ())),
            precision=lax.Precision.HIGHEST,
            preferred_element_type=jnp.float32,
        )

    still = (lax.broadcasted_iota(jnp.int32, (1, lanes), 1) % HD >= ROT).astype(jnp.float32)
    cos_ref[...] = spread(table_ref[:half_rot, :], pick_cos) + still
    sin_ref[...] = spread(table_ref[half_rot:, :], pick_sin)


def rotary_tables(table, lanes):
    stream = table.shape[1]
    block = min(512, stream)
    return pl.pallas_call(
        functools.partial(rotary_kernel, lanes),
        name="rotary_tables",
        grid=(stream // block,),
        in_specs=[pl.BlockSpec((ROT, block), lambda step: (0, step))],
        out_specs=[pl.BlockSpec((block, lanes), lambda step: (step, 0))] * 2,
        out_shape=[jax.ShapeDtypeStruct((stream, lanes), jnp.float32)] * 2,
        cost_estimate=pl.CostEstimate(
            flops=stream * lanes * 100, bytes_accessed=stream * lanes * 8, transcendentals=0
        ),
    )(table)


def project_kernel(sources, groups, slab, map_ref, *refs):
    inputs = refs[:sources]
    gain_ref, shift_ref, weight_ref, bias_ref = refs[sources : sources + 4]
    outs = refs[len(refs) - groups - 1 :]

    def run(source):
        values = source[...].astype(jnp.float32)
        normed = layer_norm(values, gain_ref[...], shift_ref[...]).astype(jnp.bfloat16)
        outs[0][...] = normed
        result = dot_f32(normed, weight_ref[...], 1, 0) + bias_ref[...]
        for group in range(groups):
            outs[1 + group][...] = result[:, group * slab : (group + 1) * slab].astype(
                jnp.bfloat16
            )

    if sources == 1:
        run(inputs[0])
    else:
        for index in range(sources):

            @pl.when(pl.program_id(0) == index)
            def _(index=index):
                run(inputs[index])


def project(blocks, sources, gain, shift, weight, bias, groups, rows, first, kept):
    features, triple = weight.shape
    slab = triple // groups
    count = len(sources)
    steps = blocks.shape[0] if count == 1 else count
    size = math.gcd(256, sources[0].shape[0])
    kept = [] if kept is None else kept
    fixed = lambda step, order: (0, 0)
    placed = lambda step, order: (first + step, 0)
    if count == 1:
        specs = [pl.BlockSpec((size, features), lambda step, order: (order[step], 0))]
    else:
        specs = [pl.BlockSpec((size, features), fixed)] * count
    specs += [
        pl.BlockSpec((1, features), fixed),
        pl.BlockSpec((1, features), fixed),
        pl.BlockSpec((features, triple), fixed),
        pl.BlockSpec((1, triple), fixed),
    ]
    specs += [pl.BlockSpec(memory_space=pl.ANY)] * len(kept)
    work = steps * size
    return pl.pallas_call(
        functools.partial(project_kernel, count, groups, slab),
        name="norm_project",
        grid_spec=pltpu.PrefetchScalarGridSpec(
            num_scalar_prefetch=1,
            grid=(steps,),
            in_specs=specs,
            out_specs=[pl.BlockSpec((size, features), placed)]
            + [pl.BlockSpec((size, slab), placed)] * groups,
        ),
        out_shape=[jax.ShapeDtypeStruct((rows, features), jnp.bfloat16)]
        + [jax.ShapeDtypeStruct((rows, slab), jnp.bfloat16)] * groups,
        input_output_aliases={count + 5 + index: index for index in range(len(kept))},
        compiler_params=pltpu.CompilerParams(vmem_limit_bytes=VMEM_LIMIT),
        cost_estimate=pl.CostEstimate(
            flops=2 * work * features * triple,
            bytes_accessed=work * features * 4 + features * triple * 2,
            transcendentals=0,
        ),
    )(blocks, *sources, gain, shift, weight, bias, *kept)


def place_kernel(count, at_ref, *refs):
    for index in range(count):

        @pl.when(pl.program_id(0) == index)
        def _(index=index):
            refs[count][...] = refs[index][...]


def place_rows(at, pieces):
    size, features = pieces[0].shape
    count = len(pieces)
    return pl.pallas_call(
        functools.partial(place_kernel, count),
        name="place_rows",
        grid_spec=pltpu.PrefetchScalarGridSpec(
            num_scalar_prefetch=1,
            grid=(count,),
            in_specs=[once((size, features))] * count,
            out_specs=pl.BlockSpec((size, features), lambda step, order: (order[step], 0)),
        ),
        out_shape=jax.ShapeDtypeStruct((size * count, features), pieces[0].dtype),
        compiler_params=pltpu.CompilerParams(vmem_limit_bytes=VMEM_LIMIT),
        cost_estimate=pl.CostEstimate(
            flops=0, bytes_accessed=size * count * features * 4, transcendentals=0
        ),
    )(at, *pieces)


def once(shape):
    return pl.BlockSpec(shape, lambda *_: (0, 0), pipeline_mode=pl.Buffered(1))


def column_tiles(columns):
    return [(start, min(512, columns - start)) for start in range(0, columns, 512)]


def store_half(step, keep_ref, send_ref, cols, values):
    values = values.astype(jnp.bfloat16)

    @pl.when(step == 0)
    def _():
        send_ref[:, cols] = values

    @pl.when(step == 1)
    def _():
        keep_ref[:, cols] = values


def matmul_call(kernel, name, half, in_specs, out_specs, out_shape, scratch, flops, args):
    bytes_moved = sum(a.size * a.dtype.itemsize for a in args)
    bytes_moved += sum(math.prod(o.shape) * o.dtype.itemsize for o in out_shape)
    return pl.pallas_call(
        kernel,
        name=name,
        grid=(2,),
        in_specs=in_specs,
        out_specs=out_specs,
        out_shape=out_shape,
        scratch_shapes=scratch,
        compiler_params=pltpu.CompilerParams(vmem_limit_bytes=VMEM_LIMIT),
        cost_estimate=pl.CostEstimate(flops=flops, bytes_accessed=bytes_moved, transcendentals=0),
    )(*args)


def low_shape(*shape):
    return jax.ShapeDtypeStruct(shape, jnp.bfloat16)


def out_kernel(count, groups, lanes, holder_ref, *refs):
    parts = refs[: count * groups]
    weight_ref, keep_ref, send_ref, attended_ref = refs[count * groups :]
    step = pl.program_id(0)
    for s in range(count):
        for c in range(count):

            @pl.when(holder_ref[s] == c)
            def _(s=s, c=c):
                for group in range(groups):
                    first = (c * groups + group) * lanes
                    attended_ref[:, first : first + lanes] = parts[s * groups + group][...]

    for start, size in column_tiles(weight_ref.shape[1]):
        cols = slice(start, start + size)
        result = dot_f32(attended_ref[...], weight_ref[:, cols], 1, 0)
        store_half(step, keep_ref, send_ref, cols, result)


def project_out(holders, parts, count, groups, weight, chunk, half):
    width, features = weight.shape
    lanes = parts[0].shape[1]
    part_spec = pl.BlockSpec((half, lanes), lambda step: (chunk * 2 + 1 - step, 0))
    return matmul_call(
        functools.partial(out_kernel, count, groups, lanes),
        "project_out",
        half,
        [pl.BlockSpec(memory_space=pltpu.SMEM)]
        + [part_spec] * len(parts)
        + [once((width, features))],
        [
            pl.BlockSpec((half, features), lambda step: (0, 0)),
            pl.BlockSpec((half, features), lambda step: (0, 0)),
            pl.BlockSpec((half, width), lambda step: (1 - step, 0)),
        ],
        [low_shape(half, features), low_shape(half, features), low_shape(2 * half, width)],
        [],
        4 * half * features * width,
        (holders, *parts, weight),
    )


def collect(step, pieces, out_ref, first_step):
    half = len(pieces) // 2
    size = pieces[0].shape[0]
    for number in range(2):

        @pl.when(step == number)
        def _(number=number):
            chosen = pieces[half:] if number == first_step else pieces[:half]
            for index, piece in enumerate(chosen):
                out_ref[index * size : (index + 1) * size, :] = piece[...]


def feed_kernel(count, hidden, *refs):
    pieces = refs[:count]
    d_hidden_ref, weight_ref = refs[count : count + 2]
    normed_ref, hidden_ref, grad_ref, keep_ref, send_ref = refs[count + 2 : count + 7]
    weight, weight_sems, piece_sems = refs[count + 7 :]
    step = pl.program_id(0)
    size = pieces[0].shape[0]
    half = count // 2

    def piece_copy(index, number):
        row = index * size
        return pltpu.make_async_copy(
            pieces[half * (1 - number) + index],
            normed_ref.at[pl.ds(row, size)],
            piece_sems.at[index],
        )

    columns = [
        (first, width)
        for start, width in column_tiles(hidden)
        for first in (start, hidden + start)
    ]
    copies = [
        pltpu.make_async_copy(
            weight_ref.at[:, pl.ds(start, width)],
            weight.at[:, pl.ds(start, width)],
            weight_sems.at[number],
        )
        for number, (start, width) in enumerate(columns)
    ]

    @pl.when(step == 0)
    def _():
        for index in range(half):
            piece_copy(index, 0).start()
        for copy in copies:
            copy.start()
        for index in range(half):
            piece_copy(index, 0).wait()

    @pl.when(step == 1)
    def _():
        for index in range(half):
            piece_copy(index, 1).start()
        for index in range(half):
            piece_copy(index, 1).wait()

    for number, (start, width) in enumerate(column_tiles(hidden)):

        @pl.when(step == 0)
        def _(number=number):
            copies[2 * number].wait()
            copies[2 * number + 1].wait()

        gate_cols = slice(start, start + width)
        up_cols = slice(hidden + start, hidden + start + width)
        gate = dot_f32(normed_ref[...], weight[:, gate_cols], 1, 0)
        up = dot_f32(normed_ref[...], weight[:, up_cols], 1, 0)
        sigmoid = 1.0 / (1.0 + jnp.exp(-gate))
        silu = gate * sigmoid
        d_hidden = d_hidden_ref[:, gate_cols]
        hidden_ref[:, gate_cols] = (silu * up).astype(jnp.bfloat16)
        d_gate = d_hidden * up * sigmoid * (1.0 + gate * (1.0 - sigmoid))
        grad_ref[:, gate_cols] = d_gate.astype(jnp.bfloat16)
        grad_ref[:, up_cols] = (d_hidden * silu).astype(jnp.bfloat16)

    for start, width in column_tiles(weight.shape[0]):
        cols = slice(start, start + width)
        result = dot_f32(grad_ref[...], weight[cols, :], 1, 1)
        store_half(step, keep_ref, send_ref, cols, result)


def feed_forward(pieces, d_hidden, weight):
    share, features = pieces[0].shape
    half = share * len(pieces) // 2
    hidden = d_hidden.shape[1]
    placed = lambda step: (1 - step, 0)
    anywhere = pl.BlockSpec(memory_space=pl.ANY)
    copies = 2 * len(column_tiles(hidden))
    return matmul_call(
        functools.partial(feed_kernel, len(pieces), hidden),
        "feed_forward",
        half,
        [anywhere] * len(pieces) + [pl.BlockSpec((half, hidden), placed), anywhere],
        [
            pl.BlockSpec((half, features), placed),
            pl.BlockSpec((half, hidden), placed),
            pl.BlockSpec((half, 2 * hidden), placed),
            pl.BlockSpec((half, features), lambda step: (0, 0)),
            pl.BlockSpec((half, features), lambda step: (0, 0)),
        ],
        [
            low_shape(2 * half, features),
            low_shape(2 * half, hidden),
            low_shape(2 * half, 2 * hidden),
            low_shape(half, features),
            low_shape(half, features),
        ],
        [
            pltpu.VMEM((features, 2 * hidden), jnp.bfloat16),
            pltpu.SemaphoreType.DMA((copies,)),
            pltpu.SemaphoreType.DMA((len(pieces) // 2,)),
        ],
        16 * half * features * hidden,
        (*pieces, d_hidden, weight),
    )


def out_back_kernel(count, pieces, width, holder_ref, *refs):
    sources = refs[:pieces]
    weight_ref, gathered_ref = refs[pieces : pieces + 2]
    outs = refs[pieces + 2 : pieces + 2 + count]
    step = pl.program_id(0)
    collect(step, sources, gathered_ref, 0)
    result = dot_f32(gathered_ref[...], weight_ref[...], 1, 0).astype(jnp.bfloat16)
    for s in range(count):
        for c in range(count):

            @pl.when(holder_ref[s] == c)
            def _(s=s, c=c):
                outs[s][...] = result[:, c * width : (c + 1) * width]


def project_out_back(holders, pieces, weight, count):
    share, features = pieces[0].shape
    half = share * len(pieces) // 2
    total = weight.shape[1]
    width = total // count
    placed = lambda step: (1 - step, 0)
    outs = matmul_call(
        functools.partial(out_back_kernel, count, len(pieces), width),
        "project_out_back",
        half,
        [pl.BlockSpec(memory_space=pltpu.SMEM)]
        + [once((share, features))] * len(pieces)
        + [once((features, total))],
        [pl.BlockSpec((half, features), placed)] + [pl.BlockSpec((half, width), placed)] * count,
        [low_shape(2 * half, features)] + [low_shape(2 * half, width)] * count,
        [],
        4 * half * features * total,
        (holders, *pieces, weight),
    )
    return outs[0], list(outs[1:])


def norm_back_kernel(count, groups, slab, *refs):
    parts = refs[: count * groups]
    weights = refs[count * groups : count * groups + count]
    keep_ref, send_ref, joined = refs[count * groups + count :]
    step = pl.program_id(0)
    if groups > 1:
        for index, part in enumerate(parts):
            joined[:, index * slab : (index + 1) * slab] = part[...]

    for start, size in column_tiles(weights[0].shape[1]):
        cols = slice(start, start + size)
        total = None
        for s in range(count):
            if groups > 1:
                left = joined[:, s * groups * slab : (s + 1) * groups * slab]
            else:
                left = parts[s][...]
            product = dot_f32(left, weights[s][:, cols], 1, 0)
            total = product if total is None else total + product
        store_half(step, keep_ref, send_ref, cols, total)


def project_back(parts, weights, groups, chunk, half):
    wide, features = weights[0].shape
    count = len(weights)
    slab = wide // groups

    def spec(first):
        return pl.BlockSpec(
            (half, slab), lambda step: (first // half + chunk * 2 + 1 - step, 0)
        )

    return matmul_call(
        functools.partial(norm_back_kernel, count, groups, slab),
        "project_back",
        half,
        [spec(first) for _, first in parts] + [once((wide, features))] * count,
        [pl.BlockSpec((half, features), lambda step: (0, 0))] * 2,
        [low_shape(half, features)] * 2,
        [pltpu.VMEM((half, count * wide), jnp.bfloat16)],
        4 * half * features * wide * count,
        (*(array for array, _ in parts), *weights),
    )


def swap_bit(values, axis, bit):
    size = lax.axis_size(axis)
    return lax.ppermute(values, axis, [(i, i ^ (1 << bit)) for i in range(size)])


def sum_over_tensor(keep, send, bits):
    return sum_further(sum_first(keep, send), bits)


def sum_first(keep, send):
    return keep.astype(jnp.float32) + swap_bit(send, "tensor", 0).astype(jnp.float32)


def sum_further(total, bits):
    for bit in range(1, bits):
        half = total.shape[0] // 2
        arrived = swap_bit(total[half:].astype(jnp.bfloat16), "tensor", bit)
        total = total[:half] + arrived.astype(jnp.float32)
    return total


def gather_pieces(own, bits):
    return gather_rest(gather_first(own, bits), bits)


def gather_first(own, bits):
    return [own, swap_bit(own, "tensor", bits - 1)]


def gather_rest(pieces, bits):
    for bit in reversed(range(bits - 1)):
        pieces = pieces + [swap_bit(piece, "tensor", bit) for piece in pieces]
    return pieces


def butterfly(values):
    for axis in ("tensor", "ctx", "dp"):
        for bit in reversed(range(lax.axis_size(axis).bit_length() - 1)):
            values = values + swap_bit(values, axis, bit)
    return values


def shift_over(values, axis, shift):
    size = lax.axis_size(axis)
    return lax.ppermute(values, axis, [(i, (i - shift) % size) for i in range(size)])


def exchange(pieces):
    count = len(pieces)
    arrived = [pieces[0]] + [None] * (count - 1)
    for shift in range(1, count):
        arrived[count - shift] = shift_over(pieces[shift], "ctx", shift)
    return arrived


def take_block(values, index, size, axis):
    return lax.dynamic_slice_in_dim(values, index * size, size, axis=axis)


def body(
    tokens,
    cotangent,
    lengths,
    offsets,
    ln1_gain,
    ln1_bias,
    w_qkv,
    b_qkv,
    w_out,
    ln2_gain,
    ln2_bias,
    w_gate_up,
    w_down,
):
    f32, low = jnp.float32, jnp.bfloat16
    split = ("dp", "ctx")
    n_dp, n_ctx, n_tensor = (lax.axis_size(name) for name in ("dp", "ctx", "tensor"))
    my_dp, me, mine = (lax.axis_index(name) for name in ("dp", "ctx", "tensor"))
    bits = n_tensor.bit_length() - 1
    rows, features = tokens.shape
    quarter = rows // n_tensor
    chunks = 2 if quarter % (2 * TILE) == 0 else 1
    share = quarter // chunks
    block = rows // chunks
    heads_width = w_qkv.shape[2]
    width = heads_width // n_ctx
    lanes = min(128, width)
    groups = width // lanes
    slab = 3 * lanes
    hidden_width = w_down.shape[0]
    stream = rows * n_ctx
    tiles = rows // TILE
    order = [int(format(p, f"0{bits}b")[::-1], 2) for p in range(n_tensor)]
    quarters = [mine ^ item for item in order]
    holders = [(me - s) % n_ctx for s in range(n_ctx)]

    def own_share(values, chunk):
        return lax.dynamic_slice_in_dim(values, mine * quarter + chunk * share, share, axis=0)

    def rotated_chunk(values, chunk):
        return jnp.concatenate(
            [
                lax.dynamic_slice_in_dim(values, q * quarter + chunk * share, share, axis=0)
                for q in quarters
            ],
            axis=0,
        )

    share_at = jnp.stack(
        [quarters[p] * chunks + chunk for chunk in range(chunks) for p in range(n_tensor)]
    ).astype(jnp.int32)

    def unrotate(columns):
        return place_rows(share_at, [piece for pieces in columns for piece in pieces])

    qkv_local = (
        w_qkv.reshape(-1, 3, n_ctx, groups, lanes)
        .transpose(0, 2, 3, 1, 4)
        .reshape(-1, n_ctx, groups * slab)
    )
    depth = qkv_local.shape[0]
    from_ctx = exchange(
        [lax.dynamic_index_in_dim(qkv_local, c, 1, keepdims=False) for c in holders]
    )

    peer_pieces = [[None] * chunks for _ in range(n_ctx)]
    for chunk in range(chunks):
        own = own_share(tokens, chunk)
        for shift in range(1, n_ctx):
            arrived = shift_over(own, "ctx", shift)
            arrived, _ = lax.optimization_barrier((arrived, from_ctx))
            peer_pieces[n_ctx - shift][chunk] = gather_pieces(arrived, bits)

    piece_at = jnp.stack(
        [(my_dp + shift) % n_dp * n_ctx + c for c in holders for shift in range(n_dp)]
    ).astype(jnp.int32)

    def gather_rows(arrived, after=()):
        pieces = []
        for item in arrived:
            pieces.append(item)
            for _ in range(1, n_dp):
                item = shift_over(item, "dp", 1)
                pieces.append(item)
        pieces, _ = lax.optimization_barrier((pieces, after))
        return place_rows(piece_at, pieces)

    def scatter_first(partial, axis):
        bit = lax.axis_size(axis).bit_length() - 2
        half = partial.shape[0] // 2
        side = (lax.axis_index(axis) >> bit) & 1
        arrived = swap_bit(take_block(partial, 1 - side, half, 0).astype(low), axis, bit)
        return take_block(partial, side, half, 0), arrived

    def scatter_rest(halves, axis):
        partial = halves[0].astype(f32) + halves[1].astype(f32)
        for bit in reversed(range(lax.axis_size(axis).bit_length() - 2)):
            half = partial.shape[0] // 2
            side = (lax.axis_index(axis) >> bit) & 1
            arrived = swap_bit(take_block(partial, 1 - side, half, 0).astype(low), axis, bit)
            partial = take_block(partial, side, half, 0) + arrived.astype(f32)
        return partial

    lengths_row = lengths[0]
    offsets_row = offsets[0].reshape(n_ctx, n_tensor, chunks, share // TILE)
    rotated_offsets = jnp.stack(
        [lax.dynamic_index_in_dim(offsets_row, q, 1, keepdims=False) for q in quarters], axis=2
    ).reshape(n_ctx, tiles)
    slots = (
        jnp.concatenate([take_block(rotated_offsets, c, 1, 0) for c in holders], axis=0).reshape(-1)
        // TILE
    )
    place = jnp.arange(stream, dtype=jnp.int32)
    ends = jnp.cumsum(lengths_row)
    begin = jnp.sum(jnp.where(place[None, :] >= ends[:, None], lengths_row[:, None], 0), axis=0)
    half_rot = ROT // 2
    frequency = jnp.exp(jnp.arange(half_rot, dtype=f32) * (-2.0 * math.log(10000.0) / ROT))
    angles = frequency[:, None] * (place - begin).astype(f32)[None, :]
    table = rotary_tables(jnp.concatenate([jnp.cos(angles), jnp.sin(angles)], axis=0), lanes)

    tokens_own = [own_share(tokens, chunk) for chunk in range(chunks)]
    cotangents = [rotated_chunk(cotangent, chunk) for chunk in range(chunks)]
    gate_up_local = w_gate_up.reshape(-1, 2 * hidden_width)
    peers_half = [item[: n_tensor // 2] for items in peer_pieces[1:] for item in items]
    qkv_mine = gather_rows(
        from_ctx, (peers_half, table, slots, tokens_own, cotangents, gate_up_local)
    )
    out_full = lax.all_gather(w_out.T, split, axis=0, tiled=True)
    down_local, _ = lax.optimization_barrier((w_down.T, qkv_mine))
    down_full = lax.all_gather(down_local, split, axis=0, tiled=True)

    gain_one, shift_one = ln1_gain.astype(f32), ln1_bias.astype(f32)
    gain_two, shift_two = ln2_gain.astype(f32), ln2_bias.astype(f32)
    bias_mine = (
        take_block(b_qkv.reshape(3, n_ctx, groups, lanes), me, 1, 1)
        .transpose(1, 2, 0, 3)
        .reshape(1, -1)
        .astype(f32)
    )
    project_args = (gain_one[None], shift_one[None], qkv_mine, bias_mine, groups, stream)
    size = math.gcd(256, rows)
    if share >= size:
        own_blocks = jnp.stack(
            [share_at * (share // size) + i for i in range(share // size)], axis=1
        ).reshape(-1)
        projected = project(own_blocks, [tokens], *project_args, 0, None)
    else:
        own_rows = jnp.concatenate([rotated_chunk(tokens, c) for c in range(chunks)], axis=0)
        projected = project(
            jnp.arange(rows // size, dtype=jnp.int32), [own_rows], *project_args, 0, None
        )
    nothing = jnp.zeros((1,), jnp.int32)
    for s in range(1, n_ctx):
        for chunk in range(chunks):
            first = (s * rows + chunk * block) // share
            projected = project(nothing, peer_pieces[s][chunk], *project_args, first, projected)
    normed1 = projected[0]

    gate_up_local, _ = lax.optimization_barrier((gate_up_local, projected))
    gate_up_full = lax.all_gather(gate_up_local, split, axis=0, tiled=True)

    qkv_all = [qkv_mine] + [None] * (n_ctx - 1)
    for shift in range(1, n_ctx):
        qkv_all[n_ctx - shift] = shift_over(
            lax.optimization_barrier((qkv_mine, projected))[0], "ctx", shift
        )

    kept_attention, arrived_mixed = [], []
    for group in range(groups):
        mixed_parts, *kept = attend(slots, lengths_row, projected[1 + group], table, n_ctx)
        kept_attention.append(kept)
        arrived_mixed.append(exchange(mixed_parts))
    arrived_mixed, _ = lax.optimization_barrier((arrived_mixed, down_full))
    holders_at = jnp.stack(holders).astype(jnp.int32)
    mixed_parts = [arrived_mixed[group][s] for s in range(n_ctx) for group in range(groups)]

    def over_rows(lefts, rights):
        total = None
        for left, right in zip(lefts, rights):
            product = dot_f32(left, right, 0, 0)
            total = product if total is None else total + product
        return total.astype(low)

    tokens_own = [item.astype(f32) for item in tokens_own]
    middle, normed2, hidden, d_gate_up, d_middle, d_middle_low = ([] for _ in range(6))
    attended, arrived_normed2, arrived_middle, d_attended = [], [], [], []
    d_gain_two, d_shift_two = 0.0, 0.0
    out_turned = out_full.T
    d_hidden = [dot_f32(cotangents[chunk], down_full, 1, 0) for chunk in range(chunks)]
    for chunk in range(chunks):
        keep, send, joined = project_out(
            holders_at, mixed_parts, n_ctx, groups, out_turned, chunk, block // 2
        )
        attended.append(joined)
        total = tokens_own[chunk] + sum_over_tensor(keep, send, bits)
        total, _ = lax.optimization_barrier((total, (d_hidden, qkv_all)))
        middle.append(total)
        own = layer_norm(middle[chunk], gain_two, shift_two).astype(low)
        arrived_normed2.append(gather_pieces(own, bits))
    d_normed2_all = []
    for chunk in range(chunks):
        joined, hidden_chunk, grad_chunk, keep, send = feed_forward(
            arrived_normed2[chunk], d_hidden[chunk], gate_up_full
        )
        normed2.append(joined)
        hidden.append(hidden_chunk)
        d_gate_up.append(grad_chunk)
        send, _ = lax.optimization_barrier((send, d_normed2_all))
        total = sum_first(keep, send)
        if chunk + 1 < chunks:
            arrived_normed2[chunk + 1], _ = lax.optimization_barrier(
                (arrived_normed2[chunk + 1], total)
            )
        d_normed2_all.append(sum_further(total, bits))
    ready, _ = lax.optimization_barrier(((normed2[0], d_gate_up[0], hidden), total))
    grad_gate_up = dot_f32(ready[0], ready[1], 0, 0)
    grad_down = over_rows(cotangents, ready[2])
    for chunk in range(chunks):
        d_normed2 = d_normed2_all[chunk]
        if chunk:
            d_normed2, _ = lax.optimization_barrier(
                (d_normed2, (grad_gate_up, grad_down, arrived_middle))
            )
        _, norm_two_back = jax.vjp(layer_norm, middle[chunk], gain_two, shift_two)
        d_middle_norm, d_gain, d_shift = norm_two_back(d_normed2)
        d_gain_two, d_shift_two = d_gain_two + d_gain, d_shift_two + d_shift
        d_middle.append(cotangents[chunk][:share].astype(f32) + d_middle_norm)
        own = d_middle[chunk].astype(low)
        arrived_middle.append(gather_first(own, bits))
    later, _ = lax.optimization_barrier(((normed2[1:], d_gate_up[1:]), own))
    for left, right in zip(*later):
        grad_gate_up = grad_gate_up + dot_f32(left, right, 0, 0)
    grad_gate_up = grad_gate_up.astype(low)
    arrived_middle[-1], _ = lax.optimization_barrier((arrived_middle[-1], grad_gate_up))
    arrived_middle = [gather_rest(item, bits) for item in arrived_middle]
    for chunk in range(chunks):
        joined, sent = project_out_back(holders_at, arrived_middle[chunk], out_full, n_ctx)
        d_middle_low.append(joined)
        d_attended.append(sent)
    arrived_back = [exchange(sent) for sent in d_attended]
    back_parts = [arrived_back[chunk][s] for s in range(n_ctx) for chunk in range(chunks)]

    grad_down = lax.psum_scatter(grad_down, split, scatter_dimension=0, tiled=True)
    grad_gate_up = lax.psum_scatter(grad_gate_up, split, scatter_dimension=0, tiled=True)

    grad_out = scatter_first(over_rows(d_middle_low, attended), "dp")

    later, _ = lax.optimization_barrier((hidden, arrived_back[0]))
    feed_partial = [dot_f32(item, down_full, 1, 1).astype(low) for item in later]
    kept_feed, arrived_feed = [], []
    for chunk in range(chunks):
        partial = feed_partial[chunk]
        kept_feed.append(partial[: block // 2])
        send, _ = lax.optimization_barrier((partial[block // 2 :], d_attended))
        arrived_feed.append(sum_first(kept_feed[chunk], send))
    back_parts, arrived_feed = lax.optimization_barrier((back_parts, arrived_feed))
    output_shares = [
        (middle[chunk] + sum_further(arrived_feed[chunk], bits)).astype(low)
        for chunk in range(chunks)
    ]

    d_parts, partials, bias_sums = [], [], []
    for group in range(groups):
        d_group, sums = attend_back(
            slots, lengths_row, back_parts, group * lanes, *kept_attention[group], table
        )
        sent = [d_group[s * rows : (s + 1) * rows] for s in range(n_ctx)]
        sent, _ = lax.optimization_barrier((sent, d_parts))
        d_parts.append([d_group] + exchange(sent)[1:])
        bias_sums.append(jnp.sum(sums, axis=0))
        partials.append(dot_f32(normed1, d_group, 0, 0).astype(low))
        if group == 0:
            output_shares, _ = lax.optimization_barrier((output_shares, d_group))
            back_parts, output_shares = lax.optimization_barrier((back_parts, output_shares))
    output_pieces = gather_first(jnp.concatenate(output_shares, axis=0), bits)
    output_pieces, _ = lax.optimization_barrier((output_pieces, d_group))
    output_pieces = gather_rest(output_pieces, bits)
    output = place_rows(jnp.stack(quarters).astype(jnp.int32), output_pieces)
    qkv_turned = [item.T for item in qkv_all]
    if groups > 1:
        partials, qkv_turned, _ = lax.optimization_barrier(
            (partials, qkv_turned, (output, grad_out))
        )
    grad_qkv = scatter_first(jnp.concatenate(partials, axis=1), "dp")
    d_projected = [(d_parts[group][s], 0) for s in range(n_ctx) for group in range(groups)]
    d_normed1_all = []
    for chunk in range(chunks):
        keep, send = project_back(d_projected, qkv_turned, groups, chunk, block // 2)
        send, _ = lax.optimization_barrier((send, d_normed1_all))
        total = sum_first(keep, send)
        if chunk + 1 < chunks:
            qkv_turned, _ = lax.optimization_barrier((qkv_turned, total))
        d_normed1_all.append(sum_further(total, bits))
    token_pieces = []
    d_gain_one, d_shift_one = 0.0, 0.0
    for chunk in range(chunks):
        d_normed1 = d_normed1_all[chunk]
        _, norm_one_back = jax.vjp(layer_norm, tokens_own[chunk], gain_one, shift_one)
        d_input, d_gain, d_shift = norm_one_back(d_normed1)
        d_gain_one, d_shift_one = d_gain_one + d_gain, d_shift_one + d_shift
        token_pieces.append(gather_pieces((d_middle[chunk] + d_input).astype(low), bits))
    grad_out, grad_qkv, _ = lax.optimization_barrier(
        (grad_out, grad_qkv, [items[: n_tensor // 2] for items in token_pieces])
    )
    grad_down = grad_down.astype(f32).T
    grad_gate_up = grad_gate_up.astype(f32).reshape(-1, 2, hidden_width)
    token_pieces[-1], _ = lax.optimization_barrier((token_pieces[-1], (grad_down, grad_gate_up)))
    grad_tokens = unrotate(token_pieces)

    grad_out = scatter_rest(scatter_first(scatter_rest(grad_out, "dp"), "ctx"), "ctx")
    grad_qkv = scatter_rest(grad_qkv, "dp").astype(low)
    grad_qkv = exchange([take_block(grad_qkv, c, depth, 0) for c in holders])
    grad_qkv = jnp.stack(grad_qkv)[(me - jnp.arange(n_ctx)) % n_ctx]
    grad_qkv = (
        grad_qkv.reshape(n_ctx, depth, groups, 3, lanes)
        .transpose(1, 3, 0, 2, 4)
        .reshape(depth, 3, heads_width)
        .astype(f32)
    )

    bias_slots = jnp.zeros((n_tensor, n_ctx, groups * slab), f32)
    bias_slots = lax.dynamic_update_slice(
        bias_slots, jnp.concatenate(bias_sums)[None, None], (mine, me, 0)
    )
    small = [d_gain_one, d_shift_one, d_gain_two, d_shift_two, bias_slots.reshape(-1)]
    small = butterfly(jnp.concatenate(small).reshape(-1, 128)).reshape(-1)
    norms = [small[index * features : (index + 1) * features] for index in range(4)]
    bias_sum = take_block(small[4 * features :].reshape(n_tensor, -1), mine, 1, 0)
    bias_sum = (
        bias_sum.reshape(n_ctx, groups, 3, lanes).transpose(2, 0, 1, 3).reshape(3, heads_width)
    )
    return (
        output,
        grad_tokens,
        norms[0],
        norms[1],
        grad_qkv,
        bias_sum,
        grad_out.T,
        norms[2],
        norms[3],
        grad_gate_up,
        grad_down,
    )


def solution(mesh):
    placed = (
        P(("dp", "ctx"), None),
        P(("dp", "ctx"), None),
        P("dp", None),
        P("dp", None),
        P(),
        P(),
        P(("dp", "ctx"), None, "tensor"),
        P(None, "tensor"),
        P("tensor", ("dp", "ctx")),
        P(),
        P(),
        P(("dp", "ctx"), None, "tensor"),
        P("tensor", ("dp", "ctx")),
    )
    return jax.shard_map(
        body,
        mesh=mesh,
        in_specs=placed,
        out_specs=(
            P(("dp", "ctx"), None),
            P(("dp", "ctx"), None),
            P(),
            P(),
            P(("dp", "ctx"), None, "tensor"),
            P(None, "tensor"),
            P("tensor", ("dp", "ctx")),
            P(),
            P(),
            P(("dp", "ctx"), None, "tensor"),
            P("tensor", ("dp", "ctx")),
        ),
        check_vma=False,
    )
```

time: 2320 us -> 1130 us (0.49)
  waiting for transfers between devices: 1170 us -> 354 us
  matrix products: 807 us -> 147 us
  Pallas kernels: 0 us -> 380 us
  other arithmetic: 232 us -> 69.6 us
  starting transfers between devices: 0.79 us -> 68.9 us
  blocking collectives: 39.7 us -> 0 us
  local copies, waits for them, and re-layouts: 44.1 us -> 80.9 us
    dot_general x18 -> x12, matrix products: 807 us -> 147 us  [dot_f32(): lax.dot_general(left, right, (((left_dim,), (right_dim,)), ((), ())), pre...]
    psum x3 -> x0, waiting for transfers between devices: 587 us -> none  [the longest x1 286 us: body(): lax.psum(jnp.dot(hidden, down_full, preferred_element_type=jnp.float32).a...]
    pallas_call x0 -> x19, Pallas kernels: none -> 380 us  [the longest x8 155 us: matmul_call(): pl.pallas_call(kernel, name=name, grid=(2,), in_specs=in_specs, out_specs...]
    ppermute x0 -> x70, waiting for transfers between devices: none -> 328 us  [the longest x53 215 us: swap_bit(): return lax.ppermute(values, axis, [(i, i ^ 1 << bit) for i in range(size)])]
    all_gather x6 -> x3, waiting for transfers between devices: 338 us -> 25.7 us  [the longest x1 25.7 us: body(): gate_up_full = lax.all_gather(gate_up_local, split, axis=0, tiled=True)]
    reduce_scatter x6 -> x2, waiting for transfers between devices: 248 us -> 0.01 us  [the longest x1 0.01 us: body(): lax.psum_scatter(grad_down, split, scatter_dimension=0, tiled=True)]
    reduce_sum x5 -> x3, other arithmetic: 95 us -> 0.15 us  [the longest x1 0.12 us: body(): jnp.sum(jnp.where(place[None, :] >= ends[:, None], lengths_row[:, None],...]
    ppermute x0 -> x70, starting transfers between devices: none -> 68.6 us  [the longest x53 36.3 us: swap_bit(): return lax.ppermute(values, axis, [(i, i ^ 1 << bit) for i in range(size)])]
  transfers between devices with their start and end apart: 15 -> 75, of which waited for: 10 -> 29; matrix products, arithmetic and copies ran while one was open for 32% -> 24% of each run, Pallas kernels for 0% -> 29%
where the time goes in v1:
time: 1130 us; the launch traced here: 1120 us
  Pallas kernels  380 us (34%)
  waiting for transfers between devices  354 us (31%)
  matrix products  147 us (13%)
  local copies, waits for them, and re-layouts  80.9 us (7%)
  other arithmetic  69.6 us (6%)
  starting transfers between devices  68.9 us (6%)
  between operations  15.6 us (1%)
    ppermute x53, waiting for transfers between devices, swap_bit(): return lax.ppermute(values, axis, [(i, i ^ 1 << bit) for i in range(size)])  215 us
    pallas_call x8, Pallas kernels, matmul_call(): pl.pallas_call(kernel, name=name, grid=(2,), in_specs=in_specs, out_specs...  155 us
    dot_general x12, matrix products, dot_f32(): lax.dot_general(left, right, (((left_dim,), (right_dim,)), ((), ())), pre...  147 us
    ppermute x17, waiting for transfers between devices, shift_over(): lax.ppermute(values, axis, [(i, (i - shift) % size) for i in range(size)])  113 us
    pallas_call x2, Pallas kernels, attend_back(): pl.pallas_call(kernel, name='attention_backward', out_shape=[jax.ShapeDty...  88.3 us
    pallas_call x2, Pallas kernels, attend(): pl.pallas_call(kernel, name='attention_forward', out_shape=[jax.ShapeDtyp...  68.3 us
    pallas_call x3, Pallas kernels, project(): pl.pallas_call(functools.partial(project_kernel, count, groups, slab), na...  38.3 us
    unnamed x201, local copies, waits for them, and re-layouts  36.6 us
  transfers between devices with their start and end apart: 75, of which 29 were waited for; matrix products, arithmetic and copies ran while one was open for 24% of the time, Pallas kernels for 29%

profile of v1, /device:TPU:0, one launch (start us, length us, event | category | flops | bytes accessed | tf_op | source)
XLA Modules:
  0.0 1115.5 jit_solution(12929634034957155665)
XLA Ops:
  31.6 17.6 %collective-permute-done.11.refs_0_ = bf16[256,2048]{1,0:T(8,128)(2,1)} collective-permute-done((bf16[256,2048]{1,0:T(8,128)(2,1)S(1)}, bf16[256,2048]{1,0:T(8,128)(2,1)}, u32[]{:S(2)}, u32[]{:S(2)}) %collective-permute-start.11) | collective-permute-done | bytes 1048608 | tf_op jit(solution)/shard_map/ppermute | solution.py:871
  51.2 30.8 %collective-permute-done.refs_0_ = bf16[256,2048]{1,0:T(8,128)(2,1)} collective-permute-done((bf16[256,2048]{1,0:T(8,128)(2,1)S(1)}, bf16[256,2048]{1,0:T(8,128)(2,1)}, u32[]{:S(2)}, u32[]{:S(2)}) %collective-permute-start) | collective-permute-done | bytes 1048608 | tf_op jit(solution)/shard_map/ppermute | solution.py:871
  89.7 7.7 collective-permute-done.6.refs_2_
  113.5 7.5 rotary_tables.1
  121.6 6.0 place_rows.3.refs_3_.refs_6_
  131.2 16.4 %norm_project.3 = (bf16[4096,2048]{1,0:T(8,128)(2,1)}, bf16[4096,384]{1,0:T(8,128)(2,1)}, bf16[4096,384]{1,0:T(8,128)(2,1)}) custom-call(s32[8]{0:T(128)} %stack.132.map_ref.at_ref, bf16[2048,2048]{1,0:T(8,128)(2,1)} %refs_0_.1, f32[1,2048]{1,0:T(1,128)} %bitcast.114, f32[1,2048]{1,0:T(1,128)} %bitcast.118, bf16[2048,768]{1,0:T(8,128)(2,1)} %place_rows.3.refs_3_.refs_6_, ...), custom_call_target="tpu_custom_call" | custom-call | flops 6442450944 | bytes 19922944 | tf_op jit(solution)/shard_map/norm_project/pallas_call | solution.py:493
  147.6 10.8 norm_project.4
  159.9 11.0 norm_project.5
  171.1 34.3 %attention_forward.3 = (bf16[2048,128]{1,0:T(8,128)(2,1)}, bf16[2048,128]{1,0:T(8,128)(2,1)}, bf16[4096,384]{1,0:T(8,128)(2,1)}, bf16[4096,128]{1,0:T(8,128)(2,1)}, f32[8,4096]{1,0:T(8,128)}) custom-call(s32[32]{0:T(128)} %and_select_fusion.1.slot_ref, s32[6]{0:T(128)} %bitcast.123, bf16[4096,384]{1,0:T(8,128)(2,1)} %get-tuple-element.152.refs_0_, ...), custom_call_target="tpu_custom_call" | custom-call | flops 11453245440 | bytes 10485760 | tf_op jit(solution)/shard_map/attention_forward/pallas_call | solution.py:221
  206.9 34.1 %attention_forward.2 = (bf16[2048,128]{1,0:T(8,128)(2,1)}, bf16[2048,128]{1,0:T(8,128)(2,1)}, bf16[4096,384]{1,0:T(8,128)(2,1)}, bf16[4096,128]{1,0:T(8,128)(2,1)}, f32[8,4096]{1,0:T(8,128)}) custom-call(s32[32]{0:T(128)} %and_select_fusion.1.slot_ref, s32[6]{0:T(128)} %bitcast.124, bf16[4096,384]{1,0:T(8,128)(2,1)} %get-tuple-element.149.refs_0_, ...), custom_call_target="tpu_custom_call" | custom-call | flops 11453245440 | bytes 10485760 | tf_op jit(solution)/shard_map/attention_forward/pallas_call | solution.py:221
  242.2 7.1 constant_dynamic-slice_fusion.10
  260.9 8.3 project_out.2
  269.3 18.2 %project_out.3 = (bf16[512,2048]{1,0:T(8,128)(2,1)}, bf16[512,2048]{1,0:T(8,128)(2,1)}, bf16[1024,512]{1,0:T(8,128)(2,1)}) custom-call(s32[2]{0:T(128)} %pad_add_fusion.3.holder_ref, bf16[2048,128]{1,0:T(8,128)(2,1)} %get-tuple-element.156.refs_0_, bf16[2048,128]{1,0:T(8,128)(2,1)} %get-tuple-element.157.refs_1_, ...), custom_call_target="tpu_custom_call" | custom-call | flops 2147483648 | bytes 9437192 | tf_op jit(solution)/shard_map/project_out/pallas_call | solution.py:566
  287.6 13.3 %fusion.31.refs_4_ = f32[1024,1408]{1,0:T(8,128)} fusion(bf16[2048,1408]{0,1:T(8,128)(2,1)} %all-gather.4.cloned.1.call-done, bf16[256,2048]{1,0:T(8,128)(2,1)} %get-tuple-element.327, bf16[256,2048]{1,0:T(8,128)(2,1)} %get-tuple-element.328, bf16[256,2048]{1,0:T(8,128)(2,1)} %get-tuple-element.322, bf16[256,2048]{1,0:T(8,128)(2,1)S(1)} %copy-done.25), kind=kOutput, calls=%fused_computation.175 | convolution fusion | flops 5922357248 | bytes 15728640 | tf_op jit(solution)/shard_map/dot_general | solution.py:27
  306.0 13.8 %fusion.33.refs_4_ = f32[1024,1408]{1,0:T(8,128)} fusion(bf16[2048,1408]{0,1:T(8,128)(2,1)} %all-gather.4.cloned.1.call-done, bf16[256,2048]{1,0:T(8,128)(2,1)S(1)} %copy-done.49, bf16[256,2048]{1,0:T(8,128)(2,1)S(1)} %copy-done.51, bf16[256,2048]{1,0:T(8,128)(2,1)S(1)} %copy-done.53, bf16[256,2048]{1,0:T(8,128)(2,1)S(1)} %copy-done.28), kind=kOutput, calls=%fused_computation.177 | convolution fusion | flops 5922357248 | bytes 15728640 | tf_op jit(solution)/shard_map/dot_general | solution.py:27
  319.9 8.0 collective-permute-done.18
  327.9 22.0 %collective-permute-done.29 = bf16[256,2048]{1,0:T(8,128)(2,1)} collective-permute-done((bf16[256,2048]{1,0:T(8,128)(2,1)S(1)}, bf16[256,2048]{1,0:T(8,128)(2,1)}, u32[]{:S(2)}, u32[]{:S(2)}) %collective-permute-start.29) | collective-permute-done | bytes 1048608 | tf_op jit(solution)/shard_map/ppermute | solution.py:829
  354.2 12.8 %collective-permute-done.19 = bf16[2048,768]{0,1:T(8,128)(2,1)} collective-permute-done((bf16[2048,768]{0,1:T(8,128)(2,1)}, bf16[2048,768]{0,1:T(8,128)(2,1)}, u32[]{:S(2)}, u32[]{:S(2)}) %collective-permute-start.19) | collective-permute-done | bytes 3145760 | tf_op jit(solution)/shard_map/ppermute | solution.py:871
  373.9 22.5 %collective-permute-done.20.refs_1_ = bf16[256,2048]{1,0:T(8,128)(2,1)S(1)} collective-permute-done((bf16[256,2048]{1,0:T(8,128)(2,1)S(1)}, bf16[256,2048]{1,0:T(8,128)(2,1)S(1)}, u32[]{:S(2)}, u32[]{:S(2)}) %collective-permute-start.20) | collective-permute-done | bytes 1048608 | tf_op jit(solution)/shard_map/ppermute | solution.py:829
  399.2 25.7 %all-gather.8.cloned.1.call-done.refs_5_ = bf16[2048,2816]{1,0:T(8,128)(2,1)} async-done(((bf16[256,2816]{1,0:T(8,128)(2,1)}), bf16[2048,2816]{1,0:T(8,128)(2,1)}) %all-gather.8.cloned.1.call-update) | async-done | bytes 11534352 | tf_op jit(solution)/shard_map/all_gather | solution.py:1046
  424.9 42.6 %feed_forward.2 = (bf16[1024,2048]{1,0:T(8,128)(2,1)}, bf16[1024,1408]{1,0:T(8,128)(2,1)}, bf16[1024,2816]{1,0:T(8,128)(2,1)}, bf16[512,2048]{1,0:T(8,128)(2,1)}, bf16[512,2048]{1,0:T(8,128)(2,1)}) custom-call(bf16[256,2048]{1,0:T(8,128)(2,1)} %copy-done.59, bf16[256,2048]{1,0:T(8,128)(2,1)} %copy-done.85, bf16[256,2048]{1,0:T(8,128)(2,1)} %copy-done.87, ...), custom_call_target="tpu_custom_call" | custom-call | flops 23622320128 | bytes 38535168 | tf_op jit(solution)/shard_map/feed_forward/pallas_call | solution.py:566
  469.4 23.9 %collective-permute-done.30.refs_1_ = bf16[256,2048]{1,0:T(8,128)(2,1)S(1)} collective-permute-done((bf16[256,2048]{1,0:T(8,128)(2,1)S(1)}, bf16[256,2048]{1,0:T(8,128)(2,1)S(1)}, u32[]{:S(2)}, u32[]{:S(2)}) %collective-permute-start.30) | collective-permute-done | bytes 1048608 | tf_op jit(solution)/shard_map/ppermute | solution.py:829
  502.6 42.8 %feed_forward.3 = (bf16[1024,2048]{1,0:T(8,128)(2,1)}, bf16[1024,1408]{1,0:T(8,128)(2,1)}, bf16[1024,2816]{1,0:T(8,128)(2,1)}, bf16[512,2048]{1,0:T(8,128)(2,1)}, bf16[512,2048]{1,0:T(8,128)(2,1)}) custom-call(bf16[256,2048]{1,0:T(8,128)(2,1)} %copy-done.58, bf16[256,2048]{1,0:T(8,128)(2,1)} %copy-done.82, bf16[256,2048]{1,0:T(8,128)(2,1)} %copy-done.83, ...), custom_call_target="tpu_custom_call" | custom-call | flops 23622320128 | bytes 38535168 | tf_op jit(solution)/shard_map/feed_forward/pallas_call | solution.py:566
  555.9 21.1 %collective-permute-done.25.refs_1_ = bf16[256,2048]{1,0:T(8,128)(2,1)} collective-permute-done((bf16[256,2048]{1,0:T(8,128)(2,1)}, bf16[256,2048]{1,0:T(8,128)(2,1)}, u32[]{:S(2)}, u32[]{:S(2)}) %collective-permute-start.25) | collective-permute-done | bytes 1048608 | tf_op jit(solution)/shard_map/ppermute | solution.py:829
  584.1 9.6 fusion.32
  593.7 7.5 project_out_back.2
  601.8 12.3 %add_convert_fusion.1 = bf16[2048,1408]{1,0:T(8,128)(2,1)} fusion(f32[2048,1408]{1,0:T(8,128)} %fusion.32, bf16[1024,1408]{1,0:T(8,128)(2,1)} %get-tuple-element.199, bf16[256,2048]{1,0:T(8,128)(2,1)S(1)} %copy-done.48, bf16[256,2048]{1,0:T(8,128)(2,1)} %get-tuple-element.328, bf16[256,2048]{1,0:T(8,128)(2,1)S(1)} %copy-done.47, ...), kind=kOutput, calls=%fused_computation.2 | convolution fusion | flops 5928124416 | bytes 24379392 | tf_op jit(solution)/shard_map/dot_general | solution.py:27
  614.1 20.3 %fusion.38 = f32[2048,2816]{1,0:T(8,128)} fusion(bf16[1024,2048]{1,0:T(8,128)(2,1)} %get-tuple-element.183, bf16[1024,2816]{1,0:T(8,128)(2,1)} %get-tuple-element.184), kind=kOutput, calls=%fused_computation.182 | convolution fusion | flops 11811160064 | bytes 33030144 | tf_op jit(solution)/shard_map/dot_general | solution.py:27
  642.2 22.2 %add_convert_fusion = bf16[2048,2816]{1,0:T(8,128)(2,1)} fusion(f32[2048,2816]{1,0:T(8,128)} %fusion.38, bf16[1024,2048]{1,0:T(8,128)(2,1)} %get-tuple-element.190, bf16[1024,2816]{1,0:T(8,128)(2,1)} %get-tuple-element.191), kind=kOutput, calls=%fused_computation.1 | convolution fusion | flops 11822694400 | bytes 44564480 | tf_op jit(solution)/shard_map/dot_general | solution.py:27
  666.9 9.6 convolution_convert_fusion
  680.2 7.4 project_out_back.3
  687.5 10.1 convolution_convert_fusion.1
  703.9 5.0 fusion.39
  723.1 44.1 %attention_backward.2 = (bf16[4096,384]{1,0:T(8,128)(2,1)}, f32[8,384]{1,0:T(8,128)}) custom-call(s32[32]{0:T(128)} %and_select_fusion.1.slot_ref, s32[6]{0:T(128)} %bitcast.125, bf16[1024,256]{1,0:T(8,128)(2,1)} %get-tuple-element.215.refs_0_, bf16[1024,256]{1,0:T(8,128)(2,1)} %get-tuple-element.216.refs_1_, bf16[1024,256]{1,0:T(8,128)(2,1)} %copy-done.89, ...), custom_call_target="tpu_custom_call" | custom-call | flops 28633112576 | bytes 10485760 | tf_op jit(solution)/shard_map/attention_backward/pallas_call | solution.py:383
  776.8 44.2 %attention_backward.3 = (bf16[4096,384]{1,0:T(8,128)(2,1)}, f32[8,384]{1,0:T(8,128)}) custom-call(s32[32]{0:T(128)} %and_select_fusion.1.slot_ref, s32[6]{0:T(128)} %bitcast.126, bf16[1024,256]{1,0:T(8,128)(2,1)} %get-tuple-element.215.refs_0_, bf16[1024,256]{1,0:T(8,128)(2,1)} %get-tuple-element.216.refs_1_, bf16[1024,256]{1,0:T(8,128)(2,1)} %copy-done.89, ...), custom_call_target="tpu_custom_call" | custom-call | flops 28633112576 | bytes 10485760 | tf_op jit(solution)/shard_map/attention_backward/pallas_call | solution.py:383
  823.6 14.6 %convolution_convert_fusion.3 = bf16[2048,384]{1,0:T(8,128)(2,1)} fusion(bf16[4096,2048]{1,0:T(8,128)(2,1)} %get-tuple-element.162, bf16[4096,384]{1,0:T(8,128)(2,1)} %get-tuple-element.210.refs_0_), kind=kOutput, calls=%fused_computation.36 | convolution fusion | flops 6443237376 | bytes 21495808 | tf_op jit(solution)/shard_map/dot_general | solution.py:27
  839.2 13.8 %convolution_convert_fusion.2 = bf16[2048,384]{1,0:T(8,128)(2,1)} fusion(bf16[4096,2048]{1,0:T(8,128)(2,1)} %get-tuple-element.162, bf16[4096,384]{1,0:T(8,128)(2,1)S(1)} %copy-done.60), kind=kOutput, calls=%fused_computation.35 | convolution fusion | flops 6443237376 | bytes 21495808 | tf_op jit(solution)/shard_map/dot_general | solution.py:27
  854.4 7.8 place_rows.4
  862.2 27.9 %collective-permute-done.48.refs_3_ = bf16[2048,384]{1,0:T(8,128)(2,1)} collective-permute-done((bf16[2048,384]{1,0:T(8,128)(2,1)S(1)}, bf16[2048,384]{1,0:T(8,128)(2,1)}, u32[]{:S(2)}, u32[]{:S(2)}) %collective-permute-start.48) | collective-permute-done | bytes 1572896 | tf_op jit(solution)/shard_map/ppermute | solution.py:871
  890.1 14.1 %project_back.2 = (bf16[512,2048]{1,0:T(8,128)(2,1)}, bf16[512,2048]{1,0:T(8,128)(2,1)}) custom-call(bf16[4096,384]{1,0:T(8,128)(2,1)} %get-tuple-element.210.refs_0_, bf16[4096,384]{1,0:T(8,128)(2,1)} %get-tuple-element.222.refs_1_, bf16[2048,384]{1,0:T(8,128)(2,1)} %collective-permute-done.47.refs_2_, bf16[2048,384]{1,0:T(8,128)(2,1)} %collective-permute-done.48.refs_3_, ...), custom_call_target="tpu_custom_call" | custom-call | flops 6442450944 | bytes 19922944 | tf_op jit(solution)/shard_map/project_back/pallas_call | solution.py:566
  913.0 13.9 %project_back.3 = (bf16[512,2048]{1,0:T(8,128)(2,1)}, bf16[512,2048]{1,0:T(8,128)(2,1)}) custom-call(bf16[4096,384]{1,0:T(8,128)(2,1)} %get-tuple-element.210.refs_0_, bf16[4096,384]{1,0:T(8,128)(2,1)} %get-tuple-element.222.refs_1_, bf16[2048,384]{1,0:T(8,128)(2,1)} %collective-permute-done.47.refs_2_, bf16[2048,384]{1,0:T(8,128)(2,1)} %collective-permute-done.48.refs_3_, ...), custom_call_target="tpu_custom_call" | custom-call | flops 6442450944 | bytes 19922944 | tf_op jit(solution)/shard_map/project_back/pallas_call | solution.py:566
  926.9 9.6 collective-permute-done.51
  957.2 18.6 %collective-permute-done.56 = bf16[256,2048]{1,0:T(8,128)(2,1)} collective-permute-done((bf16[256,2048]{1,0:T(8,128)(2,1)}, bf16[256,2048]{1,0:T(8,128)(2,1)}, u32[]{:S(2)}, u32[]{:S(2)}) %collective-permute-start.56) | collective-permute-done | bytes 1048608 | tf_op jit(solution)/shard_map/ppermute | solution.py:829
  986.6 44.8 %collective-permute-done.60 = f32[112,128]{1,0:T(8,128)S(1)} collective-permute-done((f32[112,128]{1,0:T(8,128)S(1)}, f32[112,128]{1,0:T(8,128)S(1)}, u32[]{:S(2)}, u32[]{:S(2)}) %collective-permute-start.60) | collective-permute-done | bytes 57376 | tf_op jit(solution)/shard_map/ppermute | solution.py:829
  1065.3 12.2 %collective-permute-done.66 = bf16[512,768]{1,0:T(8,128)(2,1)} collective-permute-done((bf16[512,768]{1,0:T(8,128)(2,1)}, bf16[512,768]{1,0:T(8,128)(2,1)}, u32[]{:S(2)}, u32[]{:S(2)}) %collective-permute-start.66) | collective-permute-done | bytes 786464 | tf_op jit(solution)/shard_map/ppermute | solution.py:829
  1079.6 5.8 collective-permute-done.69
  1087.1 6.0 collective-permute-done.67
  1100.2 8.7 place_rows.5
  (471 shorter events, 251.4 us)
Async XLA Ops:
  7.2 246.5 %all-gather.6.cloned.1.call-start = ((), (), s32[]{:S(2)}) async-start(), calls=%async_computation.3 | async-start | bytes 2359296 | tf_op jit(solution)/shard_map/all_gather | solution.py:1014
  9.0 251.9 %all-gather.4.cloned.1.call-start = ((), (), s32[]{:S(2)}) async-start(), calls=%async_computation.2 | async-start | bytes 6488064 | tf_op jit(solution)/shard_map/all_gather | solution.py:1016
  16.3 32.9 %collective-permute-start.11 = (bf16[256,2048]{1,0:T(8,128)(2,1)S(1)}, bf16[256,2048]{1,0:T(8,128)(2,1)}, u32[]{:S(2)}, u32[]{:S(2)}) collective-permute-start(bf16[256,2048]{1,0:T(8,128)(2,1)S(1)} %get-tuple-element.330), channel_id=1, source_target_pairs={{0,4},{4,0},{1,5},{5,1},{2,6},{6,2},{3,7},{7,3},{8,12},{12,8},{9,1... | collective-permute-start | bytes 3145736 | tf_op jit(solution)/shard_map/ppermute | solution.py:871
  16.3 65.7 %collective-permute-start = (bf16[256,2048]{1,0:T(8,128)(2,1)S(1)}, bf16[256,2048]{1,0:T(8,128)(2,1)}, u32[]{:S(2)}, u32[]{:S(2)}) collective-permute-start(bf16[256,2048]{1,0:T(8,128)(2,1)S(1)} %get-tuple-element.312), channel_id=1, source_target_pairs={{0,4},{4,0},{1,5},{5,1},{2,6},{6,2},{3,7},{7,3},{8,12},{12,8},{9,1... | collective-permute-start | bytes 3145736 | tf_op jit(solution)/shard_map/ppermute | solution.py:871
  18.5 65.4 %collective-permute-start.5 = (bf16[256,768]{1,0:T(8,128)(2,1)S(1)}, bf16[256,768]{1,0:T(8,128)(2,1)}, u32[]{:S(2)}, u32[]{:S(2)}) collective-permute-start(bf16[256,768]{1,0:T(8,128)(2,1)S(1)} %bitcast.107), channel_id=1, source_target_pairs={{0,24},{8,0},{16,8},{24,16},{1,25},{9,1},{17,9},{25,17},{2,26},{10... | collective-permute-start | bytes 1179656 | tf_op jit(solution)/shard_map/ppermute | solution.py:871
  25.3 62.3 %collective-permute-start.8 = (bf16[256,768]{1,0:T(8,128)(2,1)}, bf16[256,768]{1,0:T(8,128)(2,1)}, u32[]{:S(2)}, u32[]{:S(2)}) collective-permute-start(bf16[256,768]{1,0:T(8,128)(2,1)} %collective-permute-done.1.refs_4_), channel_id=1, source_target_pairs={{0,24},{8,0},{16,8},{24,16},{1,25},{9,1},{17,9},{25,17},{2,26},{10... | collective-permute-start | bytes 1179656 | tf_op jit(solution)/shard_map/ppermute | solution.py:871
  49.2 72.3 %collective-permute-start.12 = (bf16[256,2048]{1,0:T(8,128)(2,1)}, bf16[256,2048]{1,0:T(8,128)(2,1)}, u32[]{:S(2)}, u32[]{:S(2)}) collective-permute-start(bf16[256,2048]{1,0:T(8,128)(2,1)} %collective-permute-done.11.refs_0_), channel_id=1, source_target_pairs={{0,2},{1,3},{2,0},{3,1},{4,6},{5,7},{6,4},{7,5},{8,10},{9,11},{10,... | collective-permute-start | bytes 3145736 | tf_op jit(solution)/shard_map/ppermute | solution.py:829
  82.1 39.5 %collective-permute-start.2 = (bf16[256,2048]{1,0:T(8,128)(2,1)}, bf16[256,2048]{1,0:T(8,128)(2,1)S(1)}, u32[]{:S(2)}, u32[]{:S(2)}) collective-permute-start(bf16[256,2048]{1,0:T(8,128)(2,1)} %collective-permute-done.refs_0_), channel_id=1, source_target_pairs={{0,2},{1,3},{2,0},{3,1},{4,6},{5,7},{6,4},{7,5},{8,10},{9,11},{10,... | collective-permute-start | bytes 3145736 | tf_op jit(solution)/shard_map/ppermute | solution.py:829
  127.6 297.3 %all-gather.8.cloned.1.call-start = ((), (), s32[]{:S(2)}) async-start(), calls=%async_computation.4 | async-start | bytes 12976128 | tf_op jit(solution)/shard_map/all_gather | solution.py:1046
  128.3 30.2 %collective-permute-start.3 = (bf16[256,2048]{1,0:T(8,128)(2,1)}, bf16[256,2048]{1,0:T(8,128)(2,1)S(1)}, u32[]{:S(2)}, u32[]{:S(2)}) collective-permute-start(bf16[256,2048]{1,0:T(8,128)(2,1)} %collective-permute-done.refs_0_), channel_id=1, source_target_pairs={{0,1},{1,0},{2,3},{3,2},{4,5},{5,4},{6,7},{7,6},{8,9},{9,8},{10,11... | collective-permute-start | bytes 3145736 | tf_op jit(solution)/shard_map/ppermute | solution.py:829
  128.4 30.1 %collective-permute-start.4 = (bf16[256,2048]{1,0:T(8,128)(2,1)S(1)}, bf16[256,2048]{1,0:T(8,128)(2,1)S(1)}, u32[]{:S(2)}, u32[]{:S(2)}) collective-permute-start(bf16[256,2048]{1,0:T(8,128)(2,1)S(1)} %collective-permute-done.2.refs_1_), channel_id=1, source_target_pairs={{0,1},{1,0},{2,3},{3,2},{4,5},{5,4},{6,7},{7,6},{8,9},{9,8},{10,11... | collective-permute-start | bytes 3145736 | tf_op jit(solution)/shard_map/ppermute | solution.py:829
  170.9 882.4 %reduce-scatter.3.cloned.1.call-start = ((), (), s32[]{:S(2)}) async-start(), calls=%async_computation.5 | async-start | bytes 6488064 | tf_op jit(solution)/shard_map/reduce_scatter | solution.py:1129
  205.4 52.2 %collective-permute-start.16 = (bf16[2048,128]{1,0:T(8,128)(2,1)}, bf16[2048,128]{1,0:T(8,128)(2,1)}, u32[]{:S(2)}, u32[]{:S(2)}) collective-permute-start(bf16[2048,128]{1,0:T(8,128)(2,1)} %get-tuple-element.154), channel_id=1, source_target_pairs={{0,4},{4,0},{1,5},{5,1},{2,6},{6,2},{3,7},{7,3},{8,12},{12,8},{9,1... | collective-permute-start | bytes 1572872 | tf_op jit(solution)/shard_map/ppermute | solution.py:871
  252.2 114.9 %collective-permute-start.19 = (bf16[2048,768]{0,1:T(8,128)(2,1)}, bf16[2048,768]{0,1:T(8,128)(2,1)}, u32[]{:S(2)}, u32[]{:S(2)}) collective-permute-start(bf16[2048,768]{0,1:T(8,128)(2,1)} %copy.77), channel_id=1, source_target_pairs={{0,4},{4,0},{1,5},{5,1},{2,6},{6,2},{3,7},{7,3},{8,12},{12,8},{9,1... | collective-permute-start | bytes 9437192 | tf_op jit(solution)/shard_map/ppermute | solution.py:871
  269.2 31.6 %collective-permute-start.17 = (bf16[512,2048]{1,0:T(8,128)(2,1)}, bf16[512,2048]{1,0:T(8,128)(2,1)S(1)}, u32[]{:S(2)}, u32[]{:S(2)}) collective-permute-start(bf16[512,2048]{1,0:T(8,128)(2,1)} %get-tuple-element.161), channel_id=1, source_target_pairs={{0,1},{1,0},{2,3},{3,2},{4,5},{5,4},{6,7},{7,6},{8,9},{9,8},{10,11... | collective-permute-start | bytes 6291464 | tf_op jit(solution)/shard_map/ppermute | solution.py:829
  301.8 26.0 %collective-permute-start.18 = (bf16[256,2048]{1,0:T(8,128)(2,1)S(1)}, bf16[256,2048]{1,0:T(8,128)(2,1)S(1)}, u32[]{:S(2)}, u32[]{:S(2)}) collective-permute-start(bf16[256,2048]{1,0:T(8,128)(2,1)S(1)} %slice.201), channel_id=1, source_target_pairs={{0,2},{1,3},{2,0},{3,1},{4,6},{5,7},{6,4},{7,5},{8,10},{9,11},{10,... | collective-permute-start | bytes 3145736 | tf_op jit(solution)/shard_map/ppermute | solution.py:829
  304.5 45.4 %collective-permute-start.29 = (bf16[256,2048]{1,0:T(8,128)(2,1)S(1)}, bf16[256,2048]{1,0:T(8,128)(2,1)}, u32[]{:S(2)}, u32[]{:S(2)}) collective-permute-start(bf16[256,2048]{1,0:T(8,128)(2,1)S(1)} %slice.199), channel_id=1, source_target_pairs={{0,2},{1,3},{2,0},{3,1},{4,6},{5,7},{6,4},{7,5},{8,10},{9,11},{10,... | collective-permute-start | bytes 3145736 | tf_op jit(solution)/shard_map/ppermute | solution.py:829
  467.6 25.7 %collective-permute-start.23 = (bf16[512,2048]{1,0:T(8,128)(2,1)}, bf16[512,2048]{1,0:T(8,128)(2,1)S(1)}, u32[]{:S(2)}, u32[]{:S(2)}) collective-permute-start(bf16[512,2048]{1,0:T(8,128)(2,1)} %get-tuple-element.167), channel_id=1, source_target_pairs={{0,1},{1,0},{2,3},{3,2},{4,5},{5,4},{6,7},{7,6},{8,9},{9,8},{10,11... | collective-permute-start | bytes 6291464 | tf_op jit(solution)/shard_map/ppermute | solution.py:829
  467.7 25.6 %collective-permute-start.30 = (bf16[256,2048]{1,0:T(8,128)(2,1)S(1)}, bf16[256,2048]{1,0:T(8,128)(2,1)S(1)}, u32[]{:S(2)}, u32[]{:S(2)}) collective-permute-start(bf16[256,2048]{1,0:T(8,128)(2,1)S(1)} %get-tuple-element.172.refs_0_), channel_id=1, source_target_pairs={{0,2},{1,3},{2,0},{3,1},{4,6},{5,7},{6,4},{7,5},{8,10},{9,11},{10,... | collective-permute-start | bytes 3145736 | tf_op jit(solution)/shard_map/ppermute | solution.py:829
  469.2 30.0 %collective-permute-start.31 = (bf16[256,2048]{1,0:T(8,128)(2,1)S(1)}, bf16[256,2048]{1,0:T(8,128)(2,1)S(1)}, u32[]{:S(2)}, u32[]{:S(2)}) collective-permute-start(bf16[256,2048]{1,0:T(8,128)(2,1)S(1)} %get-tuple-element.172.refs_0_), channel_id=1, source_target_pairs={{0,1},{1,0},{2,3},{3,2},{4,5},{5,4},{6,7},{7,6},{8,9},{9,8},{10,11... | collective-permute-start | bytes 3145736 | tf_op jit(solution)/shard_map/ppermute | solution.py:829
  501.2 44.3 %collective-permute-start.24 = (bf16[256,2048]{1,0:T(8,128)(2,1)}, bf16[256,2048]{1,0:T(8,128)(2,1)S(1)}, u32[]{:S(2)}, u32[]{:S(2)}) collective-permute-start(bf16[256,2048]{1,0:T(8,128)(2,1)} %slice.200), channel_id=1, source_target_pairs={{0,2},{1,3},{2,0},{3,1},{4,6},{5,7},{6,4},{7,5},{8,10},{9,11},{10,... | collective-permute-start | bytes 3145736 | tf_op jit(solution)/shard_map/ppermute | solution.py:829
  548.6 28.4 %collective-permute-start.33 = (bf16[512,2048]{1,0:T(8,128)(2,1)}, bf16[512,2048]{1,0:T(8,128)(2,1)}, u32[]{:S(2)}, u32[]{:S(2)}) collective-permute-start(bf16[512,2048]{1,0:T(8,128)(2,1)} %get-tuple-element.178), channel_id=1, source_target_pairs={{0,1},{1,0},{2,3},{3,2},{4,5},{5,4},{6,7},{7,6},{8,9},{9,8},{10,11... | collective-permute-start | bytes 6291464 | tf_op jit(solution)/shard_map/ppermute | solution.py:829
  551.1 25.9 %collective-permute-start.25 = (bf16[256,2048]{1,0:T(8,128)(2,1)}, bf16[256,2048]{1,0:T(8,128)(2,1)}, u32[]{:S(2)}, u32[]{:S(2)}) collective-permute-start(bf16[256,2048]{1,0:T(8,128)(2,1)} %fusion.16.refs_0_), channel_id=1, source_target_pairs={{0,2},{1,3},{2,0},{3,1},{4,6},{5,7},{6,4},{7,5},{8,10},{9,11},{10,... | collective-permute-start | bytes 3145736 | tf_op jit(solution)/shard_map/ppermute | solution.py:829
  555.5 38.3 %collective-permute-start.26 = (bf16[256,2048]{1,0:T(8,128)(2,1)}, bf16[256,2048]{1,0:T(8,128)(2,1)}, u32[]{:S(2)}, u32[]{:S(2)}) collective-permute-start(bf16[256,2048]{1,0:T(8,128)(2,1)} %fusion.16.refs_0_), channel_id=1, source_target_pairs={{0,1},{1,0},{2,3},{3,2},{4,5},{5,4},{6,7},{7,6},{8,9},{9,8},{10,11... | collective-permute-start | bytes 3145736 | tf_op jit(solution)/shard_map/ppermute | solution.py:829
  583.3 51.9 %collective-permute-start.34 = (bf16[256,2048]{1,0:T(8,128)(2,1)}, bf16[256,2048]{1,0:T(8,128)(2,1)}, u32[]{:S(2)}, u32[]{:S(2)}) collective-permute-start(bf16[256,2048]{1,0:T(8,128)(2,1)} %slice.198), channel_id=1, source_target_pairs={{0,2},{1,3},{2,0},{3,1},{4,6},{5,7},{6,4},{7,5},{8,10},{9,11},{10,... | collective-permute-start | bytes 3145736 | tf_op jit(solution)/shard_map/ppermute | solution.py:829
  601.2 33.2 %collective-permute-start.38 = (bf16[1024,256]{1,0:T(8,128)(2,1)}, bf16[1024,256]{1,0:T(8,128)(2,1)S(1)}, u32[]{:S(2)}, u32[]{:S(2)}) collective-permute-start(bf16[1024,256]{1,0:T(8,128)(2,1)} %get-tuple-element.195), channel_id=1, source_target_pairs={{0,4},{4,0},{1,5},{5,1},{2,6},{6,2},{3,7},{7,3},{8,12},{12,8},{9,1... | collective-permute-start | bytes 1572872 | tf_op jit(solution)/shard_map/ppermute | solution.py:871
  614.1 481.7 %reduce-scatter.5.cloned.1.call-start = ((), (), s32[]{:S(2)}) async-start(), calls=%async_computation.6 | async-start | bytes 12976128 | tf_op jit(solution)/shard_map/reduce_scatter | solution.py:1130
  640.9 25.5 %collective-permute-start.35 = (bf16[256,2048]{1,0:T(8,128)(2,1)}, bf16[256,2048]{1,0:T(8,128)(2,1)S(1)}, u32[]{:S(2)}, u32[]{:S(2)}) collective-permute-start(bf16[256,2048]{1,0:T(8,128)(2,1)} %fusion.17.refs_0_), channel_id=1, source_target_pairs={{0,2},{1,3},{2,0},{3,1},{4,6},{5,7},{6,4},{7,5},{8,10},{9,11},{10,... | collective-permute-start | bytes 3145736 | tf_op jit(solution)/shard_map/ppermute | solution.py:829
  687.5 26.9 %collective-permute-start.41 = (bf16[512,2048]{1,0:T(8,128)(2,1)}, bf16[512,2048]{1,0:T(8,128)(2,1)}, u32[]{:S(2)}, u32[]{:S(2)}) collective-permute-start(bf16[512,2048]{1,0:T(8,128)(2,1)} %slice.148), channel_id=1, source_target_pairs={{0,1},{1,0},{2,3},{3,2},{4,5},{5,4},{6,7},{7,6},{8,9},{9,8},{10,11... | collective-permute-start | bytes 6291464 | tf_op jit(solution)/shard_map/ppermute | solution.py:829
  712.9 149.3 %collective-permute-start.49 = (bf16[1024,512]{1,0:T(8,128)(2,1)}, bf16[1024,512]{1,0:T(8,128)(2,1)}, u32[]{:S(2)}, u32[]{:S(2)}) collective-permute-start(bf16[1024,512]{1,0:T(8,128)(2,1)} %get-tuple-element.333), channel_id=1, source_target_pairs={{0,16},{8,24},{16,0},{24,8},{1,17},{9,25},{17,1},{25,9},{2,18},{10... | collective-permute-start | bytes 3145736 | tf_op jit(solution)/shard_map/ppermute | solution.py:829
  720.8 49.6 %collective-permute-start.43 = (bf16[256,2048]{1,0:T(8,128)(2,1)}, bf16[256,2048]{1,0:T(8,128)(2,1)}, u32[]{:S(2)}, u32[]{:S(2)}) collective-permute-start(bf16[256,2048]{1,0:T(8,128)(2,1)} %slice.196), channel_id=1, source_target_pairs={{0,2},{1,3},{2,0},{3,1},{4,6},{5,7},{6,4},{7,5},{8,10},{9,11},{10,... | collective-permute-start | bytes 3145736 | tf_op jit(solution)/shard_map/ppermute | solution.py:829
  722.0 51.1 %collective-permute-start.42 = (bf16[256,2048]{1,0:T(8,128)(2,1)S(1)}, bf16[256,2048]{1,0:T(8,128)(2,1)}, u32[]{:S(2)}, u32[]{:S(2)}) collective-permute-start(bf16[256,2048]{1,0:T(8,128)(2,1)S(1)} %slice.197), channel_id=1, source_target_pairs={{0,2},{1,3},{2,0},{3,1},{4,6},{5,7},{6,4},{7,5},{8,10},{9,11},{10,... | collective-permute-start | bytes 3145736 | tf_op jit(solution)/shard_map/ppermute | solution.py:829
  769.8 68.5 %collective-permute-start.47 = (bf16[2048,384]{1,0:T(8,128)(2,1)}, bf16[2048,384]{1,0:T(8,128)(2,1)}, u32[]{:S(2)}, u32[]{:S(2)}) collective-permute-start(bf16[2048,384]{1,0:T(8,128)(2,1)} %slice.120), channel_id=1, source_target_pairs={{0,4},{4,0},{1,5},{5,1},{2,6},{6,2},{3,7},{7,3},{8,12},{12,8},{9,1... | collective-permute-start | bytes 4718600 | tf_op jit(solution)/shard_map/ppermute | solution.py:871
  775.7 47.4 %collective-permute-start.44 = (bf16[512,2048]{1,0:T(8,128)(2,1)S(1)}, bf16[512,2048]{1,0:T(8,128)(2,1)}, u32[]{:S(2)}, u32[]{:S(2)}) collective-permute-start(bf16[512,2048]{1,0:T(8,128)(2,1)S(1)} %constant_dynamic-update-slice_fusion.refs_0_), channel_id=1, source_target_pairs={{0,2},{1,3},{2,0},{3,1},{4,6},{5,7},{6,4},{7,5},{8,10},{9,11},{10,... | collective-permute-start | bytes 6291464 | tf_op jit(solution)/shard_map/ppermute | solution.py:829
  823.1 29.9 %collective-permute-start.45 = (bf16[512,2048]{1,0:T(8,128)(2,1)S(1)}, bf16[512,2048]{1,0:T(8,128)(2,1)S(1)}, u32[]{:S(2)}, u32[]{:S(2)}) collective-permute-start(bf16[512,2048]{1,0:T(8,128)(2,1)S(1)} %constant_dynamic-update-slice_fusion.refs_0_), channel_id=1, source_target_pairs={{0,1},{1,0},{2,3},{3,2},{4,5},{5,4},{6,7},{7,6},{8,9},{9,8},{10,11... | collective-permute-start | bytes 6291464 | tf_op jit(solution)/shard_map/ppermute | solution.py:829
  823.1 31.2 %collective-permute-start.46 = (bf16[512,2048]{1,0:T(8,128)(2,1)}, bf16[512,2048]{1,0:T(8,128)(2,1)}, u32[]{:S(2)}, u32[]{:S(2)}) collective-permute-start(bf16[512,2048]{1,0:T(8,128)(2,1)} %collective-permute-done.44.refs_1_), channel_id=1, source_target_pairs={{0,1},{1,0},{2,3},{3,2},{4,5},{5,4},{6,7},{7,6},{8,9},{9,8},{10,11... | collective-permute-start | bytes 6291464 | tf_op jit(solution)/shard_map/ppermute | solution.py:829
  838.4 51.7 %collective-permute-start.48 = (bf16[2048,384]{1,0:T(8,128)(2,1)S(1)}, bf16[2048,384]{1,0:T(8,128)(2,1)}, u32[]{:S(2)}, u32[]{:S(2)}) collective-permute-start(bf16[2048,384]{1,0:T(8,128)(2,1)S(1)} %slice.121), channel_id=1, source_target_pairs={{0,4},{4,0},{1,5},{5,1},{2,6},{6,2},{3,7},{7,3},{8,12},{12,8},{9,1... | collective-permute-start | bytes 4718600 | tf_op jit(solution)/shard_map/ppermute | solution.py:871
  911.2 25.4 %collective-permute-start.51 = (bf16[256,2048]{1,0:T(8,128)(2,1)S(1)}, bf16[256,2048]{1,0:T(8,128)(2,1)}, u32[]{:S(2)}, u32[]{:S(2)}) collective-permute-start(bf16[256,2048]{1,0:T(8,128)(2,1)S(1)} %slice.195), channel_id=1, source_target_pairs={{0,2},{1,3},{2,0},{3,1},{4,6},{5,7},{6,4},{7,5},{8,10},{9,11},{10,... | collective-permute-start | bytes 3145736 | tf_op jit(solution)/shard_map/ppermute | solution.py:829
  950.2 25.5 %collective-permute-start.56 = (bf16[256,2048]{1,0:T(8,128)(2,1)}, bf16[256,2048]{1,0:T(8,128)(2,1)}, u32[]{:S(2)}, u32[]{:S(2)}) collective-permute-start(bf16[256,2048]{1,0:T(8,128)(2,1)} %slice.194), channel_id=1, source_target_pairs={{0,2},{1,3},{2,0},{3,1},{4,6},{5,7},{6,4},{7,5},{8,10},{9,11},{10,... | collective-permute-start | bytes 3145736 | tf_op jit(solution)/shard_map/ppermute | solution.py:829
  955.6 89.4 %collective-permute-start.65 = (bf16[1024,768]{1,0:T(8,128)(2,1)}, bf16[1024,768]{1,0:T(8,128)(2,1)}, u32[]{:S(2)}, u32[]{:S(2)}) collective-permute-start(bf16[1024,768]{1,0:T(8,128)(2,1)} %get-tuple-element.331), channel_id=1, source_target_pairs={{0,16},{8,24},{16,0},{24,8},{1,17},{9,25},{17,1},{25,9},{2,18},{10... | collective-permute-start | bytes 4718600 | tf_op jit(solution)/shard_map/ppermute | solution.py:829
  983.4 61.6 %collective-permute-start.57 = (bf16[256,2048]{1,0:T(8,128)(2,1)S(1)}, bf16[256,2048]{1,0:T(8,128)(2,1)S(1)}, u32[]{:S(2)}, u32[]{:S(2)}) collective-permute-start(bf16[256,2048]{1,0:T(8,128)(2,1)S(1)} %add_convert_fusion.3.refs_4_), channel_id=1, source_target_pairs={{0,2},{1,3},{2,0},{3,1},{4,6},{5,7},{6,4},{7,5},{8,10},{9,11},{10,... | collective-permute-start | bytes 3145736 | tf_op jit(solution)/shard_map/ppermute | solution.py:829
  984.5 60.6 %collective-permute-start.52 = (bf16[256,2048]{1,0:T(8,128)(2,1)}, bf16[256,2048]{1,0:T(8,128)(2,1)}, u32[]{:S(2)}, u32[]{:S(2)}) collective-permute-start(bf16[256,2048]{1,0:T(8,128)(2,1)} %get-tuple-element.349.refs_0_), channel_id=1, source_target_pairs={{0,2},{1,3},{2,0},{3,1},{4,6},{5,7},{6,4},{7,5},{8,10},{9,11},{10,... | collective-permute-start | bytes 3145736 | tf_op jit(solution)/shard_map/ppermute | solution.py:829
  985.6 45.9 %collective-permute-start.60 = (f32[112,128]{1,0:T(8,128)S(1)}, f32[112,128]{1,0:T(8,128)S(1)}, u32[]{:S(2)}, u32[]{:S(2)}) collective-permute-start(f32[112,128]{1,0:T(8,128)S(1)} %bitcast.117), channel_id=1, source_target_pairs={{0,2},{1,3},{2,0},{3,1},{4,6},{5,7},{6,4},{7,5},{8,10},{9,11},{10,... | collective-permute-start | bytes 172040 | tf_op jit(solution)/shard_map/ppermute | solution.py:829
  1051.3 26.1 %collective-permute-start.66 = (bf16[512,768]{1,0:T(8,128)(2,1)}, bf16[512,768]{1,0:T(8,128)(2,1)}, u32[]{:S(2)}, u32[]{:S(2)}) collective-permute-start(bf16[512,768]{1,0:T(8,128)(2,1)} %dynamic-slice_convert_fusion), channel_id=1, source_target_pairs={{0,8},{8,0},{16,24},{24,16},{1,9},{9,1},{17,25},{25,17},{2,10},{10... | collective-permute-start | bytes 2359304 | tf_op jit(solution)/shard_map/ppermute | solution.py:829
  1058.5 41.6 %collective-permute-start.58 = (bf16[256,2048]{1,0:T(8,128)(2,1)}, bf16[256,2048]{1,0:T(8,128)(2,1)}, u32[]{:S(2)}, u32[]{:S(2)}) collective-permute-start(bf16[256,2048]{1,0:T(8,128)(2,1)} %copy-done.36), channel_id=1, source_target_pairs={{0,1},{1,0},{2,3},{3,2},{4,5},{5,4},{6,7},{7,6},{8,9},{9,8},{10,11... | collective-permute-start | bytes 3145736 | tf_op jit(solution)/shard_map/ppermute | solution.py:829
  1058.5 41.6 %collective-permute-start.53 = (bf16[256,2048]{1,0:T(8,128)(2,1)}, bf16[256,2048]{1,0:T(8,128)(2,1)}, u32[]{:S(2)}, u32[]{:S(2)}) collective-permute-start(bf16[256,2048]{1,0:T(8,128)(2,1)} %get-tuple-element.349.refs_0_), channel_id=1, source_target_pairs={{0,1},{1,0},{2,3},{3,2},{4,5},{5,4},{6,7},{7,6},{8,9},{9,8},{10,11... | collective-permute-start | bytes 3145736 | tf_op jit(solution)/shard_map/ppermute | solution.py:829
  1059.7 40.4 %collective-permute-start.59 = (bf16[256,2048]{1,0:T(8,128)(2,1)}, bf16[256,2048]{1,0:T(8,128)(2,1)}, u32[]{:S(2)}, u32[]{:S(2)}) collective-permute-start(bf16[256,2048]{1,0:T(8,128)(2,1)} %copy-done.55), channel_id=1, source_target_pairs={{0,1},{1,0},{2,3},{3,2},{4,5},{5,4},{6,7},{7,6},{8,9},{9,8},{10,11... | collective-permute-start | bytes 3145736 | tf_op jit(solution)/shard_map/ppermute | solution.py:829
  1063.7 36.4 %collective-permute-start.54 = (bf16[256,2048]{1,0:T(8,128)(2,1)}, bf16[256,2048]{1,0:T(8,128)(2,1)}, u32[]{:S(2)}, u32[]{:S(2)}) collective-permute-start(bf16[256,2048]{1,0:T(8,128)(2,1)} %collective-permute-done.52.refs_1_), channel_id=1, source_target_pairs={{0,1},{1,0},{2,3},{3,2},{4,5},{5,4},{6,7},{7,6},{8,9},{9,8},{10,11... | collective-permute-start | bytes 3145736 | tf_op jit(solution)/shard_map/ppermute | solution.py:829
  (123 other events, 1874.2 us)
Sparse Core Ops, SparseCore 0:
  10.1 76.3 all-gather.5
  127.8 93.4 all-gather.3
  224.0 200.8 all-gather.7
  614.2 134.7 reduce-scatter.2
  752.5 252.6 reduce-scatter.4

commit v2 on v1

--- a/solution.py
+++ b/solution.py
@@ -540,6 +540,28 @@
     )(at, *pieces)
 
 
+def pick_kernel(at_ref, source, out):
+    out[...] = source[...]
+
+
+def pick_rows(at, values, size):
+    rows, features = values.shape
+    return pl.pallas_call(
+        pick_kernel,
+        name="pick_rows",
+        grid_spec=pltpu.PrefetchScalarGridSpec(
+            num_scalar_prefetch=1,
+            grid=(rows // size,),
+            in_specs=[pl.BlockSpec((size, features), lambda step, order: (order[step], 0))],
+            out_specs=pl.BlockSpec((size, features), lambda step, order: (step, 0)),
+        ),
+        out_shape=jax.ShapeDtypeStruct((rows, features), values.dtype),
+        cost_estimate=pl.CostEstimate(
+            flops=0, bytes_accessed=rows * features * 4, transcendentals=0
+        ),
+    )(at, values)
+
+
 def once(shape):
     return pl.BlockSpec(shape, lambda *_: (0, 0), pipeline_mode=pl.Buffered(1))
 
@@ -560,7 +582,9 @@
         keep_ref[:, cols] = values
 
 
-def matmul_call(kernel, name, half, in_specs, out_specs, out_shape, scratch, flops, args):
+def matmul_call(
+    kernel, name, half, in_specs, out_specs, out_shape, scratch, flops, args, aliases=None
+):
     bytes_moved = sum(a.size * a.dtype.itemsize for a in args)
     bytes_moved += sum(math.prod(o.shape) * o.dtype.itemsize for o in out_shape)
     return pl.pallas_call(
@@ -571,6 +595,7 @@
         out_specs=out_specs,
         out_shape=out_shape,
         scratch_shapes=scratch,
+        input_output_aliases=aliases or {},
         compiler_params=pltpu.CompilerParams(vmem_limit_bytes=VMEM_LIMIT),
         cost_estimate=pl.CostEstimate(flops=flops, bytes_accessed=bytes_moved, transcendentals=0),
     )(*args)
@@ -634,11 +659,12 @@
                 out_ref[index * size : (index + 1) * size, :] = piece[...]
 
 
-def feed_kernel(count, hidden, *refs):
+def feed_kernel(count, hidden, joined, *refs):
     pieces = refs[:count]
     d_hidden_ref, weight_ref = refs[count : count + 2]
-    normed_ref, hidden_ref, grad_ref, keep_ref, send_ref = refs[count + 2 : count + 7]
-    weight, weight_sems, piece_sems = refs[count + 7 :]
+    refs = refs[count + 2 + joined :]
+    normed_ref, hidden_ref, grad_ref, keep_ref, send_ref = refs[:5]
+    weight, weight_sems, piece_sems = refs[5:]
     step = pl.program_id(0)
     size = pieces[0].shape[0]
     half = count // 2
@@ -706,29 +732,33 @@
         store_half(step, keep_ref, send_ref, cols, result)
 
 
-def feed_forward(pieces, d_hidden, weight):
+def feed_forward(pieces, d_hidden, weight, rows, chunk, joined):
     share, features = pieces[0].shape
     half = share * len(pieces) // 2
     hidden = d_hidden.shape[1]
-    placed = lambda step: (1 - step, 0)
+    joined_at = lambda step: (chunk * 2 + 1 - step, 0)
     anywhere = pl.BlockSpec(memory_space=pl.ANY)
     copies = 2 * len(column_tiles(hidden))
+    joined = [] if joined is None else joined
+    args = (*pieces, d_hidden, weight, *joined)
     return matmul_call(
-        functools.partial(feed_kernel, len(pieces), hidden),
+        functools.partial(feed_kernel, len(pieces), hidden, len(joined)),
         "feed_forward",
         half,
-        [anywhere] * len(pieces) + [pl.BlockSpec((half, hidden), placed), anywhere],
+        [anywhere] * len(pieces)
+        + [pl.BlockSpec((half, hidden), joined_at), anywhere]
+        + [anywhere] * len(joined),
         [
-            pl.BlockSpec((half, features), placed),
-            pl.BlockSpec((half, hidden), placed),
-            pl.BlockSpec((half, 2 * hidden), placed),
+            pl.BlockSpec((half, features), joined_at),
+            pl.BlockSpec((half, hidden), joined_at),
+            pl.BlockSpec((half, 2 * hidden), joined_at),
             pl.BlockSpec((half, features), lambda step: (0, 0)),
             pl.BlockSpec((half, features), lambda step: (0, 0)),
         ],
         [
-            low_shape(2 * half, features),
-            low_shape(2 * half, hidden),
-            low_shape(2 * half, 2 * hidden),
+            low_shape(rows, features),
+            low_shape(rows, hidden),
+            low_shape(rows, 2 * hidden),
             low_shape(half, features),
             low_shape(half, features),
         ],
@@ -738,7 +768,8 @@
             pltpu.SemaphoreType.DMA((len(pieces) // 2,)),
         ],
         16 * half * features * hidden,
-        (*pieces, d_hidden, weight),
+        args,
+        {len(pieces) + 2 + index: index for index in range(len(joined))},
     )
 
 
@@ -801,14 +832,14 @@
         store_half(step, keep_ref, send_ref, cols, total)
 
 
-def project_back(parts, weights, groups, chunk, half):
+def project_back(parts, weights, groups, half):
     wide, features = weights[0].shape
     count = len(weights)
     slab = wide // groups
 
     def spec(first):
         return pl.BlockSpec(
-            (half, slab), lambda step: (first // half + chunk * 2 + 1 - step, 0)
+            (half, slab), lambda step: (first // half + 1 - step, 0)
         )
 
     return matmul_call(
@@ -860,8 +891,8 @@
 
 
 def butterfly(values):
-    for axis in ("tensor", "ctx", "dp"):
-        for bit in reversed(range(lax.axis_size(axis).bit_length() - 1)):
+    for axis in ("ctx", "dp", "tensor"):
+        for bit in range(lax.axis_size(axis).bit_length() - 1):
             values = values + swap_bit(values, axis, bit)
     return values
 
@@ -949,43 +980,41 @@
         [lax.dynamic_index_in_dim(qkv_local, c, 1, keepdims=False) for c in holders]
     )
 
-    peer_pieces = [[None] * chunks for _ in range(n_ctx)]
-    for chunk in range(chunks):
-        own = own_share(tokens, chunk)
-        for shift in range(1, n_ctx):
-            arrived = shift_over(own, "ctx", shift)
-            arrived, _ = lax.optimization_barrier((arrived, from_ctx))
-            peer_pieces[n_ctx - shift][chunk] = gather_pieces(arrived, bits)
-
     piece_at = jnp.stack(
         [(my_dp + shift) % n_dp * n_ctx + c for c in holders for shift in range(n_dp)]
     ).astype(jnp.int32)
 
-    def gather_rows(arrived, after=()):
+    def ring_rows(arrived):
         pieces = []
         for item in arrived:
             pieces.append(item)
             for _ in range(1, n_dp):
                 item = shift_over(item, "dp", 1)
                 pieces.append(item)
-        pieces, _ = lax.optimization_barrier((pieces, after))
-        return place_rows(piece_at, pieces)
-
-    def scatter_first(partial, axis):
-        bit = lax.axis_size(axis).bit_length() - 2
-        half = partial.shape[0] // 2
-        side = (lax.axis_index(axis) >> bit) & 1
-        arrived = swap_bit(take_block(partial, 1 - side, half, 0).astype(low), axis, bit)
-        return take_block(partial, side, half, 0), arrived
-
-    def scatter_rest(halves, axis):
-        partial = halves[0].astype(f32) + halves[1].astype(f32)
-        for bit in reversed(range(lax.axis_size(axis).bit_length() - 2)):
-            half = partial.shape[0] // 2
-            side = (lax.axis_index(axis) >> bit) & 1
-            arrived = swap_bit(take_block(partial, 1 - side, half, 0).astype(low), axis, bit)
-            partial = take_block(partial, side, half, 0) + arrived.astype(f32)
-        return partial
+        return pieces
+
+    qkv_pieces = ring_rows(from_ctx)
+
+    peer_pieces = [[None] * chunks for _ in range(n_ctx)]
+    for chunk in range(chunks):
+        own = own_share(tokens, chunk)
+        for shift in range(1, n_ctx):
+            arrived = shift_over(own, "ctx", shift)
+            steps = [qkv_pieces[s * n_dp + min(chunk + 1, n_dp - 1)] for s in range(n_ctx)]
+            arrived, _ = lax.optimization_barrier((arrived, steps))
+            peer_pieces[n_ctx - shift][chunk] = gather_pieces(arrived, bits)
+
+    def scatter_ring(partial, axis, after=()):
+        size, index = lax.axis_size(axis), lax.axis_index(axis)
+        deep = partial.shape[0] // size
+        totals = [take_block(partial, (index + 1) % size, deep, 0)]
+        for step in range(1, size):
+            arrived = shift_over(totals[-1].astype(low), axis, 1)
+            if step <= len(after):
+                arrived, _ = lax.optimization_barrier((arrived, after[step - 1]))
+            own = take_block(partial, (index + 1 + step) % size, deep, 0)
+            totals.append(own.astype(f32) + arrived.astype(f32))
+        return totals
 
     lengths_row = lengths[0]
     offsets_row = offsets[0].reshape(n_ctx, n_tensor, chunks, share // TILE)
@@ -1005,15 +1034,18 @@
     table = rotary_tables(jnp.concatenate([jnp.cos(angles), jnp.sin(angles)], axis=0), lanes)
 
     tokens_own = [own_share(tokens, chunk) for chunk in range(chunks)]
-    cotangents = [rotated_chunk(cotangent, chunk) for chunk in range(chunks)]
+    cotangent_rot = pick_rows(share_at, cotangent, share)
     gate_up_local = w_gate_up.reshape(-1, 2 * hidden_width)
     peers_half = [item[: n_tensor // 2] for items in peer_pieces[1:] for item in items]
-    qkv_mine = gather_rows(
-        from_ctx, (peers_half, table, slots, tokens_own, cotangents, gate_up_local)
-    )
+    qkv_pieces, _ = lax.optimization_barrier(
+        (qkv_pieces, (peers_half, table, slots, tokens_own, cotangent_rot, gate_up_local))
+    )
+    qkv_mine = place_rows(piece_at, qkv_pieces)
     out_full = lax.all_gather(w_out.T, split, axis=0, tiled=True)
-    down_local, _ = lax.optimization_barrier((w_down.T, qkv_mine))
+    down_local, _ = lax.optimization_barrier((w_down.T, from_ctx))
     down_full = lax.all_gather(down_local, split, axis=0, tiled=True)
+    gate_up_local, _ = lax.optimization_barrier((gate_up_local, qkv_mine))
+    gate_up_full = lax.all_gather(gate_up_local, split, axis=0, tiled=True)
 
     gain_one, shift_one = ln1_gain.astype(f32), ln1_bias.astype(f32)
     gain_two, shift_two = ln2_gain.astype(f32), ln2_bias.astype(f32)
@@ -1042,14 +1074,15 @@
             projected = project(nothing, peer_pieces[s][chunk], *project_args, first, projected)
     normed1 = projected[0]
 
-    gate_up_local, _ = lax.optimization_barrier((gate_up_local, projected))
-    gate_up_full = lax.all_gather(gate_up_local, split, axis=0, tiled=True)
-
-    qkv_all = [qkv_mine] + [None] * (n_ctx - 1)
+    qkv_all = [[qkv_mine]] + [None] * (n_ctx - 1)
+    arrived, _ = lax.optimization_barrier((qkv_mine, projected))
     for shift in range(1, n_ctx):
-        qkv_all[n_ctx - shift] = shift_over(
-            lax.optimization_barrier((qkv_mine, projected))[0], "ctx", shift
-        )
+        items = []
+        for half in range(2):
+            sent = take_block(qkv_mine, half, features // 2, 0)
+            arrived = shift_over(lax.optimization_barrier((sent, arrived))[0], "ctx", shift)
+            items.append(arrived)
+        qkv_all[n_ctx - shift] = items
 
     kept_attention, arrived_mixed = [], []
     for group in range(groups):
@@ -1068,56 +1101,67 @@
         return total.astype(low)
 
     tokens_own = [item.astype(f32) for item in tokens_own]
-    middle, normed2, hidden, d_gate_up, d_middle, d_middle_low = ([] for _ in range(6))
+    middle, d_middle, d_middle_low = [], [], []
     attended, arrived_normed2, arrived_middle, d_attended = [], [], [], []
     d_gain_two, d_shift_two = 0.0, 0.0
     out_turned = out_full.T
-    d_hidden = [dot_f32(cotangents[chunk], down_full, 1, 0) for chunk in range(chunks)]
+    d_hidden = dot_f32(cotangent_rot, down_full, 1, 0)
     for chunk in range(chunks):
         keep, send, joined = project_out(
             holders_at, mixed_parts, n_ctx, groups, out_turned, chunk, block // 2
         )
         attended.append(joined)
         total = tokens_own[chunk] + sum_over_tensor(keep, send, bits)
-        total, _ = lax.optimization_barrier((total, (d_hidden, qkv_all)))
+        total, _ = lax.optimization_barrier((total, d_hidden))
         middle.append(total)
         own = layer_norm(middle[chunk], gain_two, shift_two).astype(low)
-        arrived_normed2.append(gather_pieces(own, bits))
+        arrived_normed2.append(gather_first(own, bits))
+    first_normed2 = arrived_normed2
+    arrived_normed2 = [gather_rest(item, bits) for item in arrived_normed2]
+    joined = None
     d_normed2_all = []
     for chunk in range(chunks):
-        joined, hidden_chunk, grad_chunk, keep, send = feed_forward(
-            arrived_normed2[chunk], d_hidden[chunk], gate_up_full
+        *joined, keep, send = feed_forward(
+            arrived_normed2[chunk], d_hidden, gate_up_full, rows, chunk, joined
         )
-        normed2.append(joined)
-        hidden.append(hidden_chunk)
-        d_gate_up.append(grad_chunk)
-        send, _ = lax.optimization_barrier((send, d_normed2_all))
+        send, _ = lax.optimization_barrier(
+            (
+                send,
+                (
+                    d_normed2_all,
+                    first_normed2[chunk + 1 : chunk + 2],
+                    [items[chunk] for items in qkv_all[1:]],
+                ),
+            )
+        )
         total = sum_first(keep, send)
         if chunk + 1 < chunks:
             arrived_normed2[chunk + 1], _ = lax.optimization_barrier(
                 (arrived_normed2[chunk + 1], total)
             )
         d_normed2_all.append(sum_further(total, bits))
-    ready, _ = lax.optimization_barrier(((normed2[0], d_gate_up[0], hidden), total))
-    grad_gate_up = dot_f32(ready[0], ready[1], 0, 0)
-    grad_down = over_rows(cotangents, ready[2])
+    normed2, hidden, d_gate_up = joined
+    ready, _ = lax.optimization_barrier((hidden, total))
+    grad_down = dot_f32(cotangent_rot, ready, 0, 0).astype(low)
     for chunk in range(chunks):
         d_normed2 = d_normed2_all[chunk]
         if chunk:
             d_normed2, _ = lax.optimization_barrier(
-                (d_normed2, (grad_gate_up, grad_down, arrived_middle))
+                (d_normed2, grad_down)
             )
         _, norm_two_back = jax.vjp(layer_norm, middle[chunk], gain_two, shift_two)
         d_middle_norm, d_gain, d_shift = norm_two_back(d_normed2)
         d_gain_two, d_shift_two = d_gain_two + d_gain, d_shift_two + d_shift
-        d_middle.append(cotangents[chunk][:share].astype(f32) + d_middle_norm)
+        upstream = cotangent_rot[chunk * block : chunk * block + share].astype(f32)
+        d_middle.append(upstream + d_middle_norm)
         own = d_middle[chunk].astype(low)
         arrived_middle.append(gather_first(own, bits))
-    later, _ = lax.optimization_barrier(((normed2[1:], d_gate_up[1:]), own))
-    for left, right in zip(*later):
-        grad_gate_up = grad_gate_up + dot_f32(left, right, 0, 0)
-    grad_gate_up = grad_gate_up.astype(low)
-    arrived_middle[-1], _ = lax.optimization_barrier((arrived_middle[-1], grad_gate_up))
+    ready, _ = lax.optimization_barrier(((hidden, d_gate_up), own))
+    grad_gate_up = dot_f32(normed2, ready[1], 0, 0).astype(low)
+    feed_partial = dot_f32(ready[0], down_full, 1, 1).astype(low)
+    arrived_middle[-1], _ = lax.optimization_barrier(
+        (arrived_middle[-1], (grad_gate_up, feed_partial, qkv_all))
+    )
     arrived_middle = [gather_rest(item, bits) for item in arrived_middle]
     for chunk in range(chunks):
         joined, sent = project_out_back(holders_at, arrived_middle[chunk], out_full, n_ctx)
@@ -1129,72 +1173,91 @@
     grad_down = lax.psum_scatter(grad_down, split, scatter_dimension=0, tiled=True)
     grad_gate_up = lax.psum_scatter(grad_gate_up, split, scatter_dimension=0, tiled=True)
 
-    grad_out = scatter_first(over_rows(d_middle_low, attended), "dp")
-
-    later, _ = lax.optimization_barrier((hidden, arrived_back[0]))
-    feed_partial = [dot_f32(item, down_full, 1, 1).astype(low) for item in later]
+    late, _ = lax.optimization_barrier((d_middle_low, arrived_back[0]))
+    grad_out = over_rows(late, attended)
+
     kept_feed, arrived_feed = [], []
     for chunk in range(chunks):
-        partial = feed_partial[chunk]
+        partial = feed_partial[chunk * block : (chunk + 1) * block]
         kept_feed.append(partial[: block // 2])
         send, _ = lax.optimization_barrier((partial[block // 2 :], d_attended))
         arrived_feed.append(sum_first(kept_feed[chunk], send))
-    back_parts, arrived_feed = lax.optimization_barrier((back_parts, arrived_feed))
+    back_parts, arrived_feed, _ = lax.optimization_barrier((back_parts, arrived_feed, grad_out))
     output_shares = [
         (middle[chunk] + sum_further(arrived_feed[chunk], bits)).astype(low)
         for chunk in range(chunks)
     ]
 
-    d_parts, partials, bias_sums = [], [], []
+    d_parts, d_groups, bias_sums, output_pieces = [], [], [], []
     for group in range(groups):
         d_group, sums = attend_back(
             slots, lengths_row, back_parts, group * lanes, *kept_attention[group], table
         )
-        sent = [d_group[s * rows : (s + 1) * rows] for s in range(n_ctx)]
-        sent, _ = lax.optimization_barrier((sent, d_parts))
-        d_parts.append([d_group] + exchange(sent)[1:])
+        parts = 1 if group + 1 < groups else chunks
+        arrived = []
+        for part in range(parts):
+            size = rows // parts
+            sent = [
+                d_group[s * rows + part * size : s * rows + (part + 1) * size]
+                for s in range(n_ctx)
+            ]
+            sent, _ = lax.optimization_barrier((sent, (d_parts, arrived, output_pieces)))
+            arrived.append(exchange(sent)[1:])
+        d_parts.append(arrived)
         bias_sums.append(jnp.sum(sums, axis=0))
-        partials.append(dot_f32(normed1, d_group, 0, 0).astype(low))
+        d_groups.append(d_group)
         if group == 0:
             output_shares, _ = lax.optimization_barrier((output_shares, d_group))
             back_parts, output_shares = lax.optimization_barrier((back_parts, output_shares))
-    output_pieces = gather_first(jnp.concatenate(output_shares, axis=0), bits)
+            output_pieces = gather_first(jnp.concatenate(output_shares, axis=0), bits)
     output_pieces, _ = lax.optimization_barrier((output_pieces, d_group))
     output_pieces = gather_rest(output_pieces, bits)
-    output = place_rows(jnp.stack(quarters).astype(jnp.int32), output_pieces)
-    qkv_turned = [item.T for item in qkv_all]
+    partials = []
+    for group in range(groups):
+        after = d_group if group == 0 else d_parts[-1][0]
+        late, _ = lax.optimization_barrier((normed1, after))
+        partials.append(dot_f32(late, d_groups[group], 0, 0).astype(low))
+    qkv_turned = [jnp.concatenate([item.T for item in items], axis=1) for items in qkv_all]
     if groups > 1:
-        partials, qkv_turned, _ = lax.optimization_barrier(
-            (partials, qkv_turned, (output, grad_out))
-        )
-    grad_qkv = scatter_first(jnp.concatenate(partials, axis=1), "dp")
-    d_projected = [(d_parts[group][s], 0) for s in range(n_ctx) for group in range(groups)]
+        partials, qkv_turned, _ = lax.optimization_barrier((partials, qkv_turned, d_parts[-1]))
     d_normed1_all = []
     for chunk in range(chunks):
-        keep, send = project_back(d_projected, qkv_turned, groups, chunk, block // 2)
+        parts = [(d_group, chunk * block) for d_group in d_groups]
+        for s in range(1, n_ctx):
+            for arrived in d_parts:
+                if len(arrived) == 1:
+                    parts.append((arrived[0][s - 1], chunk * block))
+                else:
+                    parts.append((arrived[chunk][s - 1], 0))
+        keep, send = project_back(parts, qkv_turned, groups, block // 2)
         send, _ = lax.optimization_barrier((send, d_normed1_all))
         total = sum_first(keep, send)
         if chunk + 1 < chunks:
             qkv_turned, _ = lax.optimization_barrier((qkv_turned, total))
         d_normed1_all.append(sum_further(total, bits))
-    token_pieces = []
+    output_pieces, _ = lax.optimization_barrier((output_pieces, total))
+    output = place_rows(jnp.stack(quarters).astype(jnp.int32), output_pieces)
+    d_normed1_all[-1], _ = lax.optimization_barrier(
+        (d_normed1_all[-1], output)
+    )
+    token_pieces, token_shares = [], []
     d_gain_one, d_shift_one = 0.0, 0.0
     for chunk in range(chunks):
         d_normed1 = d_normed1_all[chunk]
         _, norm_one_back = jax.vjp(layer_norm, tokens_own[chunk], gain_one, shift_one)
         d_input, d_gain, d_shift = norm_one_back(d_normed1)
         d_gain_one, d_shift_one = d_gain_one + d_gain, d_shift_one + d_shift
-        token_pieces.append(gather_pieces((d_middle[chunk] + d_input).astype(low), bits))
-    grad_out, grad_qkv, _ = lax.optimization_barrier(
-        (grad_out, grad_qkv, [items[: n_tensor // 2] for items in token_pieces])
-    )
+        token_shares.append((d_middle[chunk] + d_input).astype(low))
+        token_pieces.append(gather_pieces(token_shares[chunk], bits))
+    after = (d_normed1_all[0], d_normed1_all[-1], token_shares)
+    grad_out = scatter_ring(grad_out, "dp", after)[-1]
+    grad_qkv = scatter_ring(jnp.concatenate(partials, axis=1), "dp", after)[-1].astype(low)
     grad_down = grad_down.astype(f32).T
     grad_gate_up = grad_gate_up.astype(f32).reshape(-1, 2, hidden_width)
     token_pieces[-1], _ = lax.optimization_barrier((token_pieces[-1], (grad_down, grad_gate_up)))
     grad_tokens = unrotate(token_pieces)
 
-    grad_out = scatter_rest(scatter_first(scatter_rest(grad_out, "dp"), "ctx"), "ctx")
-    grad_qkv = scatter_rest(grad_qkv, "dp").astype(low)
+    grad_out = scatter_ring(grad_out, "ctx")[-1]
     grad_qkv = exchange([take_block(grad_qkv, c, depth, 0) for c in holders])
     grad_qkv = jnp.stack(grad_qkv)[(me - jnp.arange(n_ctx)) % n_ctx]
     grad_qkv = (
@@ -1209,7 +1272,13 @@
         bias_slots, jnp.concatenate(bias_sums)[None, None], (mine, me, 0)
     )
     small = [d_gain_one, d_shift_one, d_gain_two, d_shift_two, bias_slots.reshape(-1)]
-    small = butterfly(jnp.concatenate(small).reshape(-1, 128)).reshape(-1)
+    small, _ = lax.optimization_barrier(
+        (
+            jnp.concatenate(small).reshape(-1, 128),
+            [items[: n_tensor // 2] for items in token_pieces],
+        )
+    )
+    small = butterfly(small).reshape(-1)
     norms = [small[index * features : (index + 1) * features] for index in range(4)]
     bias_sum = take_block(small[4 * features :].reshape(n_tensor, -1), mine, 1, 0)
     bias_sum = (

time: 1130 us -> 992 us (0.88)
  waiting for transfers between devices: 354 us -> 251 us
  matrix products: 147 us -> 115 us
  local copies, waits for them, and re-layouts: 80.9 us -> 65.8 us
  other arithmetic: 69.6 us -> 82.7 us
    ppermute x53 -> x48, waiting for transfers between devices: 215 us -> 123 us  [swap_bit(): return lax.ppermute(values, axis, [(i, i ^ 1 << bit) for i in range(size)])]
    dot_general x12 -> x8, matrix products: 147 us -> 115 us  [dot_f32(): lax.dot_general(left, right, (((left_dim,), (right_dim,)), ((), ())), pre...]
    ppermute x17 -> x26, starting transfers between devices: 32.3 us -> 49.3 us  [shift_over(): lax.ppermute(values, axis, [(i, (i - shift) % size) for i in range(size)])]
    all_gather x1, waiting for transfers between devices: 25.7 us -> 13.9 us  [body(): gate_up_full = lax.all_gather(gate_up_local, split, axis=0, tiled=True)]
    ppermute x53 -> x48, starting transfers between devices: 36.3 us -> 24.9 us  [swap_bit(): return lax.ppermute(values, axis, [(i, i ^ 1 << bit) for i in range(size)])]
    unnamed x201 -> x183, local copies, waits for them, and re-layouts: 36.6 us -> 26.7 us
    ppermute x17 -> x26, waiting for transfers between devices: 113 us -> 114 us  [shift_over(): lax.ppermute(values, axis, [(i, (i - shift) % size) for i in range(size)])]
  transfers between devices with their start and end apart: 75 -> 79, of which waited for: 29 -> 27; matrix products, arithmetic and copies ran while one was open for 24% -> 25% of each run, Pallas kernels for 29% -> 39%
where the time goes in v2:
time: 992 us; the launch traced here: 984 us
  Pallas kernels  380 us (38%)
  waiting for transfers between devices  251 us (25%)
  matrix products  115 us (12%)
  other arithmetic  82.7 us (8%)
  starting transfers between devices  74.4 us (8%)
  local copies, waits for them, and re-layouts  65.8 us (7%)
  between operations  15.8 us (2%)
    pallas_call x8, Pallas kernels, matmul_call(): pl.pallas_call(kernel, name=name, grid=(2,), in_specs=in_specs, out_specs...  145 us
    ppermute x48, waiting for transfers between devices, swap_bit(): return lax.ppermute(values, axis, [(i, i ^ 1 << bit) for i in range(size)])  123 us
    dot_general x8, matrix products, dot_f32(): lax.dot_general(left, right, (((left_dim,), (right_dim,)), ((), ())), pre...  115 us
    ppermute x26, waiting for transfers between devices, shift_over(): lax.ppermute(values, axis, [(i, (i - shift) % size) for i in range(size)])  114 us
    pallas_call x2, Pallas kernels, attend_back(): pl.pallas_call(kernel, name='attention_backward', out_shape=[jax.ShapeDty...  88.5 us
    pallas_call x2, Pallas kernels, attend(): pl.pallas_call(kernel, name='attention_forward', out_shape=[jax.ShapeDtyp...  68.5 us
    ppermute x26, starting transfers between devices, shift_over(): lax.ppermute(values, axis, [(i, (i - shift) % size) for i in range(size)])  49.3 us
    pallas_call x3, Pallas kernels, project(): pl.pallas_call(functools.partial(project_kernel, count, groups, slab), na...  38.4 us
  transfers between devices with their start and end apart: 79, of which 27 were waited for; matrix products, arithmetic and copies ran while one was open for 25% of the time, Pallas kernels for 39%

profile of v2, /device:TPU:0, one launch (start us, length us, event | category | flops | bytes accessed | tf_op | source)
XLA Modules:
  0.0 984.3 jit_solution(15642906208089774835)
XLA Ops:
  14.1 9.8 collective-permute-done.3.refs_4_
  33.7 7.9 collective-permute-done.1.refs_1_
  44.9 5.1 collective-permute-done.4.refs_5_
  58.4 21.1 %collective-permute-done.refs_0_ = bf16[256,2048]{1,0:T(8,128)(2,1)S(1)} collective-permute-done((bf16[256,2048]{1,0:T(8,128)(2,1)S(1)}, bf16[256,2048]{1,0:T(8,128)(2,1)S(1)}, u32[]{:S(2)}, u32[]{:S(2)}) %collective-permute-start) | collective-permute-done | bytes 1048608 | tf_op jit(solution)/shard_map/ppermute | solution.py:902
  84.9 9.7 pick_rows.1
  95.2 7.4 rotary_tables.1
  103.2 5.0 collective-permute-done.10.refs_7_
  108.3 5.9 place_rows.3.refs_3_.refs_6_
  117.2 16.5 %norm_project.3 = (bf16[4096,2048]{1,0:T(8,128)(2,1)}, bf16[4096,384]{1,0:T(8,128)(2,1)}, bf16[4096,384]{1,0:T(8,128)(2,1)}) custom-call(s32[8]{0:T(128)} %stack.118.at_ref.map_ref, bf16[2048,2048]{1,0:T(8,128)(2,1)} %refs_0_.1, f32[1,2048]{1,0:T(1,128)} %bitcast.115, f32[1,2048]{1,0:T(1,128)} %bitcast.119, bf16[2048,768]{1,0:T(8,128)(2,1)} %place_rows.3.refs_3_.refs_6_, ...), custom_call_target="tpu_custom_call" | custom-call | flops 6442450944 | bytes 19922944 | tf_op jit(solution)/shard_map/norm_project/pallas_call | solution.py:493
  133.7 10.8 %norm_project.4 = (bf16[4096,2048]{1,0:T(8,128)(2,1)}, bf16[4096,384]{1,0:T(8,128)(2,1)}, bf16[4096,384]{1,0:T(8,128)(2,1)}) custom-call(s32[1]{0:T(128)} %constant.165.clone.1.map_ref, bf16[256,2048]{1,0:T(8,128)(2,1)} %collective-permute-done.11.refs_0_, ...), custom_call_target="tpu_custom_call", output_to_operand_aliasing={{0}: (9, {}), {1}: (10, {}), {2}: (11, {})} | custom-call | flops 3221225472 | bytes 11534336 | tf_op jit(solution)/shard_map/norm_project/pallas_call | solution.py:493
  145.5 11.0 %norm_project.5 = (bf16[4096,2048]{1,0:T(8,128)(2,1)}, bf16[4096,384]{1,0:T(8,128)(2,1)}, bf16[4096,384]{1,0:T(8,128)(2,1)}) custom-call(s32[1]{0:T(128)} %constant.165.clone.1.map_ref, bf16[256,2048]{1,0:T(8,128)(2,1)} %copy-done.36, bf16[256,2048]{1,0:T(8,128)(2,1)} %collective-permute-done.6.refs_1_, ...), custom_call_target="tpu_custom_call", output_to_operand_aliasing={{0}: (9, {}), {1}: (10, {}), {2}: (11, {})} | custom-call | flops 3221225472 | bytes 11534336 | tf_op jit(solution)/shard_map/norm_project/pallas_call | solution.py:493
  156.5 34.1 %attention_forward.3 = (bf16[2048,128]{1,0:T(8,128)(2,1)}, bf16[2048,128]{1,0:T(8,128)(2,1)}, bf16[4096,384]{1,0:T(8,128)(2,1)}, bf16[4096,128]{1,0:T(8,128)(2,1)}, f32[8,4096]{1,0:T(8,128)}) custom-call(s32[32]{0:T(128)} %and_select_fusion.1.slot_ref, s32[6]{0:T(128)} %bitcast.124, bf16[4096,384]{1,0:T(8,128)(2,1)} %get-tuple-element.161.refs_0_, ...), custom_call_target="tpu_custom_call" | custom-call | flops 11453245440 | bytes 10485760 | tf_op jit(solution)/shard_map/attention_forward/pallas_call | solution.py:221
  192.3 34.4 %attention_forward.2 = (bf16[2048,128]{1,0:T(8,128)(2,1)}, bf16[2048,128]{1,0:T(8,128)(2,1)}, bf16[4096,384]{1,0:T(8,128)(2,1)}, bf16[4096,128]{1,0:T(8,128)(2,1)}, f32[8,4096]{1,0:T(8,128)}) custom-call(s32[32]{0:T(128)} %and_select_fusion.1.slot_ref, s32[6]{0:T(128)} %bitcast.125, bf16[4096,384]{1,0:T(8,128)(2,1)} %get-tuple-element.158.refs_0_, ...), custom_call_target="tpu_custom_call" | custom-call | flops 11453245440 | bytes 10485760 | tf_op jit(solution)/shard_map/attention_forward/pallas_call | solution.py:221
  231.8 9.9 %collective-permute-done.15.refs_2_ = bf16[2048,128]{1,0:T(8,128)(2,1)S(1)} collective-permute-done((bf16[2048,128]{1,0:T(8,128)(2,1)}, bf16[2048,128]{1,0:T(8,128)(2,1)S(1)}, u32[]{:S(2)}, u32[]{:S(2)}) %collective-permute-start.15) | collective-permute-done | bytes 524320 | tf_op jit(solution)/shard_map/ppermute | solution.py:902
  242.6 8.3 project_out.2
  250.9 8.3 project_out.3
  266.3 17.9 %fusion.37.refs_4_ = f32[2048,1408]{1,0:T(8,128)} fusion(bf16[2048,2048]{1,0:T(8,128)(2,1)S(1)} %bitcast.96, bf16[2048,1408]{0,1:T(8,128)(2,1)} %all-gather.4.cloned.1.call-done), kind=kOutput, calls=%fused_computation.168 | convolution fusion | flops 11811160064 | bytes 25690112 | tf_op jit(solution)/shard_map/dot_general | solution.py:27
  288.4 21.7 %collective-permute-done.23 = bf16[256,2048]{1,0:T(8,128)(2,1)S(1)} collective-permute-done((bf16[256,2048]{1,0:T(8,128)(2,1)S(1)}, bf16[256,2048]{1,0:T(8,128)(2,1)S(1)}, u32[]{:S(2)}, u32[]{:S(2)}) %collective-permute-start.23) | collective-permute-done | bytes 1048608 | tf_op jit(solution)/shard_map/ppermute | solution.py:860
  319.5 23.1 %collective-permute-done.19.refs_1_ = bf16[256,2048]{1,0:T(8,128)(2,1)} collective-permute-done((bf16[256,2048]{1,0:T(8,128)(2,1)S(1)}, bf16[256,2048]{1,0:T(8,128)(2,1)}, u32[]{:S(2)}, u32[]{:S(2)}) %collective-permute-start.19) | collective-permute-done | bytes 1048608 | tf_op jit(solution)/shard_map/ppermute | solution.py:860
  342.6 4.8 copy.84
  353.3 13.9 %all-gather.8.cloned.1.call-done.refs_5_ = bf16[2048,2816]{1,0:T(8,128)(2,1)} async-done(((bf16[256,2816]{1,0:T(8,128)(2,1)}), bf16[2048,2816]{1,0:T(8,128)(2,1)}) %all-gather.8.cloned.1.call-update) | async-done | bytes 11534352 | tf_op jit(solution)/shard_map/all_gather | solution.py:1048
  367.2 42.6 %feed_forward.2 = (bf16[2048,2048]{1,0:T(8,128)(2,1)}, bf16[2048,1408]{1,0:T(8,128)(2,1)}, bf16[2048,2816]{1,0:T(8,128)(2,1)}, bf16[512,2048]{1,0:T(8,128)(2,1)}, bf16[512,2048]{1,0:T(8,128)(2,1)}) custom-call(bf16[256,2048]{1,0:T(8,128)(2,1)} %copy-done.40, bf16[256,2048]{1,0:T(8,128)(2,1)} %collective-permute-done.19.refs_1_, ...), custom_call_target="tpu_custom_call" | custom-call | flops 23622320128 | bytes 57147392 | tf_op jit(solution)/shard_map/feed_forward/pallas_call | solution.py:590
  411.0 5.4 collective-permute-done.26
  423.4 42.9 %feed_forward.3 = (bf16[2048,2048]{1,0:T(8,128)(2,1)}, bf16[2048,1408]{1,0:T(8,128)(2,1)}, bf16[2048,2816]{1,0:T(8,128)(2,1)}, bf16[512,2048]{1,0:T(8,128)(2,1)}, bf16[512,2048]{1,0:T(8,128)(2,1)}) custom-call(bf16[256,2048]{1,0:T(8,128)(2,1)} %get-tuple-element.180.refs_0_, ...), custom_call_target="tpu_custom_call", output_to_operand_aliasing={{0}: (6, {}), {1}: (7, {}), {2}: (8, {})} | custom-call | flops 23622320128 | bytes 82837504 | tf_op jit(solution)/shard_map/feed_forward/pallas_call | solution.py:590
  479.6 17.4 %convolution_convert_fusion.2 = bf16[2048,1408]{1,0:T(8,128)(2,1)} fusion(bf16[2048,2048]{1,0:T(8,128)(2,1)S(1)} %bitcast.98, bf16[2048,1408]{1,0:T(8,128)(2,1)} %get-tuple-element.197), kind=kOutput, calls=%fused_computation.3 | convolution fusion | flops 11814043648 | bytes 19922944 | tf_op jit(solution)/shard_map/dot_general | solution.py:27
  497.1 7.4 collective-permute-done.35
  509.2 5.1 fusion.17
  516.4 29.2 %convolution_convert_fusion = bf16[2048,2816]{1,0:T(8,128)(2,1)} fusion(bf16[2048,2048]{1,0:T(8,128)(2,1)} %get-tuple-element.194, bf16[2048,2816]{1,0:T(8,128)(2,1)S(1)} %bitcast.132), kind=kOutput, calls=%fused_computation.1 | convolution fusion | flops 23628087296 | bytes 31457280 | tf_op jit(solution)/shard_map/dot_general | solution.py:27
  545.6 17.0 %convolution_convert_fusion.1 = bf16[2048,2048]{1,0:T(8,128)(2,1)S(1)} fusion(bf16[2048,1408]{1,0:T(8,128)(2,1)} %get-tuple-element.197, bf16[2048,1408]{0,1:T(8,128)(2,1)} %all-gather.4.cloned.1.call-done), kind=kOutput, calls=%fused_computation.2 | convolution fusion | flops 11815354368 | bytes 19922944 | tf_op jit(solution)/shard_map/dot_general | solution.py:27
  568.2 7.4 project_out_back.3
  575.7 7.7 project_out_back.2
  589.5 10.6 %collective-permute-done.39.refs_2_ = bf16[1024,256]{1,0:T(8,128)(2,1)} collective-permute-done((bf16[1024,256]{1,0:T(8,128)(2,1)}, bf16[1024,256]{1,0:T(8,128)(2,1)}, u32[]{:S(2)}, u32[]{:S(2)}) %collective-permute-start.39) | collective-permute-done | bytes 524320 | tf_op jit(solution)/shard_map/ppermute | solution.py:902
  600.1 5.0 fusion.38
  617.3 44.4 %attention_backward.2 = (bf16[4096,384]{1,0:T(8,128)(2,1)}, f32[8,384]{1,0:T(8,128)}) custom-call(s32[32]{0:T(128)} %and_select_fusion.1.slot_ref, s32[6]{0:T(128)} %bitcast.126, bf16[1024,256]{1,0:T(8,128)(2,1)} %get-tuple-element.225.refs_0_, bf16[1024,256]{1,0:T(8,128)(2,1)} %get-tuple-element.226.refs_1_, ...), custom_call_target="tpu_custom_call" | custom-call | flops 28633112576 | bytes 10485760 | tf_op jit(solution)/shard_map/attention_backward/pallas_call | solution.py:383
  671.3 44.1 %attention_backward.3 = (bf16[4096,384]{1,0:T(8,128)(2,1)}, f32[8,384]{1,0:T(8,128)}) custom-call(s32[32]{0:T(128)} %and_select_fusion.1.slot_ref, s32[6]{0:T(128)} %bitcast.127, bf16[1024,256]{1,0:T(8,128)(2,1)} %get-tuple-element.225.refs_0_, bf16[1024,256]{1,0:T(8,128)(2,1)} %get-tuple-element.226.refs_1_, ...), custom_call_target="tpu_custom_call" | custom-call | flops 28633112576 | bytes 10485760 | tf_op jit(solution)/shard_map/attention_backward/pallas_call | solution.py:383
  718.6 13.9 %convolution_convert_fusion.4 = bf16[2048,384]{1,0:T(8,128)(2,1)} fusion(bf16[4096,2048]{1,0:T(8,128)(2,1)} %get-tuple-element.239, bf16[4096,384]{1,0:T(8,128)(2,1)S(1)} %copy-done.41), kind=kOutput, calls=%fused_computation.33 | convolution fusion | flops 6443237376 | bytes 21495808 | tf_op jit(solution)/shard_map/dot_general | solution.py:27
  732.5 17.2 %collective-permute-done.49.refs_3_ = bf16[1024,384]{1,0:T(8,128)(2,1)S(1)} collective-permute-done((bf16[1024,384]{1,0:T(8,128)(2,1)S(1)}, bf16[1024,384]{1,0:T(8,128)(2,1)S(1)}, u32[]{:S(2)}, u32[]{:S(2)}) %collective-permute-start.49) | collective-permute-done | bytes 786464 | tf_op jit(solution)/shard_map/ppermute | solution.py:902
  749.8 10.3 %convolution_convert_fusion.3 = bf16[2048,384]{1,0:T(8,128)(2,1)} fusion(bf16[4096,2048]{1,0:T(8,128)(2,1)S(1)} %bitcast.94, bf16[4096,384]{1,0:T(8,128)(2,1)S(1)} %copy-done.42), kind=kOutput, calls=%fused_computation.32 | convolution fusion | flops 6443237376 | bytes 21495808 | tf_op jit(solution)/shard_map/dot_general | solution.py:27
  760.1 13.2 %collective-permute-done.50.refs_3_ = bf16[1024,384]{1,0:T(8,128)(2,1)S(1)} collective-permute-done((bf16[1024,384]{1,0:T(8,128)(2,1)S(1)}, bf16[1024,384]{1,0:T(8,128)(2,1)S(1)}, u32[]{:S(2)}, u32[]{:S(2)}) %collective-permute-start.50) | collective-permute-done | bytes 786464 | tf_op jit(solution)/shard_map/ppermute | solution.py:902
  774.2 13.8 %project_back.2 = (bf16[512,2048]{1,0:T(8,128)(2,1)}, bf16[512,2048]{1,0:T(8,128)(2,1)}) custom-call(bf16[4096,384]{1,0:T(8,128)(2,1)} %get-tuple-element.220.refs_0_, bf16[4096,384]{1,0:T(8,128)(2,1)} %get-tuple-element.232.refs_1_, bf16[2048,384]{1,0:T(8,128)(2,1)} %collective-permute-done.48.refs_2_, bf16[1024,384]{1,0:T(8,128)(2,1)} %copy-done.67, ...), custom_call_target="tpu_custom_call" | custom-call | flops 6442450944 | bytes 19136512 | tf_op jit(solution)/shard_map/project_back/pallas_call | solution.py:590
  796.7 14.0 %project_back.3 = (bf16[512,2048]{1,0:T(8,128)(2,1)}, bf16[512,2048]{1,0:T(8,128)(2,1)}) custom-call(bf16[4096,384]{1,0:T(8,128)(2,1)} %get-tuple-element.220.refs_0_, bf16[4096,384]{1,0:T(8,128)(2,1)} %get-tuple-element.232.refs_1_, bf16[2048,384]{1,0:T(8,128)(2,1)} %collective-permute-done.48.refs_2_, bf16[1024,384]{1,0:T(8,128)(2,1)} %copy-done.66, ...), custom_call_target="tpu_custom_call" | custom-call | flops 6442450944 | bytes 19136512 | tf_op jit(solution)/shard_map/project_back/pallas_call | solution.py:590
  810.7 9.4 collective-permute-done.52
  825.9 9.1 collective-permute-start.70
  854.0 10.4 %collective-permute-done.66 = bf16[512,768]{1,0:T(8,128)(2,1)} collective-permute-done((bf16[512,768]{1,0:T(8,128)(2,1)}, bf16[512,768]{1,0:T(8,128)(2,1)}, u32[]{:S(2)}, u32[]{:S(2)}) %collective-permute-start.66) | collective-permute-done | bytes 786464 | tf_op jit(solution)/shard_map/ppermute | solution.py:902
  871.1 7.8 place_rows.4
  899.2 15.4 %collective-permute-done.58.refs_5_ = bf16[256,2048]{1,0:T(8,128)(2,1)} collective-permute-done((bf16[256,2048]{1,0:T(8,128)(2,1)}, bf16[256,2048]{1,0:T(8,128)(2,1)}, u32[]{:S(2)}, u32[]{:S(2)}) %collective-permute-start.58) | collective-permute-done | bytes 1048608 | tf_op jit(solution)/shard_map/ppermute | solution.py:860
  918.2 16.9 %collective-permute-done.54.refs_1_ = bf16[256,2048]{1,0:T(8,128)(2,1)} collective-permute-done((bf16[256,2048]{1,0:T(8,128)(2,1)}, bf16[256,2048]{1,0:T(8,128)(2,1)}, u32[]{:S(2)}, u32[]{:S(2)}) %collective-permute-start.54) | collective-permute-done | bytes 1048608 | tf_op jit(solution)/shard_map/ppermute | solution.py:860
  967.4 8.7 place_rows.5
  (458 shorter events, 235.5 us)
Async XLA Ops:
  7.2 220.7 %all-gather.6.cloned.1.call-start = ((), (), s32[]{:S(2)}) async-start(), calls=%async_computation.3 | async-start | bytes 2359296 | tf_op jit(solution)/shard_map/all_gather | solution.py:1044
  9.0 232.7 %all-gather.4.cloned.1.call-start = ((), (), s32[]{:S(2)}) async-start(), calls=%async_computation.2 | async-start | bytes 6488064 | tf_op jit(solution)/shard_map/all_gather | solution.py:1046
  23.9 343.3 %all-gather.8.cloned.1.call-start = ((), (), s32[]{:S(2)}) async-start(), calls=%async_computation.4 | async-start | bytes 12976128 | tf_op jit(solution)/shard_map/all_gather | solution.py:1048
  30.2 26.7 %collective-permute-start.11 = (bf16[256,2048]{1,0:T(8,128)(2,1)S(1)}, bf16[256,2048]{1,0:T(8,128)(2,1)}, u32[]{:S(2)}, u32[]{:S(2)}) collective-permute-start(bf16[256,2048]{1,0:T(8,128)(2,1)S(1)} %get-tuple-element.348), channel_id=1, source_target_pairs={{0,4},{4,0},{1,5},{5,1},{2,6},{6,2},{3,7},{7,3},{8,12},{12,8},{9,1... | collective-permute-start | bytes 3145736 | tf_op jit(solution)/shard_map/ppermute | solution.py:902
  32.7 46.9 %collective-permute-start = (bf16[256,2048]{1,0:T(8,128)(2,1)S(1)}, bf16[256,2048]{1,0:T(8,128)(2,1)S(1)}, u32[]{:S(2)}, u32[]{:S(2)}) collective-permute-start(bf16[256,2048]{1,0:T(8,128)(2,1)S(1)} %get-tuple-element.330), channel_id=1, source_target_pairs={{0,4},{4,0},{1,5},{5,1},{2,6},{6,2},{3,7},{7,3},{8,12},{12,8},{9,1... | collective-permute-start | bytes 3145736 | tf_op jit(solution)/shard_map/ppermute | solution.py:902
  50.0 29.6 %collective-permute-start.5 = (bf16[256,768]{1,0:T(8,128)(2,1)}, bf16[256,768]{1,0:T(8,128)(2,1)}, u32[]{:S(2)}, u32[]{:S(2)}) collective-permute-start(bf16[256,768]{1,0:T(8,128)(2,1)} %collective-permute-done.4.refs_5_), channel_id=1, source_target_pairs={{0,24},{8,0},{16,8},{24,16},{1,25},{9,1},{17,9},{25,17},{2,26},{10... | collective-permute-start | bytes 1179656 | tf_op jit(solution)/shard_map/ppermute | solution.py:902
  56.9 51.3 %collective-permute-start.12 = (bf16[256,2048]{1,0:T(8,128)(2,1)}, bf16[256,2048]{1,0:T(8,128)(2,1)}, u32[]{:S(2)}, u32[]{:S(2)}) collective-permute-start(bf16[256,2048]{1,0:T(8,128)(2,1)} %collective-permute-done.11.refs_0_), channel_id=1, source_target_pairs={{0,2},{1,3},{2,0},{3,1},{4,6},{5,7},{6,4},{7,5},{8,10},{9,11},{10,... | collective-permute-start | bytes 3145736 | tf_op jit(solution)/shard_map/ppermute | solution.py:860
  79.6 28.6 %collective-permute-start.6 = (bf16[256,2048]{1,0:T(8,128)(2,1)S(1)}, bf16[256,2048]{1,0:T(8,128)(2,1)}, u32[]{:S(2)}, u32[]{:S(2)}) collective-permute-start(bf16[256,2048]{1,0:T(8,128)(2,1)S(1)} %collective-permute-done.refs_0_), channel_id=1, source_target_pairs={{0,2},{1,3},{2,0},{3,1},{4,6},{5,7},{6,4},{7,5},{8,10},{9,11},{10,... | collective-permute-start | bytes 3145736 | tf_op jit(solution)/shard_map/ppermute | solution.py:860
  81.5 26.7 %collective-permute-start.10 = (bf16[256,768]{1,0:T(8,128)(2,1)}, bf16[256,768]{1,0:T(8,128)(2,1)}, u32[]{:S(2)}, u32[]{:S(2)}) collective-permute-start(bf16[256,768]{1,0:T(8,128)(2,1)} %collective-permute-done.5.refs_6_), channel_id=1, source_target_pairs={{0,24},{8,0},{16,8},{24,16},{1,25},{9,1},{17,9},{25,17},{2,26},{10... | collective-permute-start | bytes 1179656 | tf_op jit(solution)/shard_map/ppermute | solution.py:902
  114.2 774.3 %reduce-scatter.3.cloned.1.call-start = ((), (), s32[]{:S(2)}) async-start(), calls=%async_computation.5 | async-start | bytes 6488064 | tf_op jit(solution)/shard_map/reduce_scatter | solution.py:1173
  114.9 29.7 %collective-permute-start.7 = (bf16[256,2048]{1,0:T(8,128)(2,1)S(1)}, bf16[256,2048]{1,0:T(8,128)(2,1)S(1)}, u32[]{:S(2)}, u32[]{:S(2)}) collective-permute-start(bf16[256,2048]{1,0:T(8,128)(2,1)S(1)} %collective-permute-done.refs_0_), channel_id=1, source_target_pairs={{0,1},{1,0},{2,3},{3,2},{4,5},{5,4},{6,7},{7,6},{8,9},{9,8},{10,11... | collective-permute-start | bytes 3145736 | tf_op jit(solution)/shard_map/ppermute | solution.py:860
  114.9 29.6 %collective-permute-start.8 = (bf16[256,2048]{1,0:T(8,128)(2,1)}, bf16[256,2048]{1,0:T(8,128)(2,1)}, u32[]{:S(2)}, u32[]{:S(2)}) collective-permute-start(bf16[256,2048]{1,0:T(8,128)(2,1)} %collective-permute-done.6.refs_1_), channel_id=1, source_target_pairs={{0,1},{1,0},{2,3},{3,2},{4,5},{5,4},{6,7},{7,6},{8,9},{9,8},{10,11... | collective-permute-start | bytes 3145736 | tf_op jit(solution)/shard_map/ppermute | solution.py:860
  190.7 41.2 %collective-permute-start.16 = (bf16[2048,128]{1,0:T(8,128)(2,1)}, bf16[2048,128]{1,0:T(8,128)(2,1)S(1)}, u32[]{:S(2)}, u32[]{:S(2)}) collective-permute-start(bf16[2048,128]{1,0:T(8,128)(2,1)} %get-tuple-element.163), channel_id=1, source_target_pairs={{0,4},{4,0},{1,5},{5,1},{2,6},{6,2},{3,7},{7,3},{8,12},{12,8},{9,1... | collective-permute-start | bytes 1572872 | tf_op jit(solution)/shard_map/ppermute | solution.py:902
  262.4 26.1 %collective-permute-start.18 = (bf16[256,2048]{1,0:T(8,128)(2,1)S(1)}, bf16[256,2048]{1,0:T(8,128)(2,1)S(1)}, u32[]{:S(2)}, u32[]{:S(2)}) collective-permute-start(bf16[256,2048]{1,0:T(8,128)(2,1)S(1)} %slice.218), channel_id=1, source_target_pairs={{0,2},{1,3},{2,0},{3,1},{4,6},{5,7},{6,4},{7,5},{8,10},{9,11},{10,... | collective-permute-start | bytes 3145736 | tf_op jit(solution)/shard_map/ppermute | solution.py:860
  264.9 45.2 %collective-permute-start.23 = (bf16[256,2048]{1,0:T(8,128)(2,1)S(1)}, bf16[256,2048]{1,0:T(8,128)(2,1)S(1)}, u32[]{:S(2)}, u32[]{:S(2)}) collective-permute-start(bf16[256,2048]{1,0:T(8,128)(2,1)S(1)} %slice.217), channel_id=1, source_target_pairs={{0,2},{1,3},{2,0},{3,1},{4,6},{5,7},{6,4},{7,5},{8,10},{9,11},{10,... | collective-permute-start | bytes 3145736 | tf_op jit(solution)/shard_map/ppermute | solution.py:860
  318.0 24.6 %collective-permute-start.19 = (bf16[256,2048]{1,0:T(8,128)(2,1)S(1)}, bf16[256,2048]{1,0:T(8,128)(2,1)}, u32[]{:S(2)}, u32[]{:S(2)}) collective-permute-start(bf16[256,2048]{1,0:T(8,128)(2,1)S(1)} %get-tuple-element.364.refs_0_), channel_id=1, source_target_pairs={{0,2},{1,3},{2,0},{3,1},{4,6},{5,7},{6,4},{7,5},{8,10},{9,11},{10,... | collective-permute-start | bytes 3145736 | tf_op jit(solution)/shard_map/ppermute | solution.py:860
  319.5 33.8 %collective-permute-start.20 = (bf16[256,2048]{1,0:T(8,128)(2,1)S(1)}, bf16[256,2048]{1,0:T(8,128)(2,1)}, u32[]{:S(2)}, u32[]{:S(2)}) collective-permute-start(bf16[256,2048]{1,0:T(8,128)(2,1)S(1)} %get-tuple-element.364.refs_0_), channel_id=1, source_target_pairs={{0,1},{1,0},{2,3},{3,2},{4,5},{5,4},{6,7},{7,6},{8,9},{9,8},{10,11... | collective-permute-start | bytes 3145736 | tf_op jit(solution)/shard_map/ppermute | solution.py:860
  351.2 58.6 %collective-permute-start.25 = (bf16[1024,768]{0,1:T(8,128)(2,1)}, bf16[1024,768]{0,1:T(8,128)(2,1)}, u32[]{:S(2)}, u32[]{:S(2)}) collective-permute-start(bf16[1024,768]{0,1:T(8,128)(2,1)} %get-tuple-element.352), channel_id=1, source_target_pairs={{0,4},{4,0},{1,5},{5,1},{2,6},{6,2},{3,7},{7,3},{8,12},{12,8},{9,1... | collective-permute-start | bytes 4718600 | tf_op jit(solution)/shard_map/ppermute | solution.py:902
  351.6 58.3 %collective-permute-start.24 = (bf16[256,2048]{1,0:T(8,128)(2,1)}, bf16[256,2048]{1,0:T(8,128)(2,1)}, u32[]{:S(2)}, u32[]{:S(2)}) collective-permute-start(bf16[256,2048]{1,0:T(8,128)(2,1)} %get-tuple-element.180.refs_0_), channel_id=1, source_target_pairs={{0,2},{1,3},{2,0},{3,1},{4,6},{5,7},{6,4},{7,5},{8,10},{9,11},{10,... | collective-permute-start | bytes 3145736 | tf_op jit(solution)/shard_map/ppermute | solution.py:860
  410.5 60.4 %collective-permute-start.33 = (bf16[1024,768]{0,1:T(8,128)(2,1)}, bf16[1024,768]{0,1:T(8,128)(2,1)S(1)}, u32[]{:S(2)}, u32[]{:S(2)}) collective-permute-start(bf16[1024,768]{0,1:T(8,128)(2,1)} %get-tuple-element.189), channel_id=1, source_target_pairs={{0,4},{4,0},{1,5},{5,1},{2,6},{6,2},{3,7},{7,3},{8,12},{12,8},{9,1... | collective-permute-start | bytes 4718600 | tf_op jit(solution)/shard_map/ppermute | solution.py:902
  421.9 44.4 %collective-permute-start.27 = (bf16[256,2048]{1,0:T(8,128)(2,1)}, bf16[256,2048]{1,0:T(8,128)(2,1)}, u32[]{:S(2)}, u32[]{:S(2)}) collective-permute-start(bf16[256,2048]{1,0:T(8,128)(2,1)} %slice.216), channel_id=1, source_target_pairs={{0,2},{1,3},{2,0},{3,1},{4,6},{5,7},{6,4},{7,5},{8,10},{9,11},{10,... | collective-permute-start | bytes 3145736 | tf_op jit(solution)/shard_map/ppermute | solution.py:860
  479.0 25.4 %collective-permute-start.35 = (bf16[256,2048]{1,0:T(8,128)(2,1)}, bf16[256,2048]{1,0:T(8,128)(2,1)S(1)}, u32[]{:S(2)}, u32[]{:S(2)}) collective-permute-start(bf16[256,2048]{1,0:T(8,128)(2,1)} %slice.215), channel_id=1, source_target_pairs={{0,2},{1,3},{2,0},{3,1},{4,6},{5,7},{6,4},{7,5},{8,10},{9,11},{10,... | collective-permute-start | bytes 3145736 | tf_op jit(solution)/shard_map/ppermute | solution.py:860
  497.0 441.8 %reduce-scatter.5.cloned.1.call-start = ((), (), s32[]{:S(2)}) async-start(), calls=%async_computation.6 | async-start | bytes 12976128 | tf_op jit(solution)/shard_map/reduce_scatter | solution.py:1174
  514.3 48.3 %collective-permute-start.36 = (bf16[256,2048]{1,0:T(8,128)(2,1)S(1)}, bf16[256,2048]{1,0:T(8,128)(2,1)}, u32[]{:S(2)}, u32[]{:S(2)}) collective-permute-start(bf16[256,2048]{1,0:T(8,128)(2,1)S(1)} %get-tuple-element.198.refs_0_), channel_id=1, source_target_pairs={{0,2},{1,3},{2,0},{3,1},{4,6},{5,7},{6,4},{7,5},{8,10},{9,11},{10,... | collective-permute-start | bytes 3145736 | tf_op jit(solution)/shard_map/ppermute | solution.py:860
  514.9 48.4 %collective-permute-start.28 = (bf16[256,2048]{1,0:T(8,128)(2,1)}, bf16[256,2048]{1,0:T(8,128)(2,1)}, u32[]{:S(2)}, u32[]{:S(2)}) collective-permute-start(bf16[256,2048]{1,0:T(8,128)(2,1)} %get-tuple-element.346.refs_0_), channel_id=1, source_target_pairs={{0,2},{1,3},{2,0},{3,1},{4,6},{5,7},{6,4},{7,5},{8,10},{9,11},{10,... | collective-permute-start | bytes 3145736 | tf_op jit(solution)/shard_map/ppermute | solution.py:860
  583.3 25.8 %collective-permute-start.41 = (bf16[512,2048]{1,0:T(8,128)(2,1)}, bf16[512,2048]{1,0:T(8,128)(2,1)}, u32[]{:S(2)}, u32[]{:S(2)}) collective-permute-start(bf16[512,2048]{1,0:T(8,128)(2,1)} %get-tuple-element.203), channel_id=1, source_target_pairs={{0,1},{1,0},{2,3},{3,2},{4,5},{5,4},{6,7},{7,6},{8,9},{9,8},{10,11... | collective-permute-start | bytes 6291464 | tf_op jit(solution)/shard_map/ppermute | solution.py:860
  583.4 25.7 %collective-permute-start.42 = (bf16[512,2048]{1,0:T(8,128)(2,1)}, bf16[512,2048]{1,0:T(8,128)(2,1)}, u32[]{:S(2)}, u32[]{:S(2)}) collective-permute-start(bf16[512,2048]{1,0:T(8,128)(2,1)} %get-tuple-element.204), channel_id=1, source_target_pairs={{0,1},{1,0},{2,3},{3,2},{4,5},{5,4},{6,7},{7,6},{8,9},{9,8},{10,11... | collective-permute-start | bytes 6291464 | tf_op jit(solution)/shard_map/ppermute | solution.py:860
  587.9 25.3 %collective-permute-start.40 = (bf16[1024,256]{1,0:T(8,128)(2,1)}, bf16[1024,256]{1,0:T(8,128)(2,1)S(1)}, u32[]{:S(2)}, u32[]{:S(2)}) collective-permute-start(bf16[1024,256]{1,0:T(8,128)(2,1)} %get-tuple-element.202), channel_id=1, source_target_pairs={{0,4},{4,0},{1,5},{5,1},{2,6},{6,2},{3,7},{7,3},{8,12},{12,8},{9,1... | collective-permute-start | bytes 1572872 | tf_op jit(solution)/shard_map/ppermute | solution.py:902
  614.4 50.7 %collective-permute-start.44 = (bf16[256,2048]{1,0:T(8,128)(2,1)}, bf16[256,2048]{1,0:T(8,128)(2,1)}, u32[]{:S(2)}, u32[]{:S(2)}) collective-permute-start(bf16[256,2048]{1,0:T(8,128)(2,1)} %slice.213), channel_id=1, source_target_pairs={{0,2},{1,3},{2,0},{3,1},{4,6},{5,7},{6,4},{7,5},{8,10},{9,11},{10,... | collective-permute-start | bytes 3145736 | tf_op jit(solution)/shard_map/ppermute | solution.py:860
  616.1 51.7 %collective-permute-start.43 = (bf16[256,2048]{1,0:T(8,128)(2,1)S(1)}, bf16[256,2048]{1,0:T(8,128)(2,1)}, u32[]{:S(2)}, u32[]{:S(2)}) collective-permute-start(bf16[256,2048]{1,0:T(8,128)(2,1)S(1)} %slice.214), channel_id=1, source_target_pairs={{0,2},{1,3},{2,0},{3,1},{4,6},{5,7},{6,4},{7,5},{8,10},{9,11},{10,... | collective-permute-start | bytes 3145736 | tf_op jit(solution)/shard_map/ppermute | solution.py:860
  664.6 52.6 %collective-permute-start.48 = (bf16[2048,384]{1,0:T(8,128)(2,1)}, bf16[2048,384]{1,0:T(8,128)(2,1)}, u32[]{:S(2)}, u32[]{:S(2)}) collective-permute-start(bf16[2048,384]{1,0:T(8,128)(2,1)} %slice.138), channel_id=1, source_target_pairs={{0,4},{4,0},{1,5},{5,1},{2,6},{6,2},{3,7},{7,3},{8,12},{12,8},{9,1... | collective-permute-start | bytes 4718600 | tf_op jit(solution)/shard_map/ppermute | solution.py:902
  669.8 47.4 %collective-permute-start.45 = (bf16[512,2048]{1,0:T(8,128)(2,1)S(1)}, bf16[512,2048]{1,0:T(8,128)(2,1)}, u32[]{:S(2)}, u32[]{:S(2)}) collective-permute-start(bf16[512,2048]{1,0:T(8,128)(2,1)S(1)} %constant_dynamic-update-slice_fusion.refs_0_), channel_id=1, source_target_pairs={{0,2},{1,3},{2,0},{3,1},{4,6},{5,7},{6,4},{7,5},{8,10},{9,11},{10,... | collective-permute-start | bytes 6291464 | tf_op jit(solution)/shard_map/ppermute | solution.py:860
  717.2 32.5 %collective-permute-start.49 = (bf16[1024,384]{1,0:T(8,128)(2,1)S(1)}, bf16[1024,384]{1,0:T(8,128)(2,1)S(1)}, u32[]{:S(2)}, u32[]{:S(2)}) collective-permute-start(bf16[1024,384]{1,0:T(8,128)(2,1)S(1)} %get-tuple-element.235), channel_id=1, source_target_pairs={{0,4},{4,0},{1,5},{5,1},{2,6},{6,2},{3,7},{7,3},{8,12},{12,8},{9,1... | collective-permute-start | bytes 2359304 | tf_op jit(solution)/shard_map/ppermute | solution.py:902
  794.8 25.3 %collective-permute-start.52 = (bf16[256,2048]{1,0:T(8,128)(2,1)S(1)}, bf16[256,2048]{1,0:T(8,128)(2,1)S(1)}, u32[]{:S(2)}, u32[]{:S(2)}) collective-permute-start(bf16[256,2048]{1,0:T(8,128)(2,1)S(1)} %slice.212), channel_id=1, source_target_pairs={{0,2},{1,3},{2,0},{3,1},{4,6},{5,7},{6,4},{7,5},{8,10},{9,11},{10,... | collective-permute-start | bytes 3145736 | tf_op jit(solution)/shard_map/ppermute | solution.py:860
  835.0 36.1 %collective-permute-start.46 = (bf16[512,2048]{1,0:T(8,128)(2,1)}, bf16[512,2048]{1,0:T(8,128)(2,1)}, u32[]{:S(2)}, u32[]{:S(2)}) collective-permute-start(bf16[512,2048]{1,0:T(8,128)(2,1)} %copy-done.24), channel_id=1, source_target_pairs={{0,1},{1,0},{2,3},{3,2},{4,5},{5,4},{6,7},{7,6},{8,9},{9,8},{10,11... | collective-permute-start | bytes 6291464 | tf_op jit(solution)/shard_map/ppermute | solution.py:860
  835.2 35.9 %collective-permute-start.47 = (bf16[512,2048]{1,0:T(8,128)(2,1)}, bf16[512,2048]{1,0:T(8,128)(2,1)}, u32[]{:S(2)}, u32[]{:S(2)}) collective-permute-start(bf16[512,2048]{1,0:T(8,128)(2,1)} %collective-permute-done.45.refs_1_), channel_id=1, source_target_pairs={{0,1},{1,0},{2,3},{3,2},{4,5},{5,4},{6,7},{7,6},{8,9},{9,8},{10,11... | collective-permute-start | bytes 6291464 | tf_op jit(solution)/shard_map/ppermute | solution.py:860
  838.4 26.0 %collective-permute-start.66 = (bf16[512,768]{1,0:T(8,128)(2,1)}, bf16[512,768]{1,0:T(8,128)(2,1)}, u32[]{:S(2)}, u32[]{:S(2)}) collective-permute-start(bf16[512,768]{1,0:T(8,128)(2,1)} %constant_dynamic-slice_fusion.2), channel_id=1, source_target_pairs={{0,24},{8,0},{16,8},{24,16},{1,25},{9,1},{17,9},{25,17},{2,26},{10... | collective-permute-start | bytes 2359304 | tf_op jit(solution)/shard_map/ppermute | solution.py:902
  844.9 34.1 %collective-permute-start.57 = (bf16[256,2048]{1,0:T(8,128)(2,1)}, bf16[256,2048]{1,0:T(8,128)(2,1)}, u32[]{:S(2)}, u32[]{:S(2)}) collective-permute-start(bf16[256,2048]{1,0:T(8,128)(2,1)} %slice.211), channel_id=1, source_target_pairs={{0,2},{1,3},{2,0},{3,1},{4,6},{5,7},{6,4},{7,5},{8,10},{9,11},{10,... | collective-permute-start | bytes 3145736 | tf_op jit(solution)/shard_map/ppermute | solution.py:860
  849.7 41.4 %collective-permute-start.71 = (bf16[512,512]{1,0:T(8,128)(2,1)}, bf16[512,512]{1,0:T(8,128)(2,1)}, u32[]{:S(2)}, u32[]{:S(2)}) collective-permute-start(bf16[512,512]{1,0:T(8,128)(2,1)} %add_convert_fusion.11), channel_id=1, source_target_pairs={{0,24},{8,0},{16,8},{24,16},{1,25},{9,1},{17,9},{25,17},{2,26},{10... | collective-permute-start | bytes 1572872 | tf_op jit(solution)/shard_map/ppermute | solution.py:902
  866.8 25.6 %collective-permute-start.67 = (bf16[512,768]{1,0:T(8,128)(2,1)}, bf16[512,768]{1,0:T(8,128)(2,1)}, u32[]{:S(2)}, u32[]{:S(2)}) collective-permute-start(bf16[512,768]{1,0:T(8,128)(2,1)} %add_convert_fusion.9), channel_id=1, source_target_pairs={{0,24},{8,0},{16,8},{24,16},{1,25},{9,1},{17,9},{25,17},{2,26},{10... | collective-permute-start | bytes 2359304 | tf_op jit(solution)/shard_map/ppermute | solution.py:902
  888.2 26.4 %collective-permute-start.58 = (bf16[256,2048]{1,0:T(8,128)(2,1)}, bf16[256,2048]{1,0:T(8,128)(2,1)}, u32[]{:S(2)}, u32[]{:S(2)}) collective-permute-start(bf16[256,2048]{1,0:T(8,128)(2,1)} %get-tuple-element.254.refs_4_), channel_id=1, source_target_pairs={{0,2},{1,3},{2,0},{3,1},{4,6},{5,7},{6,4},{7,5},{8,10},{9,11},{10,... | collective-permute-start | bytes 3145736 | tf_op jit(solution)/shard_map/ppermute | solution.py:860
  891.0 52.3 %collective-permute-start.59 = (bf16[256,2048]{1,0:T(8,128)(2,1)}, bf16[256,2048]{1,0:T(8,128)(2,1)}, u32[]{:S(2)}, u32[]{:S(2)}) collective-permute-start(bf16[256,2048]{1,0:T(8,128)(2,1)} %get-tuple-element.254.refs_4_), channel_id=1, source_target_pairs={{0,1},{1,0},{2,3},{3,2},{4,5},{5,4},{6,7},{7,6},{8,9},{9,8},{10,11... | collective-permute-start | bytes 3145736 | tf_op jit(solution)/shard_map/ppermute | solution.py:860
  893.8 42.0 %collective-permute-start.68 = (bf16[512,768]{1,0:T(8,128)(2,1)S(1)}, bf16[512,768]{1,0:T(8,128)(2,1)S(1)}, u32[]{:S(2)}, u32[]{:S(2)}) collective-permute-start(bf16[512,768]{1,0:T(8,128)(2,1)S(1)} %add_convert_fusion.8), channel_id=1, source_target_pairs={{0,24},{8,0},{16,8},{24,16},{1,25},{9,1},{17,9},{25,17},{2,26},{10... | collective-permute-start | bytes 2359304 | tf_op jit(solution)/shard_map/ppermute | solution.py:902
  897.7 37.3 %collective-permute-start.54 = (bf16[256,2048]{1,0:T(8,128)(2,1)}, bf16[256,2048]{1,0:T(8,128)(2,1)}, u32[]{:S(2)}, u32[]{:S(2)}) collective-permute-start(bf16[256,2048]{1,0:T(8,128)(2,1)} %get-tuple-element.340.refs_0_), channel_id=1, source_target_pairs={{0,2},{1,3},{2,0},{3,1},{4,6},{5,7},{6,4},{7,5},{8,10},{9,11},{10,... | collective-permute-start | bytes 3145736 | tf_op jit(solution)/shard_map/ppermute | solution.py:860
  914.6 28.7 %collective-permute-start.60 = (bf16[256,2048]{1,0:T(8,128)(2,1)}, bf16[256,2048]{1,0:T(8,128)(2,1)}, u32[]{:S(2)}, u32[]{:S(2)}) collective-permute-start(bf16[256,2048]{1,0:T(8,128)(2,1)} %collective-permute-done.58.refs_5_), channel_id=1, source_target_pairs={{0,1},{1,0},{2,3},{3,2},{4,5},{5,4},{6,7},{7,6},{8,9},{9,8},{10,11... | collective-permute-start | bytes 3145736 | tf_op jit(solution)/shard_map/ppermute | solution.py:860
  916.5 50.9 %collective-permute-start.55 = (bf16[256,2048]{1,0:T(8,128)(2,1)}, bf16[256,2048]{1,0:T(8,128)(2,1)}, u32[]{:S(2)}, u32[]{:S(2)}) collective-permute-start(bf16[256,2048]{1,0:T(8,128)(2,1)} %get-tuple-element.340.refs_0_), channel_id=1, source_target_pairs={{0,1},{1,0},{2,3},{3,2},{4,5},{5,4},{6,7},{7,6},{8,9},{9,8},{10,11... | collective-permute-start | bytes 3145736 | tf_op jit(solution)/shard_map/ppermute | solution.py:860
  935.1 32.3 %collective-permute-start.56 = (bf16[256,2048]{1,0:T(8,128)(2,1)}, bf16[256,2048]{1,0:T(8,128)(2,1)}, u32[]{:S(2)}, u32[]{:S(2)}) collective-permute-start(bf16[256,2048]{1,0:T(8,128)(2,1)} %collective-permute-done.54.refs_1_), channel_id=1, source_target_pairs={{0,1},{1,0},{2,3},{3,2},{4,5},{5,4},{6,7},{7,6},{8,9},{9,8},{10,11... | collective-permute-start | bytes 3145736 | tf_op jit(solution)/shard_map/ppermute | solution.py:860
  935.8 26.3 %collective-permute-start.73 = (bf16[256,512]{1,0:T(8,128)(2,1)}, bf16[256,512]{1,0:T(8,128)(2,1)S(1)}, u32[]{:S(2)}, u32[]{:S(2)}) collective-permute-start(bf16[256,512]{1,0:T(8,128)(2,1)} %dynamic-slice_convert_fusion), channel_id=1, source_target_pairs={{0,4},{4,0},{1,5},{5,1},{2,6},{6,2},{3,7},{7,3},{8,12},{12,8},{9,1... | collective-permute-start | bytes 786440 | tf_op jit(solution)/shard_map/ppermute | solution.py:902
  (118 other events, 1640.5 us)
Sparse Core Ops, SparseCore 0:
  10.1 91.8 all-gather.5
  104.1 98.3 all-gather.3
  205.2 161.9 all-gather.7
  497.1 108.3 reduce-scatter.2
  609.0 208.9 reduce-scatter.4

commit v3 on v2

--- a/solution.py
+++ b/solution.py
@@ -890,10 +890,14 @@
     return pieces
 
 
-def butterfly(values):
+def butterfly(values, steps, after):
+    count = 0
     for axis in ("ctx", "dp", "tensor"):
         for bit in range(lax.axis_size(axis).bit_length() - 1):
+            if count == steps:
+                values, _ = lax.optimization_barrier((values, after))
             values = values + swap_bit(values, axis, bit)
+            count += 1
     return values
 
 
@@ -996,13 +1000,18 @@
     qkv_pieces = ring_rows(from_ctx)
 
     peer_pieces = [[None] * chunks for _ in range(n_ctx)]
+    awaited = []
     for chunk in range(chunks):
         own = own_share(tokens, chunk)
         for shift in range(1, n_ctx):
             arrived = shift_over(own, "ctx", shift)
-            steps = [qkv_pieces[s * n_dp + min(chunk + 1, n_dp - 1)] for s in range(n_ctx)]
+            last = chunk + 1 == chunks
+            reached = n_dp - 1 if last else min(chunk + 2, n_dp - 1)
+            steps = [qkv_pieces[s * n_dp + reached] for s in range(n_ctx)]
             arrived, _ = lax.optimization_barrier((arrived, steps))
-            peer_pieces[n_ctx - shift][chunk] = gather_pieces(arrived, bits)
+            pieces = gather_pieces(arrived, bits)
+            peer_pieces[n_ctx - shift][chunk] = pieces
+            awaited.append(arrived if last else pieces[: n_tensor // 2])
 
     def scatter_ring(partial, axis, after=()):
         size, index = lax.axis_size(axis), lax.axis_index(axis)
@@ -1036,9 +1045,8 @@
     tokens_own = [own_share(tokens, chunk) for chunk in range(chunks)]
     cotangent_rot = pick_rows(share_at, cotangent, share)
     gate_up_local = w_gate_up.reshape(-1, 2 * hidden_width)
-    peers_half = [item[: n_tensor // 2] for items in peer_pieces[1:] for item in items]
     qkv_pieces, _ = lax.optimization_barrier(
-        (qkv_pieces, (peers_half, table, slots, tokens_own, cotangent_rot, gate_up_local))
+        (qkv_pieces, (awaited, table, slots, tokens_own, cotangent_rot, gate_up_local))
     )
     qkv_mine = place_rows(piece_at, qkv_pieces)
     out_full = lax.all_gather(w_out.T, split, axis=0, tiled=True)
@@ -1157,7 +1165,10 @@
         own = d_middle[chunk].astype(low)
         arrived_middle.append(gather_first(own, bits))
     ready, _ = lax.optimization_barrier(((hidden, d_gate_up), own))
-    grad_gate_up = dot_f32(normed2, ready[1], 0, 0).astype(low)
+    grad_gate_up = [
+        dot_f32(normed2, ready[1][:, part * hidden_width : (part + 1) * hidden_width], 0, 0).astype(low)
+        for part in range(2)
+    ]
     feed_partial = dot_f32(ready[0], down_full, 1, 1).astype(low)
     arrived_middle[-1], _ = lax.optimization_barrier(
         (arrived_middle[-1], (grad_gate_up, feed_partial, qkv_all))
@@ -1171,7 +1182,7 @@
     back_parts = [arrived_back[chunk][s] for s in range(n_ctx) for chunk in range(chunks)]
 
     grad_down = lax.psum_scatter(grad_down, split, scatter_dimension=0, tiled=True)
-    grad_gate_up = lax.psum_scatter(grad_gate_up, split, scatter_dimension=0, tiled=True)
+    grad_gate = lax.psum_scatter(grad_gate_up[0], split, scatter_dimension=0, tiled=True)
 
     late, _ = lax.optimization_barrier((d_middle_low, arrived_back[0]))
     grad_out = over_rows(late, attended)
@@ -1212,6 +1223,9 @@
             output_pieces = gather_first(jnp.concatenate(output_shares, axis=0), bits)
     output_pieces, _ = lax.optimization_barrier((output_pieces, d_group))
     output_pieces = gather_rest(output_pieces, bits)
+    grad_up, _ = lax.optimization_barrier((grad_gate_up[1], d_parts[-1]))
+    grad_up = lax.psum_scatter(grad_up, split, scatter_dimension=0, tiled=True)
+
     partials = []
     for group in range(groups):
         after = d_group if group == 0 else d_parts[-1][0]
@@ -1253,7 +1267,7 @@
     grad_out = scatter_ring(grad_out, "dp", after)[-1]
     grad_qkv = scatter_ring(jnp.concatenate(partials, axis=1), "dp", after)[-1].astype(low)
     grad_down = grad_down.astype(f32).T
-    grad_gate_up = grad_gate_up.astype(f32).reshape(-1, 2, hidden_width)
+    grad_gate_up = jnp.stack([grad_gate.astype(f32), grad_up.astype(f32)], axis=1)
     token_pieces[-1], _ = lax.optimization_barrier((token_pieces[-1], (grad_down, grad_gate_up)))
     grad_tokens = unrotate(token_pieces)
 
@@ -1273,12 +1287,9 @@
     )
     small = [d_gain_one, d_shift_one, d_gain_two, d_shift_two, bias_slots.reshape(-1)]
     small, _ = lax.optimization_barrier(
-        (
-            jnp.concatenate(small).reshape(-1, 128),
-            [items[: n_tensor // 2] for items in token_pieces],
-        )
-    )
-    small = butterfly(small).reshape(-1)
+        (jnp.concatenate(small).reshape(-1, 128), token_pieces[0][: n_tensor // 2])
+    )
+    small = butterfly(small, 2, token_pieces[-1][: n_tensor // 2]).reshape(-1)
     norms = [small[index * features : (index + 1) * features] for index in range(4)]
     bias_sum = take_block(small[4 * features :].reshape(n_tensor, -1), mine, 1, 0)
     bias_sum = (

time: 992 us -> 1000 us (level)
  local copies, waits for them, and re-layouts: 65.8 us -> 79.3 us
  starting transfers between devices: 74.4 us -> 62.4 us
    all_gather x1, waiting for transfers between devices: 13.9 us -> 0.01 us  [body(): gate_up_full = lax.all_gather(gate_up_local, split, axis=0, tiled=True)]
    ppermute x26, starting transfers between devices: 49.3 us -> 38.1 us  [shift_over(): lax.ppermute(values, axis, [(i, (i - shift) % size) for i in range(size)])]
    ppermute x48, waiting for transfers between devices: 123 us -> 134 us  [swap_bit(): return lax.ppermute(values, axis, [(i, i ^ 1 << bit) for i in range(size)])]
    dot_general x8 -> x9, matrix products: 115 us -> 124 us  [dot_f32(): lax.dot_general(left, right, (((left_dim,), (right_dim,)), ((), ())), pre...]
    unnamed x183 -> x184, local copies, waits for them, and re-layouts: 26.7 us -> 36 us
  transfers between devices with their start and end apart: 79 -> 80, of which waited for: 27 -> 31; matrix products, arithmetic and copies ran while one was open for 25% -> 26% of each run, Pallas kernels for 39% -> 38%
where the time goes in v3:
time: 1000 us; the launch traced here: 993 us
  Pallas kernels  381 us (38%)
  waiting for transfers between devices  253 us (25%)
  matrix products  124 us (12%)
  local copies, waits for them, and re-layouts  79.3 us (8%)
  other arithmetic  77.2 us (8%)
  starting transfers between devices  62.4 us (6%)
  between operations  16.2 us (2%)
    pallas_call x8, Pallas kernels, matmul_call(): pl.pallas_call(kernel, name=name, grid=(2,), in_specs=in_specs, out_specs...  146 us
    ppermute x48, waiting for transfers between devices, swap_bit(): return lax.ppermute(values, axis, [(i, i ^ 1 << bit) for i in range(size)])  134 us
    dot_general x9, matrix products, dot_f32(): lax.dot_general(left, right, (((left_dim,), (right_dim,)), ((), ())), pre...  124 us
    ppermute x26, waiting for transfers between devices, shift_over(): lax.ppermute(values, axis, [(i, (i - shift) % size) for i in range(size)])  119 us
    pallas_call x2, Pallas kernels, attend_back(): pl.pallas_call(kernel, name='attention_backward', out_shape=[jax.ShapeDty...  88.6 us
    pallas_call x2, Pallas kernels, attend(): pl.pallas_call(kernel, name='attention_forward', out_shape=[jax.ShapeDtyp...  68.9 us
    pallas_call x3, Pallas kernels, project(): pl.pallas_call(functools.partial(project_kernel, count, groups, slab), na...  38.4 us
    ppermute x26, starting transfers between devices, shift_over(): lax.ppermute(values, axis, [(i, (i - shift) % size) for i in range(size)])  38.1 us
  transfers between devices with their start and end apart: 80, of which 31 were waited for; matrix products, arithmetic and copies ran while one was open for 26% of the time, Pallas kernels for 38%

profile of v3, /device:TPU:0, one launch (start us, length us, event | category | flops | bytes accessed | tf_op | source)
XLA Modules:
  0.0 993.2 jit_solution(7695667798511912927)
XLA Ops:
  14.1 9.8 collective-permute-done.4.refs_4_
  33.7 7.9 collective-permute-done.1.refs_1_
  44.9 5.1 collective-permute-done.5.refs_5_
  58.4 7.5 collective-permute-done.6.refs_6_
  75.5 9.7 pick_rows.1
  85.8 7.4 rotary_tables.1
  93.8 10.4 %collective-permute-done.7.refs_7_ = bf16[256,768]{1,0:T(8,128)(2,1)} collective-permute-done((bf16[256,768]{1,0:T(8,128)(2,1)}, bf16[256,768]{1,0:T(8,128)(2,1)}, u32[]{:S(2)}, u32[]{:S(2)}) %collective-permute-start.7) | collective-permute-done | bytes 393248 | tf_op jit(solution)/shard_map/ppermute | solution.py:906
  104.3 5.9 place_rows.3.refs_3_.refs_6_
  111.0 21.5 %collective-permute-done.8.refs_1_ = bf16[256,2048]{1,0:T(8,128)(2,1)S(1)} collective-permute-done((bf16[256,2048]{1,0:T(8,128)(2,1)S(1)}, bf16[256,2048]{1,0:T(8,128)(2,1)S(1)}, u32[]{:S(2)}, u32[]{:S(2)}) %collective-permute-start.8) | collective-permute-done | bytes 1048608 | tf_op jit(solution)/shard_map/ppermute | solution.py:860
  134.4 16.4 %norm_project.3 = (bf16[4096,2048]{1,0:T(8,128)(2,1)}, bf16[4096,384]{1,0:T(8,128)(2,1)}, bf16[4096,384]{1,0:T(8,128)(2,1)}) custom-call(s32[8]{0:T(128)} %stack.132.at_ref.map_ref, bf16[2048,2048]{1,0:T(8,128)(2,1)} %refs_0_.1, f32[1,2048]{1,0:T(1,128)} %bitcast.119, f32[1,2048]{1,0:T(1,128)} %bitcast.125, bf16[2048,768]{1,0:T(8,128)(2,1)} %place_rows.3.refs_3_.refs_6_, ...), custom_call_target="tpu_custom_call" | custom-call | flops 6442450944 | bytes 19922944 | tf_op jit(solution)/shard_map/norm_project/pallas_call | solution.py:493
  150.9 10.9 %norm_project.4 = (bf16[4096,2048]{1,0:T(8,128)(2,1)}, bf16[4096,384]{1,0:T(8,128)(2,1)}, bf16[4096,384]{1,0:T(8,128)(2,1)}) custom-call(s32[1]{0:T(128)} %constant.165.clone.1.map_ref, bf16[256,2048]{1,0:T(8,128)(2,1)} %collective-permute-done.11.refs_0_, ...), custom_call_target="tpu_custom_call", output_to_operand_aliasing={{0}: (9, {}), {1}: (10, {}), {2}: (11, {})} | custom-call | flops 3221225472 | bytes 11534336 | tf_op jit(solution)/shard_map/norm_project/pallas_call | solution.py:493
  161.8 11.1 %norm_project.5 = (bf16[4096,2048]{1,0:T(8,128)(2,1)}, bf16[4096,384]{1,0:T(8,128)(2,1)}, bf16[4096,384]{1,0:T(8,128)(2,1)}) custom-call(s32[1]{0:T(128)} %constant.165.clone.1.map_ref, bf16[256,2048]{1,0:T(8,128)(2,1)} %copy-done.35, bf16[256,2048]{1,0:T(8,128)(2,1)} %copy-done.37, ...), custom_call_target="tpu_custom_call", output_to_operand_aliasing={{0}: (9, {}), {1}: (10, {}), {2}: (11, {})} | custom-call | flops 3221225472 | bytes 11534336 | tf_op jit(solution)/shard_map/norm_project/pallas_call | solution.py:493
  172.9 34.0 %attention_forward.3 = (bf16[2048,128]{1,0:T(8,128)(2,1)}, bf16[2048,128]{1,0:T(8,128)(2,1)}, bf16[4096,384]{1,0:T(8,128)(2,1)}, bf16[4096,128]{1,0:T(8,128)(2,1)}, f32[8,4096]{1,0:T(8,128)}) custom-call(s32[32]{0:T(128)} %and_select_fusion.1.slot_ref, s32[6]{0:T(128)} %bitcast.130, bf16[4096,384]{1,0:T(8,128)(2,1)} %get-tuple-element.163.refs_0_, ...), custom_call_target="tpu_custom_call" | custom-call | flops 11453245440 | bytes 10485760 | tf_op jit(solution)/shard_map/attention_forward/pallas_call | solution.py:221
  207.0 34.9 %attention_forward.2 = (bf16[2048,128]{1,0:T(8,128)(2,1)}, bf16[2048,128]{1,0:T(8,128)(2,1)}, bf16[4096,384]{1,0:T(8,128)(2,1)}, bf16[4096,128]{1,0:T(8,128)(2,1)}, f32[8,4096]{1,0:T(8,128)}) custom-call(s32[32]{0:T(128)} %and_select_fusion.1.slot_ref, s32[6]{0:T(128)} %bitcast.131, bf16[4096,384]{1,0:T(8,128)(2,1)} %get-tuple-element.160.refs_0_, ...), custom_call_target="tpu_custom_call" | custom-call | flops 11453245440 | bytes 10485760 | tf_op jit(solution)/shard_map/attention_forward/pallas_call | solution.py:221
  248.6 7.8 collective-permute-done.15.refs_2_
  257.2 8.2 project_out.2
  265.5 9.1 project_out.3
  280.9 18.2 %fusion.39.refs_4_ = f32[2048,1408]{1,0:T(8,128)} fusion(bf16[2048,2048]{1,0:T(8,128)(2,1)S(1)} %bitcast.98, bf16[2048,1408]{0,1:T(8,128)(2,1)} %all-gather.4.cloned.1.call-done), kind=kOutput, calls=%fused_computation.172 | convolution fusion | flops 11811160064 | bytes 25690112 | tf_op jit(solution)/shard_map/dot_general | solution.py:27
  303.9 21.6 %collective-permute-done.23 = bf16[256,2048]{1,0:T(8,128)(2,1)S(1)} collective-permute-done((bf16[256,2048]{1,0:T(8,128)(2,1)S(1)}, bf16[256,2048]{1,0:T(8,128)(2,1)S(1)}, u32[]{:S(2)}, u32[]{:S(2)}) %collective-permute-start.23) | collective-permute-done | bytes 1048608 | tf_op jit(solution)/shard_map/ppermute | solution.py:860
  333.7 24.3 %collective-permute-done.19.refs_1_ = bf16[256,2048]{1,0:T(8,128)(2,1)} collective-permute-done((bf16[256,2048]{1,0:T(8,128)(2,1)S(1)}, bf16[256,2048]{1,0:T(8,128)(2,1)}, u32[]{:S(2)}, u32[]{:S(2)}) %collective-permute-start.19) | collective-permute-done | bytes 1048608 | tf_op jit(solution)/shard_map/ppermute | solution.py:860
  368.8 42.6 %feed_forward.2 = (bf16[2048,2048]{1,0:T(8,128)(2,1)}, bf16[2048,1408]{1,0:T(8,128)(2,1)}, bf16[2048,2816]{1,0:T(8,128)(2,1)}, bf16[512,2048]{1,0:T(8,128)(2,1)}, bf16[512,2048]{1,0:T(8,128)(2,1)}) custom-call(bf16[256,2048]{1,0:T(8,128)(2,1)} %copy-done.40, bf16[256,2048]{1,0:T(8,128)(2,1)} %collective-permute-done.19.refs_1_, ...), custom_call_target="tpu_custom_call" | custom-call | flops 23622320128 | bytes 57147392 | tf_op jit(solution)/shard_map/feed_forward/pallas_call | solution.py:590
  412.6 5.5 collective-permute-done.26
  424.9 42.7 %feed_forward.3 = (bf16[2048,2048]{1,0:T(8,128)(2,1)}, bf16[2048,1408]{1,0:T(8,128)(2,1)}, bf16[2048,2816]{1,0:T(8,128)(2,1)}, bf16[512,2048]{1,0:T(8,128)(2,1)}, bf16[512,2048]{1,0:T(8,128)(2,1)}) custom-call(bf16[256,2048]{1,0:T(8,128)(2,1)} %get-tuple-element.182.refs_0_, ...), custom_call_target="tpu_custom_call", output_to_operand_aliasing={{0}: (6, {}), {1}: (7, {}), {2}: (8, {})} | custom-call | flops 23622320128 | bytes 82837504 | tf_op jit(solution)/shard_map/feed_forward/pallas_call | solution.py:590
  481.1 17.6 %convolution_convert_fusion.3 = bf16[2048,1408]{1,0:T(8,128)(2,1)} fusion(bf16[2048,2048]{1,0:T(8,128)(2,1)S(1)} %bitcast.100, bf16[2048,1408]{1,0:T(8,128)(2,1)} %get-tuple-element.199), kind=kOutput, calls=%fused_computation.4 | convolution fusion | flops 11814043648 | bytes 19922944 | tf_op jit(solution)/shard_map/dot_general | solution.py:27
  498.8 7.1 collective-permute-done.35
  510.7 5.1 fusion.19
  517.9 17.7 %convolution_convert_fusion.1 = bf16[2048,1408]{1,0:T(8,128)(2,1)} fusion(bf16[2048,2048]{1,0:T(8,128)(2,1)} %get-tuple-element.196, bf16[2048,2816]{1,0:T(8,128)(2,1)S(1)} %bitcast.138), kind=kOutput, calls=%fused_computation.2 | convolution fusion | flops 11814043648 | bytes 19922944 | tf_op jit(solution)/shard_map/dot_general | solution.py:27
  535.6 18.5 %convolution_convert_fusion = bf16[2048,2048]{1,0:T(8,128)(2,1)} fusion(bf16[2048,1408]{1,0:T(8,128)(2,1)} %get-tuple-element.199, bf16[2048,1408]{0,1:T(8,128)(2,1)} %all-gather.4.cloned.1.call-done), kind=kOutput, calls=%fused_computation.1 | convolution fusion | flops 11815354368 | bytes 19922944 | tf_op jit(solution)/shard_map/dot_general | solution.py:27
  554.1 19.3 %convolution_convert_fusion.2 = bf16[2048,1408]{1,0:T(8,128)(2,1)} fusion(bf16[2048,2048]{1,0:T(8,128)(2,1)} %get-tuple-element.196, bf16[2048,2816]{1,0:T(8,128)(2,1)} %get-tuple-element.198), kind=kOutput, calls=%fused_computation.3 | convolution fusion | flops 11814043648 | bytes 19922944 | tf_op jit(solution)/shard_map/dot_general | solution.py:27
  580.3 7.8 project_out_back.3
  588.1 7.5 project_out_back.2
  601.9 9.3 collective-permute-done.39.refs_2_
  628.8 44.5 %attention_backward.2 = (bf16[4096,384]{1,0:T(8,128)(2,1)}, f32[8,384]{1,0:T(8,128)}) custom-call(s32[32]{0:T(128)} %and_select_fusion.1.slot_ref, s32[6]{0:T(128)} %bitcast.132, bf16[1024,256]{1,0:T(8,128)(2,1)} %get-tuple-element.227.refs_0_, bf16[1024,256]{1,0:T(8,128)(2,1)} %get-tuple-element.228.refs_1_, ...), custom_call_target="tpu_custom_call" | custom-call | flops 28633112576 | bytes 10485760 | tf_op jit(solution)/shard_map/attention_backward/pallas_call | solution.py:383
  682.1 44.1 %attention_backward.3 = (bf16[4096,384]{1,0:T(8,128)(2,1)}, f32[8,384]{1,0:T(8,128)}) custom-call(s32[32]{0:T(128)} %and_select_fusion.1.slot_ref, s32[6]{0:T(128)} %bitcast.133, bf16[1024,256]{1,0:T(8,128)(2,1)} %get-tuple-element.227.refs_0_, bf16[1024,256]{1,0:T(8,128)(2,1)} %get-tuple-element.228.refs_1_, ...), custom_call_target="tpu_custom_call" | custom-call | flops 28633112576 | bytes 10485760 | tf_op jit(solution)/shard_map/attention_backward/pallas_call | solution.py:383
  729.4 14.0 %convolution_convert_fusion.5 = bf16[2048,384]{1,0:T(8,128)(2,1)} fusion(bf16[4096,2048]{1,0:T(8,128)(2,1)} %get-tuple-element.241, bf16[4096,384]{1,0:T(8,128)(2,1)S(1)} %copy-done.41), kind=kOutput, calls=%fused_computation.36 | convolution fusion | flops 6443237376 | bytes 21495808 | tf_op jit(solution)/shard_map/dot_general | solution.py:27
  747.1 10.3 %convolution_convert_fusion.4 = bf16[2048,384]{1,0:T(8,128)(2,1)} fusion(bf16[4096,2048]{1,0:T(8,128)(2,1)S(1)} %bitcast.96, bf16[4096,384]{1,0:T(8,128)(2,1)S(1)} %copy-done.42), kind=kOutput, calls=%fused_computation.35 | convolution fusion | flops 6443237376 | bytes 21495808 | tf_op jit(solution)/shard_map/dot_general | solution.py:27
  763.3 13.7 %project_back.2 = (bf16[512,2048]{1,0:T(8,128)(2,1)}, bf16[512,2048]{1,0:T(8,128)(2,1)}) custom-call(bf16[4096,384]{1,0:T(8,128)(2,1)} %get-tuple-element.222.refs_0_, bf16[4096,384]{1,0:T(8,128)(2,1)} %get-tuple-element.234.refs_1_, bf16[2048,384]{1,0:T(8,128)(2,1)} %collective-permute-done.48.refs_2_, bf16[1024,384]{1,0:T(8,128)(2,1)} %copy-done.67, ...), custom_call_target="tpu_custom_call" | custom-call | flops 6442450944 | bytes 19136512 | tf_op jit(solution)/shard_map/project_back/pallas_call | solution.py:590
  785.9 14.2 %project_back.3 = (bf16[512,2048]{1,0:T(8,128)(2,1)}, bf16[512,2048]{1,0:T(8,128)(2,1)}) custom-call(bf16[4096,384]{1,0:T(8,128)(2,1)} %get-tuple-element.222.refs_0_, bf16[4096,384]{1,0:T(8,128)(2,1)} %get-tuple-element.234.refs_1_, bf16[2048,384]{1,0:T(8,128)(2,1)} %collective-permute-done.48.refs_2_, bf16[1024,384]{1,0:T(8,128)(2,1)} %copy-done.66, ...), custom_call_target="tpu_custom_call" | custom-call | flops 6442450944 | bytes 19136512 | tf_op jit(solution)/shard_map/project_back/pallas_call | solution.py:590
  800.1 9.2 collective-permute-done.52
  829.5 16.9 %collective-permute-done.70 = bf16[512,512]{1,0:T(8,128)(2,1)} collective-permute-done((bf16[512,512]{1,0:T(8,128)(2,1)}, bf16[512,512]{1,0:T(8,128)(2,1)}, u32[]{:S(2)}, u32[]{:S(2)}) %collective-permute-start.70) | collective-permute-done | bytes 524320 | tf_op jit(solution)/shard_map/ppermute | solution.py:906
  847.8 15.4 %collective-permute-done.66 = bf16[512,768]{1,0:T(8,128)(2,1)} collective-permute-done((bf16[512,768]{1,0:T(8,128)(2,1)}, bf16[512,768]{1,0:T(8,128)(2,1)}, u32[]{:S(2)}, u32[]{:S(2)}) %collective-permute-start.66) | collective-permute-done | bytes 786464 | tf_op jit(solution)/shard_map/ppermute | solution.py:906
  868.0 7.8 place_rows.4
  896.9 6.0 collective-permute-done.72
  902.9 8.4 collective-permute-done.58.refs_5_
  912.5 8.3 collective-permute-done.68
  920.8 11.5 %collective-permute-done.54.refs_1_ = bf16[256,2048]{1,0:T(8,128)(2,1)} collective-permute-done((bf16[256,2048]{1,0:T(8,128)(2,1)}, bf16[256,2048]{1,0:T(8,128)(2,1)}, u32[]{:S(2)}, u32[]{:S(2)}) %collective-permute-start.54) | collective-permute-done | bytes 1048608 | tf_op jit(solution)/shard_map/ppermute | solution.py:860
  938.0 5.8 collective-permute-done.62
  975.9 8.7 place_rows.5
  (463 shorter events, 255.7 us)
Async XLA Ops:
  7.2 237.4 %all-gather.6.cloned.1.call-start = ((), (), s32[]{:S(2)}) async-start(), calls=%async_computation.4 | async-start | bytes 2359296 | tf_op jit(solution)/shard_map/all_gather | solution.py:1052
  9.0 247.4 %all-gather.4.cloned.1.call-start = ((), (), s32[]{:S(2)}) async-start(), calls=%async_computation.3 | async-start | bytes 6488064 | tf_op jit(solution)/shard_map/all_gather | solution.py:1054
  23.9 344.8 %all-gather.8.cloned.1.call-start = ((), (), s32[]{:S(2)}) async-start(), calls=%async_computation.5 | async-start | bytes 12976128 | tf_op jit(solution)/shard_map/all_gather | solution.py:1056
  30.2 28.2 %collective-permute-start.11 = (bf16[256,2048]{1,0:T(8,128)(2,1)S(1)}, bf16[256,2048]{1,0:T(8,128)(2,1)}, u32[]{:S(2)}, u32[]{:S(2)}) collective-permute-start(bf16[256,2048]{1,0:T(8,128)(2,1)S(1)} %get-tuple-element.352), channel_id=1, source_target_pairs={{0,4},{4,0},{1,5},{5,1},{2,6},{6,2},{3,7},{7,3},{8,12},{12,8},{9,1... | collective-permute-start | bytes 3145736 | tf_op jit(solution)/shard_map/ppermute | solution.py:906
  32.7 61.1 %collective-permute-start = (bf16[256,2048]{1,0:T(8,128)(2,1)S(1)}, bf16[256,2048]{1,0:T(8,128)(2,1)S(1)}, u32[]{:S(2)}, u32[]{:S(2)}) collective-permute-start(bf16[256,2048]{1,0:T(8,128)(2,1)S(1)} %get-tuple-element.334), channel_id=1, source_target_pairs={{0,4},{4,0},{1,5},{5,1},{2,6},{6,2},{3,7},{7,3},{8,12},{12,8},{9,1... | collective-permute-start | bytes 3145736 | tf_op jit(solution)/shard_map/ppermute | solution.py:906
  65.9 38.3 %collective-permute-start.12 = (bf16[256,2048]{1,0:T(8,128)(2,1)}, bf16[256,2048]{1,0:T(8,128)(2,1)}, u32[]{:S(2)}, u32[]{:S(2)}) collective-permute-start(bf16[256,2048]{1,0:T(8,128)(2,1)} %collective-permute-done.11.refs_0_), channel_id=1, source_target_pairs={{0,2},{1,3},{2,0},{3,1},{4,6},{5,7},{6,4},{7,5},{8,10},{9,11},{10,... | collective-permute-start | bytes 3145736 | tf_op jit(solution)/shard_map/ppermute | solution.py:860
  68.2 25.6 %collective-permute-start.3 = (bf16[256,768]{1,0:T(8,128)(2,1)}, bf16[256,768]{1,0:T(8,128)(2,1)S(1)}, u32[]{:S(2)}, u32[]{:S(2)}) collective-permute-start(bf16[256,768]{1,0:T(8,128)(2,1)} %collective-permute-done.2.refs_2_), channel_id=1, source_target_pairs={{0,24},{8,0},{16,8},{24,16},{1,25},{9,1},{17,9},{25,17},{2,26},{10... | collective-permute-start | bytes 1179656 | tf_op jit(solution)/shard_map/ppermute | solution.py:906
  71.4 32.9 %collective-permute-start.7 = (bf16[256,768]{1,0:T(8,128)(2,1)}, bf16[256,768]{1,0:T(8,128)(2,1)}, u32[]{:S(2)}, u32[]{:S(2)}) collective-permute-start(bf16[256,768]{1,0:T(8,128)(2,1)} %collective-permute-done.6.refs_6_), channel_id=1, source_target_pairs={{0,24},{8,0},{16,8},{24,16},{1,25},{9,1},{17,9},{25,17},{2,26},{10... | collective-permute-start | bytes 1179656 | tf_op jit(solution)/shard_map/ppermute | solution.py:906
  110.2 716.9 %reduce-scatter.4.cloned.1.call-start = ((), (), s32[]{:S(2)}) async-start(), calls=%async_computation.6 | async-start | bytes 6488064 | tf_op jit(solution)/shard_map/reduce_scatter | solution.py:1184
  110.4 40.4 %collective-permute-start.13 = (bf16[256,2048]{1,0:T(8,128)(2,1)}, bf16[256,2048]{1,0:T(8,128)(2,1)}, u32[]{:S(2)}, u32[]{:S(2)}) collective-permute-start(bf16[256,2048]{1,0:T(8,128)(2,1)} %collective-permute-done.11.refs_0_), channel_id=1, source_target_pairs={{0,1},{1,0},{2,3},{3,2},{4,5},{5,4},{6,7},{7,6},{8,9},{9,8},{10,11... | collective-permute-start | bytes 3145736 | tf_op jit(solution)/shard_map/ppermute | solution.py:860
  110.4 40.4 %collective-permute-start.14 = (bf16[256,2048]{1,0:T(8,128)(2,1)}, bf16[256,2048]{1,0:T(8,128)(2,1)}, u32[]{:S(2)}, u32[]{:S(2)}) collective-permute-start(bf16[256,2048]{1,0:T(8,128)(2,1)} %collective-permute-done.12.refs_1_), channel_id=1, source_target_pairs={{0,1},{1,0},{2,3},{3,2},{4,5},{5,4},{6,7},{7,6},{8,9},{9,8},{10,11... | collective-permute-start | bytes 3145736 | tf_op jit(solution)/shard_map/ppermute | solution.py:860
  110.9 50.9 %collective-permute-start.9 = (bf16[256,2048]{1,0:T(8,128)(2,1)S(1)}, bf16[256,2048]{1,0:T(8,128)(2,1)}, u32[]{:S(2)}, u32[]{:S(2)}) collective-permute-start(bf16[256,2048]{1,0:T(8,128)(2,1)S(1)} %collective-permute-done.refs_0_), channel_id=1, source_target_pairs={{0,1},{1,0},{2,3},{3,2},{4,5},{5,4},{6,7},{7,6},{8,9},{9,8},{10,11... | collective-permute-start | bytes 3145736 | tf_op jit(solution)/shard_map/ppermute | solution.py:860
  132.6 29.3 %collective-permute-start.10 = (bf16[256,2048]{1,0:T(8,128)(2,1)S(1)}, bf16[256,2048]{1,0:T(8,128)(2,1)}, u32[]{:S(2)}, u32[]{:S(2)}) collective-permute-start(bf16[256,2048]{1,0:T(8,128)(2,1)S(1)} %collective-permute-done.8.refs_1_), channel_id=1, source_target_pairs={{0,1},{1,0},{2,3},{3,2},{4,5},{5,4},{6,7},{7,6},{8,9},{9,8},{10,11... | collective-permute-start | bytes 3145736 | tf_op jit(solution)/shard_map/ppermute | solution.py:860
  206.9 41.6 %collective-permute-start.16 = (bf16[2048,128]{1,0:T(8,128)(2,1)}, bf16[2048,128]{1,0:T(8,128)(2,1)S(1)}, u32[]{:S(2)}, u32[]{:S(2)}) collective-permute-start(bf16[2048,128]{1,0:T(8,128)(2,1)} %get-tuple-element.165), channel_id=1, source_target_pairs={{0,4},{4,0},{1,5},{5,1},{2,6},{6,2},{3,7},{7,3},{8,12},{12,8},{9,1... | collective-permute-start | bytes 1572872 | tf_op jit(solution)/shard_map/ppermute | solution.py:906
  277.8 26.1 %collective-permute-start.18 = (bf16[256,2048]{1,0:T(8,128)(2,1)S(1)}, bf16[256,2048]{1,0:T(8,128)(2,1)S(1)}, u32[]{:S(2)}, u32[]{:S(2)}) collective-permute-start(bf16[256,2048]{1,0:T(8,128)(2,1)S(1)} %slice.230), channel_id=1, source_target_pairs={{0,2},{1,3},{2,0},{3,1},{4,6},{5,7},{6,4},{7,5},{8,10},{9,11},{10,... | collective-permute-start | bytes 3145736 | tf_op jit(solution)/shard_map/ppermute | solution.py:860
  280.2 45.3 %collective-permute-start.23 = (bf16[256,2048]{1,0:T(8,128)(2,1)S(1)}, bf16[256,2048]{1,0:T(8,128)(2,1)S(1)}, u32[]{:S(2)}, u32[]{:S(2)}) collective-permute-start(bf16[256,2048]{1,0:T(8,128)(2,1)S(1)} %slice.229), channel_id=1, source_target_pairs={{0,2},{1,3},{2,0},{3,1},{4,6},{5,7},{6,4},{7,5},{8,10},{9,11},{10,... | collective-permute-start | bytes 3145736 | tf_op jit(solution)/shard_map/ppermute | solution.py:860
  333.4 24.5 %collective-permute-start.19 = (bf16[256,2048]{1,0:T(8,128)(2,1)S(1)}, bf16[256,2048]{1,0:T(8,128)(2,1)}, u32[]{:S(2)}, u32[]{:S(2)}) collective-permute-start(bf16[256,2048]{1,0:T(8,128)(2,1)S(1)} %get-tuple-element.368.refs_0_), channel_id=1, source_target_pairs={{0,2},{1,3},{2,0},{3,1},{4,6},{5,7},{6,4},{7,5},{8,10},{9,11},{10,... | collective-permute-start | bytes 3145736 | tf_op jit(solution)/shard_map/ppermute | solution.py:860
  333.7 35.0 %collective-permute-start.20 = (bf16[256,2048]{1,0:T(8,128)(2,1)S(1)}, bf16[256,2048]{1,0:T(8,128)(2,1)}, u32[]{:S(2)}, u32[]{:S(2)}) collective-permute-start(bf16[256,2048]{1,0:T(8,128)(2,1)S(1)} %get-tuple-element.368.refs_0_), channel_id=1, source_target_pairs={{0,1},{1,0},{2,3},{3,2},{4,5},{5,4},{6,7},{7,6},{8,9},{9,8},{10,11... | collective-permute-start | bytes 3145736 | tf_op jit(solution)/shard_map/ppermute | solution.py:860
  366.6 44.8 %collective-permute-start.25 = (bf16[1024,768]{0,1:T(8,128)(2,1)}, bf16[1024,768]{0,1:T(8,128)(2,1)}, u32[]{:S(2)}, u32[]{:S(2)}) collective-permute-start(bf16[1024,768]{0,1:T(8,128)(2,1)} %get-tuple-element.356), channel_id=1, source_target_pairs={{0,4},{4,0},{1,5},{5,1},{2,6},{6,2},{3,7},{7,3},{8,12},{12,8},{9,1... | collective-permute-start | bytes 4718600 | tf_op jit(solution)/shard_map/ppermute | solution.py:906
  368.1 43.3 %collective-permute-start.24 = (bf16[256,2048]{1,0:T(8,128)(2,1)}, bf16[256,2048]{1,0:T(8,128)(2,1)}, u32[]{:S(2)}, u32[]{:S(2)}) collective-permute-start(bf16[256,2048]{1,0:T(8,128)(2,1)} %get-tuple-element.182.refs_0_), channel_id=1, source_target_pairs={{0,2},{1,3},{2,0},{3,1},{4,6},{5,7},{6,4},{7,5},{8,10},{9,11},{10,... | collective-permute-start | bytes 3145736 | tf_op jit(solution)/shard_map/ppermute | solution.py:860
  412.1 60.3 %collective-permute-start.33 = (bf16[1024,768]{0,1:T(8,128)(2,1)}, bf16[1024,768]{0,1:T(8,128)(2,1)S(1)}, u32[]{:S(2)}, u32[]{:S(2)}) collective-permute-start(bf16[1024,768]{0,1:T(8,128)(2,1)} %get-tuple-element.191), channel_id=1, source_target_pairs={{0,4},{4,0},{1,5},{5,1},{2,6},{6,2},{3,7},{7,3},{8,12},{12,8},{9,1... | collective-permute-start | bytes 4718600 | tf_op jit(solution)/shard_map/ppermute | solution.py:906
  423.5 44.1 %collective-permute-start.27 = (bf16[256,2048]{1,0:T(8,128)(2,1)}, bf16[256,2048]{1,0:T(8,128)(2,1)}, u32[]{:S(2)}, u32[]{:S(2)}) collective-permute-start(bf16[256,2048]{1,0:T(8,128)(2,1)} %slice.228), channel_id=1, source_target_pairs={{0,2},{1,3},{2,0},{3,1},{4,6},{5,7},{6,4},{7,5},{8,10},{9,11},{10,... | collective-permute-start | bytes 3145736 | tf_op jit(solution)/shard_map/ppermute | solution.py:860
  480.5 25.4 %collective-permute-start.35 = (bf16[256,2048]{1,0:T(8,128)(2,1)}, bf16[256,2048]{1,0:T(8,128)(2,1)S(1)}, u32[]{:S(2)}, u32[]{:S(2)}) collective-permute-start(bf16[256,2048]{1,0:T(8,128)(2,1)} %slice.227), channel_id=1, source_target_pairs={{0,2},{1,3},{2,0},{3,1},{4,6},{5,7},{6,4},{7,5},{8,10},{9,11},{10,... | collective-permute-start | bytes 3145736 | tf_op jit(solution)/shard_map/ppermute | solution.py:860
  498.8 448.0 %reduce-scatter.6.cloned.1.call-start = ((), (), s32[]{:S(2)}) async-start(), calls=%async_computation.7 | async-start | bytes 6488064 | tf_op jit(solution)/shard_map/reduce_scatter | solution.py:1185
  515.8 57.7 %collective-permute-start.36 = (bf16[256,2048]{1,0:T(8,128)(2,1)S(1)}, bf16[256,2048]{1,0:T(8,128)(2,1)}, u32[]{:S(2)}, u32[]{:S(2)}) collective-permute-start(bf16[256,2048]{1,0:T(8,128)(2,1)S(1)} %get-tuple-element.200.refs_0_), channel_id=1, source_target_pairs={{0,2},{1,3},{2,0},{3,1},{4,6},{5,7},{6,4},{7,5},{8,10},{9,11},{10,... | collective-permute-start | bytes 3145736 | tf_op jit(solution)/shard_map/ppermute | solution.py:860
  516.5 57.6 %collective-permute-start.28 = (bf16[256,2048]{1,0:T(8,128)(2,1)}, bf16[256,2048]{1,0:T(8,128)(2,1)}, u32[]{:S(2)}, u32[]{:S(2)}) collective-permute-start(bf16[256,2048]{1,0:T(8,128)(2,1)} %get-tuple-element.350.refs_0_), channel_id=1, source_target_pairs={{0,2},{1,3},{2,0},{3,1},{4,6},{5,7},{6,4},{7,5},{8,10},{9,11},{10,... | collective-permute-start | bytes 3145736 | tf_op jit(solution)/shard_map/ppermute | solution.py:860
  600.2 346.5 %reduce-scatter.8.cloned.1.call-start = ((), (), s32[]{:S(2)}) async-start(), calls=%async_computation.8 | async-start | bytes 6488064 | tf_op jit(solution)/shard_map/reduce_scatter | solution.py:1227
  600.5 24.5 %collective-permute-start.40 = (bf16[1024,256]{1,0:T(8,128)(2,1)}, bf16[1024,256]{1,0:T(8,128)(2,1)S(1)}, u32[]{:S(2)}, u32[]{:S(2)}) collective-permute-start(bf16[1024,256]{1,0:T(8,128)(2,1)} %get-tuple-element.204), channel_id=1, source_target_pairs={{0,4},{4,0},{1,5},{5,1},{2,6},{6,2},{3,7},{7,3},{8,12},{12,8},{9,1... | collective-permute-start | bytes 1572872 | tf_op jit(solution)/shard_map/ppermute | solution.py:906
  626.3 50.0 %collective-permute-start.44 = (bf16[256,2048]{1,0:T(8,128)(2,1)}, bf16[256,2048]{1,0:T(8,128)(2,1)}, u32[]{:S(2)}, u32[]{:S(2)}) collective-permute-start(bf16[256,2048]{1,0:T(8,128)(2,1)} %slice.225), channel_id=1, source_target_pairs={{0,2},{1,3},{2,0},{3,1},{4,6},{5,7},{6,4},{7,5},{8,10},{9,11},{10,... | collective-permute-start | bytes 3145736 | tf_op jit(solution)/shard_map/ppermute | solution.py:860
  627.3 51.7 %collective-permute-start.43 = (bf16[256,2048]{1,0:T(8,128)(2,1)S(1)}, bf16[256,2048]{1,0:T(8,128)(2,1)}, u32[]{:S(2)}, u32[]{:S(2)}) collective-permute-start(bf16[256,2048]{1,0:T(8,128)(2,1)S(1)} %slice.226), channel_id=1, source_target_pairs={{0,2},{1,3},{2,0},{3,1},{4,6},{5,7},{6,4},{7,5},{8,10},{9,11},{10,... | collective-permute-start | bytes 3145736 | tf_op jit(solution)/shard_map/ppermute | solution.py:860
  676.1 51.8 %collective-permute-start.48 = (bf16[2048,384]{1,0:T(8,128)(2,1)}, bf16[2048,384]{1,0:T(8,128)(2,1)}, u32[]{:S(2)}, u32[]{:S(2)}) collective-permute-start(bf16[2048,384]{1,0:T(8,128)(2,1)} %slice.146), channel_id=1, source_target_pairs={{0,4},{4,0},{1,5},{5,1},{2,6},{6,2},{3,7},{7,3},{8,12},{12,8},{9,1... | collective-permute-start | bytes 4718600 | tf_op jit(solution)/shard_map/ppermute | solution.py:906
  681.5 46.5 %collective-permute-start.45 = (bf16[512,2048]{1,0:T(8,128)(2,1)S(1)}, bf16[512,2048]{1,0:T(8,128)(2,1)}, u32[]{:S(2)}, u32[]{:S(2)}) collective-permute-start(bf16[512,2048]{1,0:T(8,128)(2,1)S(1)} %constant_dynamic-update-slice_fusion.refs_0_), channel_id=1, source_target_pairs={{0,2},{1,3},{2,0},{3,1},{4,6},{5,7},{6,4},{7,5},{8,10},{9,11},{10,... | collective-permute-start | bytes 6291464 | tf_op jit(solution)/shard_map/ppermute | solution.py:860
  784.1 25.3 %collective-permute-start.52 = (bf16[256,2048]{1,0:T(8,128)(2,1)S(1)}, bf16[256,2048]{1,0:T(8,128)(2,1)S(1)}, u32[]{:S(2)}, u32[]{:S(2)}) collective-permute-start(bf16[256,2048]{1,0:T(8,128)(2,1)S(1)} %slice.224), channel_id=1, source_target_pairs={{0,2},{1,3},{2,0},{3,1},{4,6},{5,7},{6,4},{7,5},{8,10},{9,11},{10,... | collective-permute-start | bytes 3145736 | tf_op jit(solution)/shard_map/ppermute | solution.py:860
  815.8 30.6 %collective-permute-start.70 = (bf16[512,512]{1,0:T(8,128)(2,1)}, bf16[512,512]{1,0:T(8,128)(2,1)}, u32[]{:S(2)}, u32[]{:S(2)}) collective-permute-start(bf16[512,512]{1,0:T(8,128)(2,1)} %constant_dynamic-slice_fusion), channel_id=1, source_target_pairs={{0,24},{8,0},{16,8},{24,16},{1,25},{9,1},{17,9},{25,17},{2,26},{10... | collective-permute-start | bytes 1572872 | tf_op jit(solution)/shard_map/ppermute | solution.py:906
  816.1 51.9 %collective-permute-start.46 = (bf16[512,2048]{1,0:T(8,128)(2,1)}, bf16[512,2048]{1,0:T(8,128)(2,1)}, u32[]{:S(2)}, u32[]{:S(2)}) collective-permute-start(bf16[512,2048]{1,0:T(8,128)(2,1)} %copy-done.22), channel_id=1, source_target_pairs={{0,1},{1,0},{2,3},{3,2},{4,5},{5,4},{6,7},{7,6},{8,9},{9,8},{10,11... | collective-permute-start | bytes 6291464 | tf_op jit(solution)/shard_map/ppermute | solution.py:860
  816.4 51.6 %collective-permute-start.47 = (bf16[512,2048]{1,0:T(8,128)(2,1)}, bf16[512,2048]{1,0:T(8,128)(2,1)}, u32[]{:S(2)}, u32[]{:S(2)}) collective-permute-start(bf16[512,2048]{1,0:T(8,128)(2,1)} %collective-permute-done.45.refs_1_), channel_id=1, source_target_pairs={{0,1},{1,0},{2,3},{3,2},{4,5},{5,4},{6,7},{7,6},{8,9},{9,8},{10,11... | collective-permute-start | bytes 6291464 | tf_op jit(solution)/shard_map/ppermute | solution.py:860
  819.5 43.7 %collective-permute-start.66 = (bf16[512,768]{1,0:T(8,128)(2,1)}, bf16[512,768]{1,0:T(8,128)(2,1)}, u32[]{:S(2)}, u32[]{:S(2)}) collective-permute-start(bf16[512,768]{1,0:T(8,128)(2,1)} %constant_dynamic-slice_fusion.2), channel_id=1, source_target_pairs={{0,24},{8,0},{16,8},{24,16},{1,25},{9,1},{17,9},{25,17},{2,26},{10... | collective-permute-start | bytes 2359304 | tf_op jit(solution)/shard_map/ppermute | solution.py:906
  826.1 49.7 %collective-permute-start.57 = (bf16[256,2048]{1,0:T(8,128)(2,1)}, bf16[256,2048]{1,0:T(8,128)(2,1)}, u32[]{:S(2)}, u32[]{:S(2)}) collective-permute-start(bf16[256,2048]{1,0:T(8,128)(2,1)} %slice.223), channel_id=1, source_target_pairs={{0,2},{1,3},{2,0},{3,1},{4,6},{5,7},{6,4},{7,5},{8,10},{9,11},{10,... | collective-permute-start | bytes 3145736 | tf_op jit(solution)/shard_map/ppermute | solution.py:860
  847.8 39.1 %collective-permute-start.71 = (bf16[512,512]{1,0:T(8,128)(2,1)S(1)}, bf16[512,512]{1,0:T(8,128)(2,1)}, u32[]{:S(2)}, u32[]{:S(2)}) collective-permute-start(bf16[512,512]{1,0:T(8,128)(2,1)S(1)} %add_convert_fusion.11), channel_id=1, source_target_pairs={{0,24},{8,0},{16,8},{24,16},{1,25},{9,1},{17,9},{25,17},{2,26},{10... | collective-permute-start | bytes 1572872 | tf_op jit(solution)/shard_map/ppermute | solution.py:906
  865.7 25.7 %collective-permute-start.67 = (bf16[512,768]{1,0:T(8,128)(2,1)}, bf16[512,768]{1,0:T(8,128)(2,1)}, u32[]{:S(2)}, u32[]{:S(2)}) collective-permute-start(bf16[512,768]{1,0:T(8,128)(2,1)} %add_convert_fusion.9), channel_id=1, source_target_pairs={{0,24},{8,0},{16,8},{24,16},{1,25},{9,1},{17,9},{25,17},{2,26},{10... | collective-permute-start | bytes 2359304 | tf_op jit(solution)/shard_map/ppermute | solution.py:906
  885.1 26.3 %collective-permute-start.58 = (bf16[256,2048]{1,0:T(8,128)(2,1)S(1)}, bf16[256,2048]{1,0:T(8,128)(2,1)}, u32[]{:S(2)}, u32[]{:S(2)}) collective-permute-start(bf16[256,2048]{1,0:T(8,128)(2,1)S(1)} %get-tuple-element.257.refs_4_), channel_id=1, source_target_pairs={{0,2},{1,3},{2,0},{3,1},{4,6},{5,7},{6,4},{7,5},{8,10},{9,11},{10,... | collective-permute-start | bytes 3145736 | tf_op jit(solution)/shard_map/ppermute | solution.py:860
  886.8 58.4 %collective-permute-start.59 = (bf16[256,2048]{1,0:T(8,128)(2,1)S(1)}, bf16[256,2048]{1,0:T(8,128)(2,1)S(1)}, u32[]{:S(2)}, u32[]{:S(2)}) collective-permute-start(bf16[256,2048]{1,0:T(8,128)(2,1)S(1)} %get-tuple-element.257.refs_4_), channel_id=1, source_target_pairs={{0,1},{1,0},{2,3},{3,2},{4,5},{5,4},{6,7},{7,6},{8,9},{9,8},{10,11... | collective-permute-start | bytes 3145736 | tf_op jit(solution)/shard_map/ppermute | solution.py:860
  892.7 28.1 %collective-permute-start.68 = (bf16[512,768]{1,0:T(8,128)(2,1)S(1)}, bf16[512,768]{1,0:T(8,128)(2,1)S(1)}, u32[]{:S(2)}, u32[]{:S(2)}) collective-permute-start(bf16[512,768]{1,0:T(8,128)(2,1)S(1)} %add_convert_fusion.8), channel_id=1, source_target_pairs={{0,24},{8,0},{16,8},{24,16},{1,25},{9,1},{17,9},{25,17},{2,26},{10... | collective-permute-start | bytes 2359304 | tf_op jit(solution)/shard_map/ppermute | solution.py:906
  895.1 37.2 %collective-permute-start.54 = (bf16[256,2048]{1,0:T(8,128)(2,1)}, bf16[256,2048]{1,0:T(8,128)(2,1)}, u32[]{:S(2)}, u32[]{:S(2)}) collective-permute-start(bf16[256,2048]{1,0:T(8,128)(2,1)} %get-tuple-element.344.refs_0_), channel_id=1, source_target_pairs={{0,2},{1,3},{2,0},{3,1},{4,6},{5,7},{6,4},{7,5},{8,10},{9,11},{10,... | collective-permute-start | bytes 3145736 | tf_op jit(solution)/shard_map/ppermute | solution.py:860
  902.9 72.9 %collective-permute-start.55 = (bf16[256,2048]{1,0:T(8,128)(2,1)}, bf16[256,2048]{1,0:T(8,128)(2,1)}, u32[]{:S(2)}, u32[]{:S(2)}) collective-permute-start(bf16[256,2048]{1,0:T(8,128)(2,1)} %get-tuple-element.344.refs_0_), channel_id=1, source_target_pairs={{0,1},{1,0},{2,3},{3,2},{4,5},{5,4},{6,7},{7,6},{8,9},{9,8},{10,11... | collective-permute-start | bytes 3145736 | tf_op jit(solution)/shard_map/ppermute | solution.py:860
  911.3 37.0 %collective-permute-start.60 = (bf16[256,2048]{1,0:T(8,128)(2,1)}, bf16[256,2048]{1,0:T(8,128)(2,1)}, u32[]{:S(2)}, u32[]{:S(2)}) collective-permute-start(bf16[256,2048]{1,0:T(8,128)(2,1)} %collective-permute-done.58.refs_5_), channel_id=1, source_target_pairs={{0,1},{1,0},{2,3},{3,2},{4,5},{5,4},{6,7},{7,6},{8,9},{9,8},{10,11... | collective-permute-start | bytes 3145736 | tf_op jit(solution)/shard_map/ppermute | solution.py:860
  933.9 41.9 %collective-permute-start.56 = (bf16[256,2048]{1,0:T(8,128)(2,1)}, bf16[256,2048]{1,0:T(8,128)(2,1)}, u32[]{:S(2)}, u32[]{:S(2)}) collective-permute-start(bf16[256,2048]{1,0:T(8,128)(2,1)} %collective-permute-done.54.refs_1_), channel_id=1, source_target_pairs={{0,1},{1,0},{2,3},{3,2},{4,5},{5,4},{6,7},{7,6},{8,9},{9,8},{10,11... | collective-permute-start | bytes 3145736 | tf_op jit(solution)/shard_map/ppermute | solution.py:860
  955.8 28.8 %collective-permute-start.65 = (f32[112,128]{1,0:T(8,128)S(1)}, f32[112,128]{1,0:T(8,128)S(1)}, u32[]{:S(2)}, u32[]{:S(2)}) collective-permute-start(f32[112,128]{1,0:T(8,128)S(1)} %add.466), channel_id=1, source_target_pairs={{0,2},{1,3},{2,0},{3,1},{4,6},{5,7},{6,4},{7,5},{8,10},{9,11},{10,... | collective-permute-start | bytes 172040 | tf_op jit(solution)/shard_map/ppermute | solution.py:860
  (119 other events, 1581.7 us)
Sparse Core Ops, SparseCore 0:
  10.1 94.0 all-gather.5
  106.3 94.5 all-gather.3
  203.7 161.8 all-gather.7
  498.9 108.7 reduce-scatter.3
  611.2 123.3 reduce-scatter.5
  777.2 167.3 reduce-scatter.7

commit v4 on v2

--- a/solution.py
+++ b/solution.py
@@ -890,8 +890,10 @@
     return pieces
 
 
-def butterfly(values):
+def butterfly(values, after):
     for axis in ("ctx", "dp", "tensor"):
+        if axis == "tensor":
+            values, _ = lax.optimization_barrier((values, after))
         for bit in range(lax.axis_size(axis).bit_length() - 1):
             values = values + swap_bit(values, axis, bit)
     return values
@@ -1273,12 +1275,9 @@
     )
     small = [d_gain_one, d_shift_one, d_gain_two, d_shift_two, bias_slots.reshape(-1)]
     small, _ = lax.optimization_barrier(
-        (
-            jnp.concatenate(small).reshape(-1, 128),
-            [items[: n_tensor // 2] for items in token_pieces],
-        )
-    )
-    small = butterfly(small).reshape(-1)
+        (jnp.concatenate(small).reshape(-1, 128), token_pieces[0][: n_tensor // 2])
+    )
+    small = butterfly(small, token_pieces[-1][: n_tensor // 2]).reshape(-1)
     norms = [small[index * features : (index + 1) * features] for index in range(4)]
     bias_sum = take_block(small[4 * features :].reshape(n_tensor, -1), mine, 1, 0)
     bias_sum = (

time: 992 us -> 987 us (level)
  starting transfers between devices: 74.4 us -> 53.8 us
  waiting for transfers between devices: 251 us -> 267 us
    ppermute x26, waiting for transfers between devices: 114 us -> 135 us  [shift_over(): lax.ppermute(values, axis, [(i, (i - shift) % size) for i in range(size)])]
    ppermute x26, starting transfers between devices: 49.3 us -> 30.8 us  [shift_over(): lax.ppermute(values, axis, [(i, (i - shift) % size) for i in range(size)])]
    unnamed x183 -> x185, local copies, waits for them, and re-layouts: 26.7 us -> 30.1 us
  transfers between devices with their start and end apart: 79 -> 79, of which waited for: 27 -> 29; matrix products, arithmetic and copies ran while one was open for 25% -> 24% of each run, Pallas kernels for 39% -> 39%
where the time goes in v4:
time: 987 us; the launch traced here: 980 us
  Pallas kernels  385 us (39%)
  waiting for transfers between devices  267 us (27%)
  matrix products  116 us (12%)
  other arithmetic  73.8 us (7%)
  local copies, waits for them, and re-layouts  68.5 us (7%)
  starting transfers between devices  53.8 us (5%)
  between operations  15.9 us (2%)
    pallas_call x8, Pallas kernels, matmul_call(): pl.pallas_call(kernel, name=name, grid=(2,), in_specs=in_specs, out_specs...  145 us
    ppermute x26, waiting for transfers between devices, shift_over(): lax.ppermute(values, axis, [(i, (i - shift) % size) for i in range(size)])  135 us
    ppermute x48, waiting for transfers between devices, swap_bit(): return lax.ppermute(values, axis, [(i, i ^ 1 << bit) for i in range(size)])  119 us
    dot_general x8, matrix products, dot_f32(): lax.dot_general(left, right, (((left_dim,), (right_dim,)), ((), ())), pre...  116 us
    pallas_call x2, Pallas kernels, attend_back(): pl.pallas_call(kernel, name='attention_backward', out_shape=[jax.ShapeDty...  92 us
    pallas_call x2, Pallas kernels, attend(): pl.pallas_call(kernel, name='attention_forward', out_shape=[jax.ShapeDtyp...  70.8 us
    pallas_call x3, Pallas kernels, project(): pl.pallas_call(functools.partial(project_kernel, count, groups, slab), na...  38.4 us
    ppermute x26, starting transfers between devices, shift_over(): lax.ppermute(values, axis, [(i, (i - shift) % size) for i in range(size)])  30.8 us
  transfers between devices with their start and end apart: 79, of which 29 were waited for; matrix products, arithmetic and copies ran while one was open for 24% of the time, Pallas kernels for 39%

profile of v4, /device:TPU:0, one launch (start us, length us, event | category | flops | bytes accessed | tf_op | source)
XLA Modules:
  0.0 979.7 jit_solution(11913746835074078372)
XLA Ops:
  14.1 9.9 %collective-permute-done.3.refs_4_ = bf16[256,768]{1,0:T(8,128)(2,1)S(1)} collective-permute-done((bf16[256,768]{1,0:T(8,128)(2,1)S(1)}, bf16[256,768]{1,0:T(8,128)(2,1)S(1)}, u32[]{:S(2)}, u32[]{:S(2)}) %collective-permute-start.3) | collective-permute-done | bytes 393248 | tf_op jit(solution)/shard_map/ppermute | solution.py:904
  33.8 7.8 collective-permute-done.1.refs_1_
  44.9 5.1 collective-permute-done.4.refs_5_
  58.5 21.1 %collective-permute-done.refs_0_ = bf16[256,2048]{1,0:T(8,128)(2,1)S(1)} collective-permute-done((bf16[256,2048]{1,0:T(8,128)(2,1)S(1)}, bf16[256,2048]{1,0:T(8,128)(2,1)S(1)}, u32[]{:S(2)}, u32[]{:S(2)}) %collective-permute-start) | collective-permute-done | bytes 1048608 | tf_op jit(solution)/shard_map/ppermute | solution.py:904
  85.0 9.7 pick_rows.1
  95.3 7.4 rotary_tables.1
  103.3 4.9 collective-permute-done.10.refs_7_
  108.3 5.9 place_rows.3.refs_3_.refs_6_
  117.2 16.5 %norm_project.3 = (bf16[4096,2048]{1,0:T(8,128)(2,1)}, bf16[4096,384]{1,0:T(8,128)(2,1)}, bf16[4096,384]{1,0:T(8,128)(2,1)}) custom-call(s32[8]{0:T(128)} %stack.118.at_ref.map_ref, bf16[2048,2048]{1,0:T(8,128)(2,1)} %refs_0_.1, f32[1,2048]{1,0:T(1,128)} %bitcast.115, f32[1,2048]{1,0:T(1,128)} %bitcast.121, bf16[2048,768]{1,0:T(8,128)(2,1)} %place_rows.3.refs_3_.refs_6_, ...), custom_call_target="tpu_custom_call" | custom-call | flops 6442450944 | bytes 19922944 | tf_op jit(solution)/shard_map/norm_project/pallas_call | solution.py:493
  133.7 10.8 %norm_project.4 = (bf16[4096,2048]{1,0:T(8,128)(2,1)}, bf16[4096,384]{1,0:T(8,128)(2,1)}, bf16[4096,384]{1,0:T(8,128)(2,1)}) custom-call(s32[1]{0:T(128)} %constant.165.clone.1.map_ref, bf16[256,2048]{1,0:T(8,128)(2,1)} %collective-permute-done.11.refs_0_, ...), custom_call_target="tpu_custom_call", output_to_operand_aliasing={{0}: (9, {}), {1}: (10, {}), {2}: (11, {})} | custom-call | flops 3221225472 | bytes 11534336 | tf_op jit(solution)/shard_map/norm_project/pallas_call | solution.py:493
  145.5 11.0 %norm_project.5 = (bf16[4096,2048]{1,0:T(8,128)(2,1)}, bf16[4096,384]{1,0:T(8,128)(2,1)}, bf16[4096,384]{1,0:T(8,128)(2,1)}) custom-call(s32[1]{0:T(128)} %constant.165.clone.1.map_ref, bf16[256,2048]{1,0:T(8,128)(2,1)} %copy-done.34, bf16[256,2048]{1,0:T(8,128)(2,1)} %collective-permute-done.6.refs_1_, ...), custom_call_target="tpu_custom_call", output_to_operand_aliasing={{0}: (9, {}), {1}: (10, {}), {2}: (11, {})} | custom-call | flops 3221225472 | bytes 11534336 | tf_op jit(solution)/shard_map/norm_project/pallas_call | solution.py:493
  156.6 35.3 %attention_forward.3 = (bf16[2048,128]{1,0:T(8,128)(2,1)}, bf16[2048,128]{1,0:T(8,128)(2,1)}, bf16[4096,384]{1,0:T(8,128)(2,1)}, bf16[4096,128]{1,0:T(8,128)(2,1)}, f32[8,4096]{1,0:T(8,128)}) custom-call(s32[32]{0:T(128)} %and_select_fusion.1.slot_ref, s32[6]{0:T(128)} %bitcast.126, bf16[4096,384]{1,0:T(8,128)(2,1)} %get-tuple-element.162.refs_0_, ...), custom_call_target="tpu_custom_call" | custom-call | flops 11453245440 | bytes 10485760 | tf_op jit(solution)/shard_map/attention_forward/pallas_call | solution.py:221
  193.5 35.5 %attention_forward.2 = (bf16[2048,128]{1,0:T(8,128)(2,1)}, bf16[2048,128]{1,0:T(8,128)(2,1)}, bf16[4096,384]{1,0:T(8,128)(2,1)}, bf16[4096,128]{1,0:T(8,128)(2,1)}, f32[8,4096]{1,0:T(8,128)}) custom-call(s32[32]{0:T(128)} %and_select_fusion.1.slot_ref, s32[6]{0:T(128)} %bitcast.127, bf16[4096,384]{1,0:T(8,128)(2,1)} %get-tuple-element.159.refs_0_, ...), custom_call_target="tpu_custom_call" | custom-call | flops 11453245440 | bytes 10485760 | tf_op jit(solution)/shard_map/attention_forward/pallas_call | solution.py:221
  234.2 8.7 collective-permute-done.15.refs_2_
  243.7 8.2 project_out.2
  252.0 8.3 project_out.3
  267.4 18.6 %fusion.37.refs_4_ = f32[2048,1408]{1,0:T(8,128)} fusion(bf16[2048,2048]{1,0:T(8,128)(2,1)S(1)} %bitcast.96, bf16[2048,1408]{0,1:T(8,128)(2,1)} %all-gather.4.cloned.1.call-done), kind=kOutput, calls=%fused_computation.168 | convolution fusion | flops 11811160064 | bytes 25690112 | tf_op jit(solution)/shard_map/dot_general | solution.py:27
  289.5 21.7 %collective-permute-done.23 = bf16[256,2048]{1,0:T(8,128)(2,1)S(1)} collective-permute-done((bf16[256,2048]{1,0:T(8,128)(2,1)S(1)}, bf16[256,2048]{1,0:T(8,128)(2,1)S(1)}, u32[]{:S(2)}, u32[]{:S(2)}) %collective-permute-start.23) | collective-permute-done | bytes 1048608 | tf_op jit(solution)/shard_map/ppermute | solution.py:860
  320.5 23.1 %collective-permute-done.19.refs_1_ = bf16[256,2048]{1,0:T(8,128)(2,1)} collective-permute-done((bf16[256,2048]{1,0:T(8,128)(2,1)S(1)}, bf16[256,2048]{1,0:T(8,128)(2,1)}, u32[]{:S(2)}, u32[]{:S(2)}) %collective-permute-start.19) | collective-permute-done | bytes 1048608 | tf_op jit(solution)/shard_map/ppermute | solution.py:860
  354.4 12.7 %all-gather.8.cloned.1.call-done.refs_5_ = bf16[2048,2816]{1,0:T(8,128)(2,1)} async-done(((bf16[256,2816]{1,0:T(8,128)(2,1)}), bf16[2048,2816]{1,0:T(8,128)(2,1)}) %all-gather.8.cloned.1.call-update) | async-done | bytes 11534352 | tf_op jit(solution)/shard_map/all_gather | solution.py:1050
  367.1 42.6 %feed_forward.2 = (bf16[2048,2048]{1,0:T(8,128)(2,1)}, bf16[2048,1408]{1,0:T(8,128)(2,1)}, bf16[2048,2816]{1,0:T(8,128)(2,1)}, bf16[512,2048]{1,0:T(8,128)(2,1)}, bf16[512,2048]{1,0:T(8,128)(2,1)}) custom-call(bf16[256,2048]{1,0:T(8,128)(2,1)} %copy-done.39, bf16[256,2048]{1,0:T(8,128)(2,1)} %collective-permute-done.19.refs_1_, ...), custom_call_target="tpu_custom_call" | custom-call | flops 23622320128 | bytes 57147392 | tf_op jit(solution)/shard_map/feed_forward/pallas_call | solution.py:590
  410.9 5.4 collective-permute-done.26
  423.3 42.9 %feed_forward.3 = (bf16[2048,2048]{1,0:T(8,128)(2,1)}, bf16[2048,1408]{1,0:T(8,128)(2,1)}, bf16[2048,2816]{1,0:T(8,128)(2,1)}, bf16[512,2048]{1,0:T(8,128)(2,1)}, bf16[512,2048]{1,0:T(8,128)(2,1)}) custom-call(bf16[256,2048]{1,0:T(8,128)(2,1)} %get-tuple-element.181.refs_0_, ...), custom_call_target="tpu_custom_call", output_to_operand_aliasing={{0}: (6, {}), {1}: (7, {}), {2}: (8, {})} | custom-call | flops 23622320128 | bytes 82837504 | tf_op jit(solution)/shard_map/feed_forward/pallas_call | solution.py:590
  479.5 17.4 %convolution_convert_fusion.2 = bf16[2048,1408]{1,0:T(8,128)(2,1)} fusion(bf16[2048,2048]{1,0:T(8,128)(2,1)S(1)} %bitcast.98, bf16[2048,1408]{1,0:T(8,128)(2,1)} %get-tuple-element.198), kind=kOutput, calls=%fused_computation.3 | convolution fusion | flops 11814043648 | bytes 19922944 | tf_op jit(solution)/shard_map/dot_general | solution.py:27
  497.0 7.4 collective-permute-done.35
  509.1 5.1 fusion.17
  516.3 29.2 %convolution_convert_fusion = bf16[2048,2816]{1,0:T(8,128)(2,1)} fusion(bf16[2048,2048]{1,0:T(8,128)(2,1)} %get-tuple-element.195, bf16[2048,2816]{1,0:T(8,128)(2,1)S(1)} %bitcast.134), kind=kOutput, calls=%fused_computation.1 | convolution fusion | flops 23628087296 | bytes 31457280 | tf_op jit(solution)/shard_map/dot_general | solution.py:27
  545.6 17.0 %convolution_convert_fusion.1 = bf16[2048,2048]{1,0:T(8,128)(2,1)S(1)} fusion(bf16[2048,1408]{1,0:T(8,128)(2,1)} %get-tuple-element.198, bf16[2048,1408]{0,1:T(8,128)(2,1)} %all-gather.4.cloned.1.call-done), kind=kOutput, calls=%fused_computation.2 | convolution fusion | flops 11815354368 | bytes 19922944 | tf_op jit(solution)/shard_map/dot_general | solution.py:27
  568.2 7.4 project_out_back.3
  575.6 7.7 project_out_back.2
  589.5 10.6 %collective-permute-done.39.refs_2_ = bf16[1024,256]{1,0:T(8,128)(2,1)} collective-permute-done((bf16[1024,256]{1,0:T(8,128)(2,1)}, bf16[1024,256]{1,0:T(8,128)(2,1)}, u32[]{:S(2)}, u32[]{:S(2)}) %collective-permute-start.39) | collective-permute-done | bytes 524320 | tf_op jit(solution)/shard_map/ppermute | solution.py:904
  600.1 5.0 fusion.38
  617.2 46.1 %attention_backward.2 = (bf16[4096,384]{1,0:T(8,128)(2,1)}, f32[8,384]{1,0:T(8,128)}) custom-call(s32[32]{0:T(128)} %and_select_fusion.1.slot_ref, s32[6]{0:T(128)} %bitcast.128, bf16[1024,256]{1,0:T(8,128)(2,1)} %get-tuple-element.226.refs_0_, bf16[1024,256]{1,0:T(8,128)(2,1)} %get-tuple-element.227.refs_1_, ...), custom_call_target="tpu_custom_call" | custom-call | flops 28633112576 | bytes 10485760 | tf_op jit(solution)/shard_map/attention_backward/pallas_call | solution.py:383
  673.7 45.9 %attention_backward.3 = (bf16[4096,384]{1,0:T(8,128)(2,1)}, f32[8,384]{1,0:T(8,128)}) custom-call(s32[32]{0:T(128)} %and_select_fusion.1.slot_ref, s32[6]{0:T(128)} %bitcast.129, bf16[1024,256]{1,0:T(8,128)(2,1)} %get-tuple-element.226.refs_0_, bf16[1024,256]{1,0:T(8,128)(2,1)} %get-tuple-element.227.refs_1_, ...), custom_call_target="tpu_custom_call" | custom-call | flops 28633112576 | bytes 10485760 | tf_op jit(solution)/shard_map/attention_backward/pallas_call | solution.py:383
  722.4 14.1 %convolution_convert_fusion.4 = bf16[2048,384]{1,0:T(8,128)(2,1)} fusion(bf16[4096,2048]{1,0:T(8,128)(2,1)} %get-tuple-element.240, bf16[4096,384]{1,0:T(8,128)(2,1)S(1)} %copy-done.40), kind=kOutput, calls=%fused_computation.33 | convolution fusion | flops 6443237376 | bytes 21495808 | tf_op jit(solution)/shard_map/dot_general | solution.py:27
  736.5 19.9 %collective-permute-done.49.refs_3_ = bf16[1024,384]{1,0:T(8,128)(2,1)S(1)} collective-permute-done((bf16[1024,384]{1,0:T(8,128)(2,1)S(1)}, bf16[1024,384]{1,0:T(8,128)(2,1)S(1)}, u32[]{:S(2)}, u32[]{:S(2)}) %collective-permute-start.49) | collective-permute-done | bytes 786464 | tf_op jit(solution)/shard_map/ppermute | solution.py:904
  756.6 10.3 %convolution_convert_fusion.3 = bf16[2048,384]{1,0:T(8,128)(2,1)} fusion(bf16[4096,2048]{1,0:T(8,128)(2,1)S(1)} %bitcast.94, bf16[4096,384]{1,0:T(8,128)(2,1)S(1)} %copy-done.41), kind=kOutput, calls=%fused_computation.32 | convolution fusion | flops 6443237376 | bytes 21495808 | tf_op jit(solution)/shard_map/dot_general | solution.py:27
  766.9 14.6 %collective-permute-done.50.refs_3_ = bf16[1024,384]{1,0:T(8,128)(2,1)S(1)} collective-permute-done((bf16[1024,384]{1,0:T(8,128)(2,1)S(1)}, bf16[1024,384]{1,0:T(8,128)(2,1)S(1)}, u32[]{:S(2)}, u32[]{:S(2)}) %collective-permute-start.50) | collective-permute-done | bytes 786464 | tf_op jit(solution)/shard_map/ppermute | solution.py:904
  782.4 13.7 %project_back.2 = (bf16[512,2048]{1,0:T(8,128)(2,1)}, bf16[512,2048]{1,0:T(8,128)(2,1)}) custom-call(bf16[4096,384]{1,0:T(8,128)(2,1)} %get-tuple-element.221.refs_0_, bf16[4096,384]{1,0:T(8,128)(2,1)} %get-tuple-element.233.refs_1_, bf16[2048,384]{1,0:T(8,128)(2,1)} %collective-permute-done.48.refs_2_, bf16[1024,384]{1,0:T(8,128)(2,1)} %copy-done.68, ...), custom_call_target="tpu_custom_call" | custom-call | flops 6442450944 | bytes 19136512 | tf_op jit(solution)/shard_map/project_back/pallas_call | solution.py:590
  805.0 13.9 %project_back.3 = (bf16[512,2048]{1,0:T(8,128)(2,1)}, bf16[512,2048]{1,0:T(8,128)(2,1)}) custom-call(bf16[4096,384]{1,0:T(8,128)(2,1)} %get-tuple-element.221.refs_0_, bf16[4096,384]{1,0:T(8,128)(2,1)} %get-tuple-element.233.refs_1_, bf16[2048,384]{1,0:T(8,128)(2,1)} %collective-permute-done.48.refs_2_, bf16[1024,384]{1,0:T(8,128)(2,1)} %copy-done.67, ...), custom_call_target="tpu_custom_call" | custom-call | flops 6442450944 | bytes 19136512 | tf_op jit(solution)/shard_map/project_back/pallas_call | solution.py:590
  818.9 9.5 collective-permute-done.52
  852.5 13.6 %collective-permute-done.66 = bf16[512,768]{1,0:T(8,128)(2,1)} collective-permute-done((bf16[512,768]{1,0:T(8,128)(2,1)}, bf16[512,768]{1,0:T(8,128)(2,1)}, u32[]{:S(2)}, u32[]{:S(2)}) %collective-permute-start.66) | collective-permute-done | bytes 786464 | tf_op jit(solution)/shard_map/ppermute | solution.py:904
  870.5 7.8 place_rows.4
  889.2 5.0 collective-permute-done.67
  897.6 7.8 collective-permute-done.72
  905.4 8.4 collective-permute-done.58.refs_5_
  914.0 20.5 %collective-permute-done.54.refs_1_ = bf16[256,2048]{1,0:T(8,128)(2,1)} collective-permute-done((bf16[256,2048]{1,0:T(8,128)(2,1)}, bf16[256,2048]{1,0:T(8,128)(2,1)}, u32[]{:S(2)}, u32[]{:S(2)}) %collective-permute-start.54) | collective-permute-done | bytes 1048608 | tf_op jit(solution)/shard_map/ppermute | solution.py:860
  962.7 8.7 place_rows.5
  (460 shorter events, 223.7 us)
Async XLA Ops:
  7.2 223.0 %all-gather.6.cloned.1.call-start = ((), (), s32[]{:S(2)}) async-start(), calls=%async_computation.3 | async-start | bytes 2359296 | tf_op jit(solution)/shard_map/all_gather | solution.py:1046
  9.0 233.9 %all-gather.4.cloned.1.call-start = ((), (), s32[]{:S(2)}) async-start(), calls=%async_computation.2 | async-start | bytes 6488064 | tf_op jit(solution)/shard_map/all_gather | solution.py:1048
  24.0 343.1 %all-gather.8.cloned.1.call-start = ((), (), s32[]{:S(2)}) async-start(), calls=%async_computation.4 | async-start | bytes 12976128 | tf_op jit(solution)/shard_map/all_gather | solution.py:1050
  30.3 26.7 %collective-permute-start.11 = (bf16[256,2048]{1,0:T(8,128)(2,1)S(1)}, bf16[256,2048]{1,0:T(8,128)(2,1)}, u32[]{:S(2)}, u32[]{:S(2)}) collective-permute-start(bf16[256,2048]{1,0:T(8,128)(2,1)S(1)} %get-tuple-element.350), channel_id=1, source_target_pairs={{0,4},{4,0},{1,5},{5,1},{2,6},{6,2},{3,7},{7,3},{8,12},{12,8},{9,1... | collective-permute-start | bytes 3145736 | tf_op jit(solution)/shard_map/ppermute | solution.py:904
  32.7 46.9 %collective-permute-start = (bf16[256,2048]{1,0:T(8,128)(2,1)S(1)}, bf16[256,2048]{1,0:T(8,128)(2,1)S(1)}, u32[]{:S(2)}, u32[]{:S(2)}) collective-permute-start(bf16[256,2048]{1,0:T(8,128)(2,1)S(1)} %get-tuple-element.332), channel_id=1, source_target_pairs={{0,4},{4,0},{1,5},{5,1},{2,6},{6,2},{3,7},{7,3},{8,12},{12,8},{9,1... | collective-permute-start | bytes 3145736 | tf_op jit(solution)/shard_map/ppermute | solution.py:904
  50.0 29.6 %collective-permute-start.5 = (bf16[256,768]{1,0:T(8,128)(2,1)}, bf16[256,768]{1,0:T(8,128)(2,1)}, u32[]{:S(2)}, u32[]{:S(2)}) collective-permute-start(bf16[256,768]{1,0:T(8,128)(2,1)} %collective-permute-done.4.refs_5_), channel_id=1, source_target_pairs={{0,24},{8,0},{16,8},{24,16},{1,25},{9,1},{17,9},{25,17},{2,26},{10... | collective-permute-start | bytes 1179656 | tf_op jit(solution)/shard_map/ppermute | solution.py:904
  56.9 51.3 %collective-permute-start.12 = (bf16[256,2048]{1,0:T(8,128)(2,1)}, bf16[256,2048]{1,0:T(8,128)(2,1)}, u32[]{:S(2)}, u32[]{:S(2)}) collective-permute-start(bf16[256,2048]{1,0:T(8,128)(2,1)} %collective-permute-done.11.refs_0_), channel_id=1, source_target_pairs={{0,2},{1,3},{2,0},{3,1},{4,6},{5,7},{6,4},{7,5},{8,10},{9,11},{10,... | collective-permute-start | bytes 3145736 | tf_op jit(solution)/shard_map/ppermute | solution.py:860
  79.6 28.6 %collective-permute-start.6 = (bf16[256,2048]{1,0:T(8,128)(2,1)S(1)}, bf16[256,2048]{1,0:T(8,128)(2,1)}, u32[]{:S(2)}, u32[]{:S(2)}) collective-permute-start(bf16[256,2048]{1,0:T(8,128)(2,1)S(1)} %collective-permute-done.refs_0_), channel_id=1, source_target_pairs={{0,2},{1,3},{2,0},{3,1},{4,6},{5,7},{6,4},{7,5},{8,10},{9,11},{10,... | collective-permute-start | bytes 3145736 | tf_op jit(solution)/shard_map/ppermute | solution.py:860
  81.5 26.7 %collective-permute-start.10 = (bf16[256,768]{1,0:T(8,128)(2,1)}, bf16[256,768]{1,0:T(8,128)(2,1)}, u32[]{:S(2)}, u32[]{:S(2)}) collective-permute-start(bf16[256,768]{1,0:T(8,128)(2,1)} %collective-permute-done.5.refs_6_), channel_id=1, source_target_pairs={{0,24},{8,0},{16,8},{24,16},{1,25},{9,1},{17,9},{25,17},{2,26},{10... | collective-permute-start | bytes 1179656 | tf_op jit(solution)/shard_map/ppermute | solution.py:904
  114.2 835.2 %reduce-scatter.3.cloned.1.call-start = ((), (), s32[]{:S(2)}) async-start(), calls=%async_computation.5 | async-start | bytes 6488064 | tf_op jit(solution)/shard_map/reduce_scatter | solution.py:1175
  114.9 29.7 %collective-permute-start.7 = (bf16[256,2048]{1,0:T(8,128)(2,1)S(1)}, bf16[256,2048]{1,0:T(8,128)(2,1)S(1)}, u32[]{:S(2)}, u32[]{:S(2)}) collective-permute-start(bf16[256,2048]{1,0:T(8,128)(2,1)S(1)} %collective-permute-done.refs_0_), channel_id=1, source_target_pairs={{0,1},{1,0},{2,3},{3,2},{4,5},{5,4},{6,7},{7,6},{8,9},{9,8},{10,11... | collective-permute-start | bytes 3145736 | tf_op jit(solution)/shard_map/ppermute | solution.py:860
  114.9 29.6 %collective-permute-start.8 = (bf16[256,2048]{1,0:T(8,128)(2,1)}, bf16[256,2048]{1,0:T(8,128)(2,1)}, u32[]{:S(2)}, u32[]{:S(2)}) collective-permute-start(bf16[256,2048]{1,0:T(8,128)(2,1)} %collective-permute-done.6.refs_1_), channel_id=1, source_target_pairs={{0,1},{1,0},{2,3},{3,2},{4,5},{5,4},{6,7},{7,6},{8,9},{9,8},{10,11... | collective-permute-start | bytes 3145736 | tf_op jit(solution)/shard_map/ppermute | solution.py:860
  191.9 42.3 %collective-permute-start.16 = (bf16[2048,128]{1,0:T(8,128)(2,1)}, bf16[2048,128]{1,0:T(8,128)(2,1)S(1)}, u32[]{:S(2)}, u32[]{:S(2)}) collective-permute-start(bf16[2048,128]{1,0:T(8,128)(2,1)} %get-tuple-element.164), channel_id=1, source_target_pairs={{0,4},{4,0},{1,5},{5,1},{2,6},{6,2},{3,7},{7,3},{8,12},{12,8},{9,1... | collective-permute-start | bytes 1572872 | tf_op jit(solution)/shard_map/ppermute | solution.py:904
  263.4 26.1 %collective-permute-start.18 = (bf16[256,2048]{1,0:T(8,128)(2,1)S(1)}, bf16[256,2048]{1,0:T(8,128)(2,1)S(1)}, u32[]{:S(2)}, u32[]{:S(2)}) collective-permute-start(bf16[256,2048]{1,0:T(8,128)(2,1)S(1)} %slice.218), channel_id=1, source_target_pairs={{0,2},{1,3},{2,0},{3,1},{4,6},{5,7},{6,4},{7,5},{8,10},{9,11},{10,... | collective-permute-start | bytes 3145736 | tf_op jit(solution)/shard_map/ppermute | solution.py:860
  265.9 45.2 %collective-permute-start.23 = (bf16[256,2048]{1,0:T(8,128)(2,1)S(1)}, bf16[256,2048]{1,0:T(8,128)(2,1)S(1)}, u32[]{:S(2)}, u32[]{:S(2)}) collective-permute-start(bf16[256,2048]{1,0:T(8,128)(2,1)S(1)} %slice.217), channel_id=1, source_target_pairs={{0,2},{1,3},{2,0},{3,1},{4,6},{5,7},{6,4},{7,5},{8,10},{9,11},{10,... | collective-permute-start | bytes 3145736 | tf_op jit(solution)/shard_map/ppermute | solution.py:860
  319.1 24.6 %collective-permute-start.19 = (bf16[256,2048]{1,0:T(8,128)(2,1)S(1)}, bf16[256,2048]{1,0:T(8,128)(2,1)}, u32[]{:S(2)}, u32[]{:S(2)}) collective-permute-start(bf16[256,2048]{1,0:T(8,128)(2,1)S(1)} %get-tuple-element.366.refs_0_), channel_id=1, source_target_pairs={{0,2},{1,3},{2,0},{3,1},{4,6},{5,7},{6,4},{7,5},{8,10},{9,11},{10,... | collective-permute-start | bytes 3145736 | tf_op jit(solution)/shard_map/ppermute | solution.py:860
  320.5 33.8 %collective-permute-start.20 = (bf16[256,2048]{1,0:T(8,128)(2,1)S(1)}, bf16[256,2048]{1,0:T(8,128)(2,1)}, u32[]{:S(2)}, u32[]{:S(2)}) collective-permute-start(bf16[256,2048]{1,0:T(8,128)(2,1)S(1)} %get-tuple-element.366.refs_0_), channel_id=1, source_target_pairs={{0,1},{1,0},{2,3},{3,2},{4,5},{5,4},{6,7},{7,6},{8,9},{9,8},{10,11... | collective-permute-start | bytes 3145736 | tf_op jit(solution)/shard_map/ppermute | solution.py:860
  352.3 57.4 %collective-permute-start.25 = (bf16[1024,768]{0,1:T(8,128)(2,1)}, bf16[1024,768]{0,1:T(8,128)(2,1)}, u32[]{:S(2)}, u32[]{:S(2)}) collective-permute-start(bf16[1024,768]{0,1:T(8,128)(2,1)} %get-tuple-element.354), channel_id=1, source_target_pairs={{0,4},{4,0},{1,5},{5,1},{2,6},{6,2},{3,7},{7,3},{8,12},{12,8},{9,1... | collective-permute-start | bytes 4718600 | tf_op jit(solution)/shard_map/ppermute | solution.py:904
  352.9 56.8 %collective-permute-start.24 = (bf16[256,2048]{1,0:T(8,128)(2,1)}, bf16[256,2048]{1,0:T(8,128)(2,1)}, u32[]{:S(2)}, u32[]{:S(2)}) collective-permute-start(bf16[256,2048]{1,0:T(8,128)(2,1)} %get-tuple-element.181.refs_0_), channel_id=1, source_target_pairs={{0,2},{1,3},{2,0},{3,1},{4,6},{5,7},{6,4},{7,5},{8,10},{9,11},{10,... | collective-permute-start | bytes 3145736 | tf_op jit(solution)/shard_map/ppermute | solution.py:860
  410.4 60.5 %collective-permute-start.33 = (bf16[1024,768]{0,1:T(8,128)(2,1)}, bf16[1024,768]{0,1:T(8,128)(2,1)S(1)}, u32[]{:S(2)}, u32[]{:S(2)}) collective-permute-start(bf16[1024,768]{0,1:T(8,128)(2,1)} %get-tuple-element.190), channel_id=1, source_target_pairs={{0,4},{4,0},{1,5},{5,1},{2,6},{6,2},{3,7},{7,3},{8,12},{12,8},{9,1... | collective-permute-start | bytes 4718600 | tf_op jit(solution)/shard_map/ppermute | solution.py:904
  421.8 44.4 %collective-permute-start.27 = (bf16[256,2048]{1,0:T(8,128)(2,1)}, bf16[256,2048]{1,0:T(8,128)(2,1)}, u32[]{:S(2)}, u32[]{:S(2)}) collective-permute-start(bf16[256,2048]{1,0:T(8,128)(2,1)} %slice.216), channel_id=1, source_target_pairs={{0,2},{1,3},{2,0},{3,1},{4,6},{5,7},{6,4},{7,5},{8,10},{9,11},{10,... | collective-permute-start | bytes 3145736 | tf_op jit(solution)/shard_map/ppermute | solution.py:860
  478.9 25.4 %collective-permute-start.35 = (bf16[256,2048]{1,0:T(8,128)(2,1)}, bf16[256,2048]{1,0:T(8,128)(2,1)S(1)}, u32[]{:S(2)}, u32[]{:S(2)}) collective-permute-start(bf16[256,2048]{1,0:T(8,128)(2,1)} %slice.215), channel_id=1, source_target_pairs={{0,2},{1,3},{2,0},{3,1},{4,6},{5,7},{6,4},{7,5},{8,10},{9,11},{10,... | collective-permute-start | bytes 3145736 | tf_op jit(solution)/shard_map/ppermute | solution.py:860
  496.9 456.2 %reduce-scatter.5.cloned.1.call-start = ((), (), s32[]{:S(2)}) async-start(), calls=%async_computation.6 | async-start | bytes 12976128 | tf_op jit(solution)/shard_map/reduce_scatter | solution.py:1176
  514.2 48.3 %collective-permute-start.36 = (bf16[256,2048]{1,0:T(8,128)(2,1)S(1)}, bf16[256,2048]{1,0:T(8,128)(2,1)}, u32[]{:S(2)}, u32[]{:S(2)}) collective-permute-start(bf16[256,2048]{1,0:T(8,128)(2,1)S(1)} %get-tuple-element.199.refs_0_), channel_id=1, source_target_pairs={{0,2},{1,3},{2,0},{3,1},{4,6},{5,7},{6,4},{7,5},{8,10},{9,11},{10,... | collective-permute-start | bytes 3145736 | tf_op jit(solution)/shard_map/ppermute | solution.py:860
  514.8 48.4 %collective-permute-start.28 = (bf16[256,2048]{1,0:T(8,128)(2,1)}, bf16[256,2048]{1,0:T(8,128)(2,1)}, u32[]{:S(2)}, u32[]{:S(2)}) collective-permute-start(bf16[256,2048]{1,0:T(8,128)(2,1)} %get-tuple-element.348.refs_0_), channel_id=1, source_target_pairs={{0,2},{1,3},{2,0},{3,1},{4,6},{5,7},{6,4},{7,5},{8,10},{9,11},{10,... | collective-permute-start | bytes 3145736 | tf_op jit(solution)/shard_map/ppermute | solution.py:860
  583.3 25.8 %collective-permute-start.41 = (bf16[512,2048]{1,0:T(8,128)(2,1)}, bf16[512,2048]{1,0:T(8,128)(2,1)}, u32[]{:S(2)}, u32[]{:S(2)}) collective-permute-start(bf16[512,2048]{1,0:T(8,128)(2,1)} %get-tuple-element.204), channel_id=1, source_target_pairs={{0,1},{1,0},{2,3},{3,2},{4,5},{5,4},{6,7},{7,6},{8,9},{9,8},{10,11... | collective-permute-start | bytes 6291464 | tf_op jit(solution)/shard_map/ppermute | solution.py:860
  583.4 25.7 %collective-permute-start.42 = (bf16[512,2048]{1,0:T(8,128)(2,1)}, bf16[512,2048]{1,0:T(8,128)(2,1)}, u32[]{:S(2)}, u32[]{:S(2)}) collective-permute-start(bf16[512,2048]{1,0:T(8,128)(2,1)} %get-tuple-element.205), channel_id=1, source_target_pairs={{0,1},{1,0},{2,3},{3,2},{4,5},{5,4},{6,7},{7,6},{8,9},{9,8},{10,11... | collective-permute-start | bytes 6291464 | tf_op jit(solution)/shard_map/ppermute | solution.py:860
  587.8 25.3 %collective-permute-start.40 = (bf16[1024,256]{1,0:T(8,128)(2,1)}, bf16[1024,256]{1,0:T(8,128)(2,1)S(1)}, u32[]{:S(2)}, u32[]{:S(2)}) collective-permute-start(bf16[1024,256]{1,0:T(8,128)(2,1)} %get-tuple-element.203), channel_id=1, source_target_pairs={{0,4},{4,0},{1,5},{5,1},{2,6},{6,2},{3,7},{7,3},{8,12},{12,8},{9,1... | collective-permute-start | bytes 1572872 | tf_op jit(solution)/shard_map/ppermute | solution.py:904
  614.4 52.6 %collective-permute-start.44 = (bf16[256,2048]{1,0:T(8,128)(2,1)}, bf16[256,2048]{1,0:T(8,128)(2,1)}, u32[]{:S(2)}, u32[]{:S(2)}) collective-permute-start(bf16[256,2048]{1,0:T(8,128)(2,1)} %slice.213), channel_id=1, source_target_pairs={{0,2},{1,3},{2,0},{3,1},{4,6},{5,7},{6,4},{7,5},{8,10},{9,11},{10,... | collective-permute-start | bytes 3145736 | tf_op jit(solution)/shard_map/ppermute | solution.py:860
  616.0 54.1 %collective-permute-start.43 = (bf16[256,2048]{1,0:T(8,128)(2,1)S(1)}, bf16[256,2048]{1,0:T(8,128)(2,1)}, u32[]{:S(2)}, u32[]{:S(2)}) collective-permute-start(bf16[256,2048]{1,0:T(8,128)(2,1)S(1)} %slice.214), channel_id=1, source_target_pairs={{0,2},{1,3},{2,0},{3,1},{4,6},{5,7},{6,4},{7,5},{8,10},{9,11},{10,... | collective-permute-start | bytes 3145736 | tf_op jit(solution)/shard_map/ppermute | solution.py:860
  666.3 55.0 %collective-permute-start.48 = (bf16[2048,384]{1,0:T(8,128)(2,1)}, bf16[2048,384]{1,0:T(8,128)(2,1)}, u32[]{:S(2)}, u32[]{:S(2)}) collective-permute-start(bf16[2048,384]{1,0:T(8,128)(2,1)} %slice.138), channel_id=1, source_target_pairs={{0,4},{4,0},{1,5},{5,1},{2,6},{6,2},{3,7},{7,3},{8,12},{12,8},{9,1... | collective-permute-start | bytes 4718600 | tf_op jit(solution)/shard_map/ppermute | solution.py:904
  672.1 49.2 %collective-permute-start.45 = (bf16[512,2048]{1,0:T(8,128)(2,1)S(1)}, bf16[512,2048]{1,0:T(8,128)(2,1)}, u32[]{:S(2)}, u32[]{:S(2)}) collective-permute-start(bf16[512,2048]{1,0:T(8,128)(2,1)S(1)} %constant_dynamic-update-slice_fusion.refs_0_), channel_id=1, source_target_pairs={{0,2},{1,3},{2,0},{3,1},{4,6},{5,7},{6,4},{7,5},{8,10},{9,11},{10,... | collective-permute-start | bytes 6291464 | tf_op jit(solution)/shard_map/ppermute | solution.py:860
  721.4 35.0 %collective-permute-start.49 = (bf16[1024,384]{1,0:T(8,128)(2,1)S(1)}, bf16[1024,384]{1,0:T(8,128)(2,1)S(1)}, u32[]{:S(2)}, u32[]{:S(2)}) collective-permute-start(bf16[1024,384]{1,0:T(8,128)(2,1)S(1)} %get-tuple-element.236), channel_id=1, source_target_pairs={{0,4},{4,0},{1,5},{5,1},{2,6},{6,2},{3,7},{7,3},{8,12},{12,8},{9,1... | collective-permute-start | bytes 2359304 | tf_op jit(solution)/shard_map/ppermute | solution.py:904
  756.4 25.1 %collective-permute-start.50 = (bf16[1024,384]{1,0:T(8,128)(2,1)S(1)}, bf16[1024,384]{1,0:T(8,128)(2,1)S(1)}, u32[]{:S(2)}, u32[]{:S(2)}) collective-permute-start(bf16[1024,384]{1,0:T(8,128)(2,1)S(1)} %get-tuple-element.237), channel_id=1, source_target_pairs={{0,4},{4,0},{1,5},{5,1},{2,6},{6,2},{3,7},{7,3},{8,12},{12,8},{9,1... | collective-permute-start | bytes 2359304 | tf_op jit(solution)/shard_map/ppermute | solution.py:904
  803.1 25.2 %collective-permute-start.52 = (bf16[256,2048]{1,0:T(8,128)(2,1)S(1)}, bf16[256,2048]{1,0:T(8,128)(2,1)S(1)}, u32[]{:S(2)}, u32[]{:S(2)}) collective-permute-start(bf16[256,2048]{1,0:T(8,128)(2,1)S(1)} %slice.212), channel_id=1, source_target_pairs={{0,2},{1,3},{2,0},{3,1},{4,6},{5,7},{6,4},{7,5},{8,10},{9,11},{10,... | collective-permute-start | bytes 3145736 | tf_op jit(solution)/shard_map/ppermute | solution.py:860
  834.2 36.2 %collective-permute-start.46 = (bf16[512,2048]{1,0:T(8,128)(2,1)}, bf16[512,2048]{1,0:T(8,128)(2,1)}, u32[]{:S(2)}, u32[]{:S(2)}) collective-permute-start(bf16[512,2048]{1,0:T(8,128)(2,1)} %copy-done.23), channel_id=1, source_target_pairs={{0,1},{1,0},{2,3},{3,2},{4,5},{5,4},{6,7},{7,6},{8,9},{9,8},{10,11... | collective-permute-start | bytes 6291464 | tf_op jit(solution)/shard_map/ppermute | solution.py:860
  834.6 35.8 %collective-permute-start.47 = (bf16[512,2048]{1,0:T(8,128)(2,1)}, bf16[512,2048]{1,0:T(8,128)(2,1)}, u32[]{:S(2)}, u32[]{:S(2)}) collective-permute-start(bf16[512,2048]{1,0:T(8,128)(2,1)} %collective-permute-done.45.refs_1_), channel_id=1, source_target_pairs={{0,1},{1,0},{2,3},{3,2},{4,5},{5,4},{6,7},{7,6},{8,9},{9,8},{10,11... | collective-permute-start | bytes 6291464 | tf_op jit(solution)/shard_map/ppermute | solution.py:860
  837.6 28.5 %collective-permute-start.66 = (bf16[512,768]{1,0:T(8,128)(2,1)}, bf16[512,768]{1,0:T(8,128)(2,1)}, u32[]{:S(2)}, u32[]{:S(2)}) collective-permute-start(bf16[512,768]{1,0:T(8,128)(2,1)} %constant_dynamic-slice_fusion.2), channel_id=1, source_target_pairs={{0,24},{8,0},{16,8},{24,16},{1,25},{9,1},{17,9},{25,17},{2,26},{10... | collective-permute-start | bytes 2359304 | tf_op jit(solution)/shard_map/ppermute | solution.py:904
  844.1 34.1 %collective-permute-start.57 = (bf16[256,2048]{1,0:T(8,128)(2,1)}, bf16[256,2048]{1,0:T(8,128)(2,1)}, u32[]{:S(2)}, u32[]{:S(2)}) collective-permute-start(bf16[256,2048]{1,0:T(8,128)(2,1)} %slice.211), channel_id=1, source_target_pairs={{0,2},{1,3},{2,0},{3,1},{4,6},{5,7},{6,4},{7,5},{8,10},{9,11},{10,... | collective-permute-start | bytes 3145736 | tf_op jit(solution)/shard_map/ppermute | solution.py:860
  850.6 37.3 %collective-permute-start.71 = (bf16[512,512]{1,0:T(8,128)(2,1)S(1)}, bf16[512,512]{1,0:T(8,128)(2,1)}, u32[]{:S(2)}, u32[]{:S(2)}) collective-permute-start(bf16[512,512]{1,0:T(8,128)(2,1)S(1)} %add_convert_fusion.11), channel_id=1, source_target_pairs={{0,24},{8,0},{16,8},{24,16},{1,25},{9,1},{17,9},{25,17},{2,26},{10... | collective-permute-start | bytes 1572872 | tf_op jit(solution)/shard_map/ppermute | solution.py:904
  868.6 25.7 %collective-permute-start.67 = (bf16[512,768]{1,0:T(8,128)(2,1)}, bf16[512,768]{1,0:T(8,128)(2,1)}, u32[]{:S(2)}, u32[]{:S(2)}) collective-permute-start(bf16[512,768]{1,0:T(8,128)(2,1)} %add_convert_fusion.9), channel_id=1, source_target_pairs={{0,24},{8,0},{16,8},{24,16},{1,25},{9,1},{17,9},{25,17},{2,26},{10... | collective-permute-start | bytes 2359304 | tf_op jit(solution)/shard_map/ppermute | solution.py:904
  887.5 26.3 %collective-permute-start.58 = (bf16[256,2048]{1,0:T(8,128)(2,1)S(1)}, bf16[256,2048]{1,0:T(8,128)(2,1)}, u32[]{:S(2)}, u32[]{:S(2)}) collective-permute-start(bf16[256,2048]{1,0:T(8,128)(2,1)S(1)} %get-tuple-element.255.refs_4_), channel_id=1, source_target_pairs={{0,2},{1,3},{2,0},{3,1},{4,6},{5,7},{6,4},{7,5},{8,10},{9,11},{10,... | collective-permute-start | bytes 3145736 | tf_op jit(solution)/shard_map/ppermute | solution.py:860
  887.9 55.2 %collective-permute-start.59 = (bf16[256,2048]{1,0:T(8,128)(2,1)S(1)}, bf16[256,2048]{1,0:T(8,128)(2,1)S(1)}, u32[]{:S(2)}, u32[]{:S(2)}) collective-permute-start(bf16[256,2048]{1,0:T(8,128)(2,1)S(1)} %get-tuple-element.255.refs_4_), channel_id=1, source_target_pairs={{0,1},{1,0},{2,3},{3,2},{4,5},{5,4},{6,7},{7,6},{8,9},{9,8},{10,11... | collective-permute-start | bytes 3145736 | tf_op jit(solution)/shard_map/ppermute | solution.py:860
  895.5 40.4 %collective-permute-start.68 = (bf16[512,768]{1,0:T(8,128)(2,1)S(1)}, bf16[512,768]{1,0:T(8,128)(2,1)S(1)}, u32[]{:S(2)}, u32[]{:S(2)}) collective-permute-start(bf16[512,768]{1,0:T(8,128)(2,1)S(1)} %add_convert_fusion.8), channel_id=1, source_target_pairs={{0,24},{8,0},{16,8},{24,16},{1,25},{9,1},{17,9},{25,17},{2,26},{10... | collective-permute-start | bytes 2359304 | tf_op jit(solution)/shard_map/ppermute | solution.py:904
  897.5 37.0 %collective-permute-start.54 = (bf16[256,2048]{1,0:T(8,128)(2,1)}, bf16[256,2048]{1,0:T(8,128)(2,1)}, u32[]{:S(2)}, u32[]{:S(2)}) collective-permute-start(bf16[256,2048]{1,0:T(8,128)(2,1)} %get-tuple-element.342.refs_0_), channel_id=1, source_target_pairs={{0,2},{1,3},{2,0},{3,1},{4,6},{5,7},{6,4},{7,5},{8,10},{9,11},{10,... | collective-permute-start | bytes 3145736 | tf_op jit(solution)/shard_map/ppermute | solution.py:860
  905.4 57.4 %collective-permute-start.55 = (bf16[256,2048]{1,0:T(8,128)(2,1)}, bf16[256,2048]{1,0:T(8,128)(2,1)}, u32[]{:S(2)}, u32[]{:S(2)}) collective-permute-start(bf16[256,2048]{1,0:T(8,128)(2,1)} %get-tuple-element.342.refs_0_), channel_id=1, source_target_pairs={{0,1},{1,0},{2,3},{3,2},{4,5},{5,4},{6,7},{7,6},{8,9},{9,8},{10,11... | collective-permute-start | bytes 3145736 | tf_op jit(solution)/shard_map/ppermute | solution.py:860
  913.8 43.6 %collective-permute-start.60 = (bf16[256,2048]{1,0:T(8,128)(2,1)}, bf16[256,2048]{1,0:T(8,128)(2,1)}, u32[]{:S(2)}, u32[]{:S(2)}) collective-permute-start(bf16[256,2048]{1,0:T(8,128)(2,1)} %collective-permute-done.58.refs_5_), channel_id=1, source_target_pairs={{0,1},{1,0},{2,3},{3,2},{4,5},{5,4},{6,7},{7,6},{8,9},{9,8},{10,11... | collective-permute-start | bytes 3145736 | tf_op jit(solution)/shard_map/ppermute | solution.py:860
  935.9 26.8 %collective-permute-start.56 = (bf16[256,2048]{1,0:T(8,128)(2,1)}, bf16[256,2048]{1,0:T(8,128)(2,1)}, u32[]{:S(2)}, u32[]{:S(2)}) collective-permute-start(bf16[256,2048]{1,0:T(8,128)(2,1)} %collective-permute-done.54.refs_1_), channel_id=1, source_target_pairs={{0,1},{1,0},{2,3},{3,2},{4,5},{5,4},{6,7},{7,6},{8,9},{9,8},{10,11... | collective-permute-start | bytes 3145736 | tf_op jit(solution)/shard_map/ppermute | solution.py:860
  (119 other events, 1532.9 us)
Sparse Core Ops, SparseCore 0:
  10.1 91.9 all-gather.5
  104.1 98.2 all-gather.3
  205.2 161.8 all-gather.7
  497.0 108.3 reduce-scatter.2
  608.9 208.1 reduce-scatter.4
